TPU v7x, 32 devices: a whole 2x2x4 slice. The times are simulated.
32 devices in a mesh: seq: 16 (over z, y, x), head: 2 (over core).
Axes of the slice: x: 2, y: 2, z: 4, core: 2. Of those that a mesh axis runs over, the one named last changes fastest.
Arguments:
- queries: bfloat16 [17408, 512], P('seq', 'head'), may hold values from -50 to 50
- keys: bfloat16 [17408, 512], P('seq', 'head'), may hold values from -6 to 6
- values: bfloat16 [17408, 512], P('seq', 'head'), may hold values from -48 to 48
- rand_group: int32 [272, 3], replicated, may hold values from 0 to 15, all different within a row; in each aligned block of 17 rows (0 to 16, 17 to 33, ...) at most 4 rows name the same one
- rand_offset: int32 [272, 3], replicated, may hold values from 0 to 16
- glob_blocks: int32 [2], replicated, may hold values from 0 to 271
- w_out: bfloat16 [512, 4096], P(None, 'head'), may hold values from -0.25 to 0.25
Outputs:
- layer_out: bfloat16 [17408, 4096], P('seq', 'head')
Inputs may be any that keep to these rules, and one draw needn't show every extreme that they name: `rand_group`: each row names 3 different groups. Among the 17 rows of one aligned block of 17 rows, no group is named more than 4 times, and in every draw some group is named exactly 4 times in some such block.
All inputs are finite; a program needn't handle non-finite values.
Results may differ from a plain program's by a relative error of at most 0.0056.
Values may be sent and summed in bfloat16 or wider, within the bound.
No kernel may reach another device: no remote copies, remote signals or barrier semaphores. Data moves between devices by JAX's collectives and lax.ppermute only.
A program may use at most 128 MiB of HBM per device.

v0:
```python
import functools
import math

import jax
import jax.numpy as jnp
from jax import lax
from jax.experimental import pallas as pl
from jax.experimental.pallas import tpu as pltpu
from jax.sharding import PartitionSpec as P

DH = 128
BLOCK = 64
R = 3
G = 2
VMEM = pltpu.MemorySpace.VMEM
SMEM = pltpu.MemorySpace.SMEM
BF16 = jnp.bfloat16
F32 = jnp.float32
I32 = jnp.int32
NONE = -1e30
PIECES = 3


def params(mib):
    return pltpu.CompilerParams(vmem_limit_bytes=mib * 1024 * 1024)


LIGHT = pl.CostEstimate(flops=1, bytes_accessed=1, transcendentals=0)
HEAVY = pl.CostEstimate(flops=4 * 10**9, bytes_accessed=1, transcendentals=0)


def spec(space=VMEM):
    return pl.BlockSpec(memory_space=space)


def rank_kernel(n, per, cap, g_ref, o_ref, spot_ref, arrive_ref, g_pad, o_pad):
    me = lax.axis_index("seq")
    nb = g_ref.shape[1]
    wide = g_pad.shape[1]
    tall = spot_ref.shape[0]
    g_pad[...] = jnp.full(g_pad.shape, -1, I32)
    o_pad[...] = jnp.zeros(o_pad.shape, I32)
    g_pad[:R, :nb] = g_ref[...]
    o_pad[:R, :nb] = o_ref[...]
    g = g_pad[...]
    lane = lax.broadcasted_iota(I32, g.shape, 1)
    place = lane
    for d in range(1, n):
        place = jnp.where(lane >= d * per, lane - d * per, place)
    rank = jnp.zeros(g.shape, I32)
    for s in range(1, per):
        back = pltpu.roll(g, s, axis=1)
        ahead = place >= s
        for r in range(R):
            same = jnp.broadcast_to(back[r : r + 1, :], g.shape) == g
            rank = rank + jnp.where(ahead & same, 1, 0)
    arrive_ref[...] = g * cap + rank
    row = lax.broadcasted_iota(I32, (tall, wide), 0)
    spots = jnp.zeros((tall, wide), F32)
    for side in range(2):
        named = jnp.where(g == lax.bitwise_xor(me, side * (n // 4)), o_pad[...], 0)
        for s in range(cap):
            picked = jnp.where(rank == s, named, 0).astype(F32)
            total = jnp.sum(picked, axis=0, keepdims=True)
            here = row == side * cap + s
            spots = spots + jnp.where(here, jnp.broadcast_to(total, (tall, wide)), 0.0)
    token = lax.broadcasted_iota(I32, (wide, 128), 0)
    first = lax.broadcasted_iota(I32, (wide, 128), 1) * per
    belongs = jnp.where((token >= first) & (token < first + per), 1.0, 0.0)
    spot_ref[...] = jnp.dot(
        spots.astype(BF16), belongs.astype(BF16), preferred_element_type=F32
    ).astype(I32)


def ranks(n, per, cap, groups, offsets):
    nb = groups.shape[1]
    wide = -(-nb // 128) * 128
    tall = -(-2 * cap // 8) * 8
    return pl.pallas_call(
        functools.partial(rank_kernel, n, per, cap),
        out_shape=(
            jax.ShapeDtypeStruct((tall, 128), I32),
            jax.ShapeDtypeStruct((8, wide), I32),
        ),
        in_specs=[spec(), spec()],
        out_specs=(spec(), spec()),
        scratch_shapes=[pltpu.VMEM((8, wide), I32), pltpu.VMEM((8, wide), I32)],
        compiler_params=params(4),
        cost_estimate=LIGHT,
        name="ranks",
    )(groups, offsets)


def gather_kernel(n, per, cap, lists, shared, names, spot_ref, *refs):
    plane = n // 4
    me = lax.axis_index("seq")
    sources, outs = dict(zip(names, refs)), refs[-plane:]
    for k, out_ref in enumerate(outs):
        at = 0
        for side, far, parts in lists:
            d = lax.bitwise_xor(me, k + (n // 2 if far else 0))
            for c in parts:
                for s in range(cap):
                    start = spot_ref[side * cap + s, d] * BLOCK
                    rows = pl.ds(pl.multiple_of(start, BLOCK), BLOCK)
                    out_ref[pl.ds(at, BLOCK)] = sources[side, c][rows]
                    at += BLOCK
        if shared:
            (c,) = lists[0][2]
            place_ref = refs[len(names)]
            shared_rows(n, per, k, at, place_ref, sources[0, c], sources[1, c], out_ref)


def shared_rows(n, per, k, at, place_ref, own_ref, mate_ref, out_ref):
    plane = n // 4
    me = lax.axis_index("seq")
    for g in range(G):
        owner = lax.div(place_ref[g], per)
        start = pl.multiple_of((place_ref[g] - owner * per) * BLOCK, BLOCK)
        rows = pl.ds(start, BLOCK)
        mine = lax.bitwise_and(lax.bitwise_xor(owner, me), plane) == 0
        out_ref[pl.ds(at + g * BLOCK, BLOCK)] = jnp.where(mine, own_ref[rows], mate_ref[rows])
    place = lax.bitwise_and(me, plane - 1)
    target = lax.bitwise_xor(place, k)
    is_before = lax.rem(place + 1, plane) == target
    is_end = jnp.where(is_before, target == 0, target == plane - 1)
    rows = pl.ds(pl.multiple_of(jnp.where(is_before, (per - 1) * BLOCK, 0), BLOCK), BLOCK)
    out_ref[pl.ds(at + G * BLOCK, BLOCK)] = jnp.where(is_end, mate_ref[rows], own_ref[rows])


def gather(n, per, cap, lists, spots, sources, shared=(), earlier=()):
    plane = n // 4
    names, arrays = tuple(sources), list(sources.values())
    rows = sum(len(parts) for _, _, parts in lists) * cap * BLOCK
    rows += (G + 1) * BLOCK if shared else 0
    out = jax.ShapeDtypeStruct((rows, arrays[0].shape[1]), BF16)
    return pl.pallas_call(
        functools.partial(gather_kernel, n, per, cap, lists, bool(shared), names),
        out_shape=(out,) * plane,
        in_specs=[spec(SMEM)]
        + [spec()] * len(arrays)
        + [spec(SMEM)] * len(shared)
        + [spec(pl.ANY)] * len(earlier),
        out_specs=(spec(),) * plane,
        compiler_params=params(8),
        cost_estimate=LIGHT,
        name="gather_blocks",
    )(spots, *arrays, *shared, *earlier)


def exchange(parts, n):
    got = [parts[0]]
    for k in range(1, n // 4):
        got.append(lax.ppermute(parts[k], "seq", [(i, i ^ k) for i in range(n)]))
    return got


def choose(n, cap, per, span, arrive_ref, d, sources, held, keys, vals):
    half = n // 2
    me = lax.axis_index("seq")
    for k, pair in enumerate(sources):
        for c, (ref, row) in enumerate(pair):
            held[k, pl.ds(c * cap * BLOCK, cap * BLOCK)] = ref[pl.ds(row, cap * BLOCK)]
    biases = {}
    for i in range(*span):
        row = []
        for r in range(R):
            spot = arrive_ref[r, d * per + i]
            group = lax.div(spot, cap)
            differ = lax.bitwise_xor(group, me)
            here = differ < half
            slot = jnp.where(here, spot - group * cap, 0)
            k = jnp.where(here, differ, 0)
            at = pl.ds((i * R + r) * BLOCK, BLOCK)
            keys[at] = held[k, pl.ds(pl.multiple_of(slot * BLOCK, BLOCK), BLOCK), :]
            vals[at] = held[k, pl.ds(pl.multiple_of((cap + slot) * BLOCK, BLOCK), BLOCK), :]
            row.append(jnp.where(here, 0.0, NONE))
        biases[i] = row
    return biases


def shared_blocks(n, per, place_ref, key_refs, val_refs, skip, glob, ends):
    plane = n // 4
    me = lax.axis_index("seq")
    place = lax.bitwise_and(me, plane - 1)
    biases = []
    for g in range(G):
        differ = lax.bitwise_xor(lax.div(place_ref[g], per), me)
        for p, pair in enumerate(zip(key_refs, val_refs)):
            @pl.when(lax.bitwise_and(differ, plane - 1) == p)
            def _(g=g, pair=pair):
                for c, ref in enumerate(pair):
                    at = pl.ds((c * G + g) * BLOCK, BLOCK)
                    glob[at] = ref[pl.ds(skip + g * BLOCK, BLOCK)]
        biases.append(jnp.where(differ < n // 2, 0.0, NONE))
    for e, neighbour in enumerate((place + plane - 1, place + 1)):
        k = lax.bitwise_xor(place, lax.bitwise_and(neighbour, plane - 1))
        for p, pair in enumerate(zip(key_refs, val_refs)):
            @pl.when(k == p)
            def _(e=e, pair=pair):
                for c, ref in enumerate(pair):
                    at = pl.ds((2 * e + c) * BLOCK, BLOCK)
                    ends[at] = ref[pl.ds(skip + G * BLOCK, BLOCK)]
    return biases


def widen(biases):
    count = len(biases)
    lane = lax.broadcasted_iota(I32, (1, count * BLOCK), 1)
    bias = jnp.full((1, count * BLOCK), biases[-1], F32)
    for r in reversed(range(count - 1)):
        bias = jnp.where(lane < (r + 1) * BLOCK, biases[r], bias)
    return bias


def batches(span, heads, step):
    for first in range(*span, step):
        yield [(i, h) for i in range(first, min(span[1], first + step)) for h in range(heads)]


def rows_of(i):
    return pl.ds(i * BLOCK, BLOCK)


def picked_of(i):
    return pl.ds(i * R * BLOCK, R * BLOCK)


def cols_of(h):
    return pl.ds(h * DH, DH)


def dot_t(a, b):
    return lax.dot_general(a, b, (((1,), (1,)), ((), ())), preferred_element_type=F32)


def eye():
    shape = (BLOCK, BLOCK)
    return lax.broadcasted_iota(I32, shape, 0) == lax.broadcasted_iota(I32, shape, 1)


def flatten(columns, diagonal):
    return [jnp.sum(jnp.where(diagonal, x, 0.0), axis=0, keepdims=True) for x in columns]


def attend(queries, sets):
    scale = 1.0 / math.sqrt(DH)
    s = [
        [dot_t(q, ks) * scale + bias if bias is not None else dot_t(q, ks) * scale
         for ks, vs, bias in group]
        for q, group in zip(queries, sets)
    ]
    top = [[jnp.max(x, axis=1, keepdims=True) for x in group] for group in s]
    top = [functools.reduce(jnp.maximum, group) for group in top]
    w = [[jnp.exp(x - t) for x in group] for group, t in zip(s, top)]
    total = [sum(jnp.sum(x, axis=1, keepdims=True) for x in group) for group in w]
    part = [
        sum(
            jnp.dot(x.astype(BF16), vs, preferred_element_type=F32)
            for x, (ks, vs, bias) in zip(ws, group)
        )
        for ws, group in zip(w, sets)
    ]
    return part, top, total


def far_kernel(n, cap, per, heads, span, arrive_ref, place_ref, q_ref, *refs):
    half, plane = n // 2, n // 4
    first, second = refs[:plane], (refs[plane:half], refs[half : half + plane])
    out_ref, held, keys, vals, glob, ends, stat, pieces = refs[half + plane + 1 :]
    me = lax.axis_index("seq")
    d = lax.bitwise_xor(me, half)
    diagonal = eye()
    stat[...] = jnp.zeros_like(stat)
    size = cap * BLOCK
    sources = [((ref, 0), (ref, size)) for ref in first]
    sources += [((x, 0), (y, 0)) for x, y in zip(*second)]
    biases = choose(n, cap, per, span, arrive_ref, d, sources, held, keys, vals)
    glob_bias = widen(shared_blocks(n, per, place_ref, *second, size, glob, ends))
    inside = lax.bitwise_and(me, half - 1)
    end_bias = [jnp.where(inside == x, 0.0, NONE) for x in (0, half - 1)]
    low, high = span
    count = high - low
    for pairs in batches(span, heads, 3):
        sets = []
        for i, h in pairs:
            cols = cols_of(h)
            group = [
                (keys[picked_of(i), cols], vals[picked_of(i), cols], widen(biases[i])),
                (glob[: G * BLOCK, cols], glob[G * BLOCK :, cols], glob_bias),
            ]
            for e, edge in enumerate((0, per - 1)):
                if i == edge:
                    at = e * 2 * BLOCK
                    group.append(
                        (ends[at : at + BLOCK, cols], ends[at + BLOCK : at + 2 * BLOCK, cols],
                         end_bias[e])
                    )
            sets.append(group)
        part, top, total = attend([q_ref[rows_of(i), cols_of(h)] for i, h in pairs], sets)
        for x, t, (i, h) in zip(part, total, pairs):
            out_ref[rows_of(i - low), cols_of(h)] = (x / t).astype(BF16)
        for c, columns in enumerate((top, total)):
            for x, (i, h) in zip(flatten(columns, diagonal), pairs):
                stat[i - low : i - low + 1, pl.ds(h * DH + c * BLOCK, BLOCK)] = x
    rest = stat[...]
    pieces[...] = jnp.zeros_like(pieces)
    for p in range(PIECES):
        piece = rest.astype(BF16).astype(F32)
        rest = rest - piece
        pieces[p * count : (p + 1) * count] = piece[:count]
    out_ref[pl.ds(count * BLOCK, pieces.shape[0])] = pieces[...].astype(BF16)


def stat_rows(per):
    return -(-per // 8) * 8


def piece_rows(per):
    return -(-PIECES * per // 16) * 16


def scratches(n, cap, per, columns):
    return (
        [pltpu.VMEM((n // 2, 2 * cap * BLOCK, columns), BF16)]
        + [pltpu.VMEM((per * R * BLOCK, columns), BF16)] * 2
        + [pltpu.VMEM((2 * G * BLOCK, columns), BF16), pltpu.VMEM((4 * BLOCK, columns), BF16)]
    )


def far_part(n, cap, per, span, arrive, places, q, got, earlier):
    columns = q.shape[1]
    count = span[1] - span[0]
    heads = columns // DH
    return pl.pallas_call(
        functools.partial(far_kernel, n, cap, per, heads, span),
        out_shape=jax.ShapeDtypeStruct((count * BLOCK + piece_rows(count), columns), BF16),
        in_specs=[spec(SMEM)] * 2 + [spec()] * (1 + len(got)) + [spec(pl.ANY)],
        out_specs=spec(),
        scratch_shapes=scratches(n, cap, per, columns)
        + [pltpu.VMEM((stat_rows(count), columns), F32)]
        + [pltpu.VMEM((piece_rows(count), columns), F32)],
        compiler_params=params(16),
        cost_estimate=HEAVY,
        name="far_part",
    )(arrive, places, q, *got, earlier)


def store_part(heads, pairs, part, top, total, part_ref, stat_ref, diagonal):
    for x, (i, h) in zip(part, pairs):
        part_ref[rows_of(i), cols_of(h)] = x
    for c, columns in enumerate((top, total)):
        for x, (i, h) in zip(flatten(columns, diagonal), pairs):
            stat_ref[i : i + 1, pl.ds(h * DH + c * BLOCK, BLOCK)] = x


def near_kernel(n, cap, per, heads, place_ref, q_ref, k_ref, v_ref, *refs):
    half, plane = n // 2, n // 4
    second = refs[:plane], refs[plane:half]
    part_ref, stat_ref, glob, ends, keys, vals = refs[half + 1 :]
    me = lax.axis_index("seq")
    rows = per * BLOCK
    diagonal = eye()
    stat_ref[...] = jnp.zeros_like(stat_ref)
    size = cap * BLOCK
    glob_bias = widen(shared_blocks(n, per, place_ref, *second, size, glob, ends))
    keys[:BLOCK] = ends[:BLOCK]
    vals[:BLOCK] = ends[BLOCK : 2 * BLOCK]
    keys[pl.ds(BLOCK, rows)] = k_ref[...]
    vals[pl.ds(BLOCK, rows)] = v_ref[...]
    keys[pl.ds(BLOCK + rows, BLOCK)] = ends[2 * BLOCK : 3 * BLOCK]
    vals[pl.ds(BLOCK + rows, BLOCK)] = ends[3 * BLOCK :]
    inside = lax.bitwise_and(me, half - 1)
    first_bias, last_bias = [jnp.where(inside == x, NONE, 0.0) for x in (0, half - 1)]
    for pairs in batches((0, per), heads, 2):
        sets = []
        for i, h in pairs:
            window, cols = pl.ds(i * BLOCK, 3 * BLOCK), cols_of(h)
            bias = None
            if i in (0, per - 1):
                bias = widen([first_bias if i == 0 else 0.0, 0.0, last_bias if i else 0.0])
            sets.append(
                [
                    (keys[window, cols], vals[window, cols], bias),
                    (glob[: G * BLOCK, cols], glob[G * BLOCK :, cols], glob_bias),
                ]
            )
        parts = attend([q_ref[rows_of(i), cols_of(h)] for i, h in pairs], sets)
        store_part(heads, pairs, *parts, part_ref, stat_ref, diagonal)


def part_shapes(per, columns):
    return (
        jax.ShapeDtypeStruct((per * BLOCK, columns), F32),
        jax.ShapeDtypeStruct((stat_rows(per), columns), F32),
    )


def near_part(n, cap, per, places, q, k, v, shared, earlier):
    rows, columns = q.shape
    heads = columns // DH
    return pl.pallas_call(
        functools.partial(near_kernel, n, cap, per, heads),
        out_shape=part_shapes(per, columns),
        in_specs=[spec(SMEM)] + [spec()] * (3 + len(shared)) + [spec(pl.ANY)],
        out_specs=(spec(), spec()),
        scratch_shapes=scratches(n, cap, per, columns)[3:]
        + [pltpu.VMEM((rows + 2 * BLOCK, columns), BF16)] * 2,
        compiler_params=params(16),
        cost_estimate=LIGHT,
        name="near_part",
    )(places, q, k, v, *shared, earlier)


def rand_kernel(n, cap, per, heads, arrive_ref, q_ref, *refs):
    plane = n // 4
    early, late = refs[:plane], refs[plane : 2 * plane]
    part_ref, stat_ref, held, keys, vals = refs[2 * plane :]
    diagonal = eye()
    stat_ref[...] = jnp.zeros_like(stat_ref)
    me = lax.axis_index("seq")
    size = cap * BLOCK
    sources = [((x, 2 * size), (y, 0)) for x, y in zip(early, late)]
    sources += [((y, size), (y, 2 * size)) for y in late]
    biases = choose(n, cap, per, (0, per), arrive_ref, me, sources, held, keys, vals)
    for pairs in batches((0, per), heads, 4):
        sets = [
            [(keys[picked_of(i), cols_of(h)], vals[picked_of(i), cols_of(h)], widen(biases[i]))]
            for i, h in pairs
        ]
        parts = attend([q_ref[rows_of(i), cols_of(h)] for i, h in pairs], sets)
        store_part(heads, pairs, *parts, part_ref, stat_ref, diagonal)


def rand_part(n, cap, per, arrive, q, early, late):
    columns = q.shape[1]
    return pl.pallas_call(
        functools.partial(rand_kernel, n, cap, per, columns // DH),
        out_shape=part_shapes(per, columns),
        in_specs=[spec(SMEM), spec()] + [spec()] * (len(early) + len(late)),
        out_specs=(spec(), spec()),
        scratch_shapes=scratches(n, cap, per, columns)[:3],
        compiler_params=params(16),
        cost_estimate=HEAVY,
        name="rand_part",
    )(arrive, q, *early, *late)


def context_kernel(
    span, heads, near_ref, near_stat_ref, rand_ref, rand_stat_ref, far_ref, out_ref, pieces
):
    low, high = span
    count = high - low
    pieces[...] = far_ref[pl.ds(count * BLOCK, pieces.shape[0])].astype(F32)
    far = sum(pieces[p * count : (p + 1) * count] for p in range(PIECES))
    stats = (near_stat_ref[low:high], rand_stat_ref[low:high], far)
    weights = []
    for h in range(heads):
        tops = [x[:, h * DH : h * DH + BLOCK] for x in stats]
        sums = [x[:, h * DH + BLOCK : (h + 1) * DH] for x in stats]
        top = functools.reduce(jnp.maximum, tops)
        w = [jnp.exp(x - top) for x in tops]
        total = sum(x * y for x, y in zip(w, sums))
        w[2] = w[2] * sums[2]
        weights.append([jnp.transpose(x / total) for x in w])
    for i in range(count):
        for h, ws in enumerate(weights):
            rows, here, cols = rows_of(low + i), rows_of(i), cols_of(h)
            parts = (near_ref[rows, cols], rand_ref[rows, cols], far_ref[here, cols].astype(F32))
            out_ref[here, cols] = sum(x * w[:, i : i + 1] for x, w in zip(parts, ws)).astype(BF16)


def contexts(span, near, near_stat, rand, rand_stat, far):
    columns = near.shape[1]
    count = span[1] - span[0]
    return pl.pallas_call(
        functools.partial(context_kernel, span, columns // DH),
        out_shape=jax.ShapeDtypeStruct((count * BLOCK, columns), BF16),
        in_specs=[spec()] * 5,
        out_specs=spec(),
        scratch_shapes=[pltpu.VMEM((piece_rows(count), columns), F32)],
        compiler_params=params(8),
        cost_estimate=LIGHT,
        name="contexts",
    )(near, near_stat, rand, rand_stat, far)


def project_kernel(span, count, steps, *refs):
    parts, w_ref, (out_ref, joined, product, sems) = refs[:count], refs[count], refs[-4:]
    me = lax.axis_index("head")
    columns = parts[0].shape[1]
    for step, rows_ref in enumerate(parts):
        owner = lax.rem(me + step, count)
        for h in range(count):
            @pl.when(owner == h)
            def _(h=h, rows_ref=rows_ref):
                joined[:, pl.ds(h * columns, columns)] = rows_ref[...]
    size = joined.shape[0] // steps
    copies = []
    for step in range(steps):
        rows = pl.ds(step * size, size)
        product[rows] = jnp.dot(
            joined[rows], w_ref[...], preferred_element_type=F32
        ).astype(BF16)
        target = out_ref.at[pl.ds(span[0] * BLOCK + step * size, size)]
        copies.append(pltpu.make_async_copy(product.at[rows], target, sems.at[step]))
        copies[-1].start()
    for copy in copies:
        copy.wait()


def project(span, tokens, parts, w_out, done=None):
    rows = parts[0].shape[0]
    wide = w_out.shape[1]
    steps = 4
    before = [] if done is None else [done]
    return pl.pallas_call(
        functools.partial(project_kernel, span, len(parts), steps),
        out_shape=jax.ShapeDtypeStruct((tokens, wide), BF16),
        in_specs=[spec()] * (len(parts) + 1) + [spec(pl.ANY)] * len(before),
        out_specs=spec(pl.ANY),
        scratch_shapes=[
            pltpu.VMEM((rows, w_out.shape[0]), BF16),
            pltpu.VMEM((rows, wide), BF16),
            pltpu.SemaphoreType.DMA((steps,)),
        ],
        input_output_aliases={len(parts) + 1: 0} if before else {},
        compiler_params=params(16),
        cost_estimate=LIGHT,
        name="project",
    )(*parts, w_out, *before)


def on_device(queries, keys, values, rand_group, rand_offset, glob_blocks, w_out):
    tokens_dev = queries.shape[0]
    per = tokens_dev // BLOCK
    n = lax.axis_size("seq")
    heads = lax.axis_size("head")
    cap = max(2, (rand_group.shape[0] // n * R + n - 1) // n)

    mates = [(i, i ^ (n // 4)) for i in range(n)]
    partners = [(i, i ^ (n // 2)) for i in range(n)]
    mate_k = lax.ppermute(keys, "seq", mates)
    mate_v = lax.ppermute(values, "seq", mates)
    later_q, _ = lax.optimization_barrier((queries, mate_k))
    far_q = lax.ppermute(later_q, "seq", partners)
    spots, arrive = ranks(n, per, cap, rand_group.T, rand_offset.T)
    rows = {(0, 0): keys, (0, 1): values}
    lists = ((0, True, (0, 1)), (0, False, (0,)))
    first = exchange(gather(n, per, cap, lists, spots, rows), n)
    rows = {(0, 0): keys, (1, 0): mate_k}
    lists = ((1, True, (0,)),)
    second_k = exchange(gather(n, per, cap, lists, spots, rows, [glob_blocks], first[1:4]), n)
    rows = {(0, 1): values, (1, 1): mate_v}
    lists = ((1, True, (1,)),)
    sent = gather(n, per, cap, lists, spots, rows, [glob_blocks], second_k[1:2])
    second = second_k + exchange(sent, n)
    rows = {(0, 0): keys, (0, 1): values, (1, 0): mate_k, (1, 1): mate_v}
    lists = ((0, False, (1,)), (1, False, (0, 1)))
    third = gather(n, per, cap, lists, spots, rows, (), sent[:1])
    middle = (per + 1) // 2
    spans = ((0, middle), (middle, per))
    fars = []
    earlier = third[0]
    for span in spans:
        earlier = far_part(
            n, cap, per, span, arrive, glob_blocks, far_q, first + second, earlier
        )
        fars.append(lax.ppermute(earlier, "seq", partners))
    third = exchange(third, n)
    near, near_stat = near_part(n, cap, per, glob_blocks, queries, keys, values, second, earlier)
    rand, rand_stat = rand_part(n, cap, per, arrive, queries, first, third)
    out = None
    for span, far in zip(spans, fars):
        context = contexts(span, near, near_stat, rand, rand_stat, far)
        others = [
            lax.ppermute(context, "head", [((i + s) % heads, i) for i in range(heads)])
            for s in range(1, heads)
        ]
        out = project(span, tokens_dev, [context] + others, w_out, out)
    return out


def solution(mesh):
    return jax.shard_map(
        on_device,
        mesh=mesh,
        in_specs=(
            P("seq", "head"),
            P("seq", "head"),
            P("seq", "head"),
            P(),
            P(),
            P(),
            P(None, "head"),
        ),
        out_specs=P("seq", "head"),
        check_vma=False,
    )
```

profile of v0, /device:TPU:0, one launch (start us, length us, event | category | flops | bytes accessed | tf_op | source)
XLA Modules:
  0.0 87.5 jit_solution(17858708987874586343)
XLA Ops:
  0.0 3.0 %collective-permute-start = (bf16[1088,256]{1,0:T(8,128)(2,1)}, bf16[1088,256]{1,0:T(8,128)(2,1)S(1)}, u32[]{:S(2)}, u32[]{:S(2)}) collective-permute-start(bf16[1088,256]{1,0:T(8,128)(2,1)} %k_ref.1), channel_id=1, source_target_pairs={{0,8},{2,10},{4,12},{6,14},{8,0},{10,2},{12,4},{14,6},{16,24},{18,... | collective-permute-start | bytes 1671176 | tf_op jit(solution)/shard_map/ppermute | solution.py:543
  3.0 0.0 copy-start.4
  3.0 0.7 copy-done.4
  3.7 0.7 copy-done.5
  4.4 0.4 ranks.1
  4.8 1.1 %copy-done = bf16[1088,256]{1,0:T(8,128)(2,1)S(1)} copy-done((bf16[1088,256]{1,0:T(8,128)(2,1)S(1)}, bf16[1088,256]{1,0:T(8,128)(2,1)}, u32[]{:S(2)}) %copy-start) | copy-done | bytes 557080
  5.8 1.2 %gather_blocks.4 = (bf16[768,256]{1,0:T(8,128)(2,1)S(1)}, bf16[768,256]{1,0:T(8,128)(2,1)S(1)}, bf16[768,256]{1,0:T(8,128)(2,1)S(1)}, bf16[768,256]{1,0:T(8,128)(2,1)S(1)}) custom-call(s32[8,128]{1,0:T(8,128)S(1)} %get-tuple-element.28.spot_ref, bf16[1088,256]{1,0:T(8,128)(2,1)S(1)} %copy-done, bf16[1088,256]{1,0:T(8,128)(2,1)} %v_ref.1), custom_call_target="tpu_custom_call" | custom-call | flops 1 | bytes 1 | tf_op jit(solution)/shard_map/gather_blocks/pallas_call | solution.py:137
  7.0 0.0 copy-start.1
  7.0 1.6 %collective-permute-start.1 = (bf16[768,256]{1,0:T(8,128)(2,1)S(1)}, bf16[768,256]{1,0:T(8,128)(2,1)S(1)}, u32[]{:S(2)}, u32[]{:S(2)}) collective-permute-start(bf16[768,256]{1,0:T(8,128)(2,1)S(1)} %get-tuple-element.29), channel_id=1, source_target_pairs={{0,2},{2,0},{4,6},{6,4},{8,10},{10,8},{12,14},{14,12},{16,18},{18,... | collective-permute-start | bytes 1179656 | tf_op jit(solution)/shard_map/ppermute | solution.py:154
  8.6 1.5 %collective-permute-start.2 = (bf16[768,256]{1,0:T(8,128)(2,1)S(1)}, bf16[768,256]{1,0:T(8,128)(2,1)S(1)}, u32[]{:S(2)}, u32[]{:S(2)}) collective-permute-start(bf16[768,256]{1,0:T(8,128)(2,1)S(1)} %get-tuple-element.30), channel_id=1, source_target_pairs={{0,4},{2,6},{4,0},{6,2},{8,12},{10,14},{12,8},{14,10},{16,20},{18,... | collective-permute-start | bytes 1179656 | tf_op jit(solution)/shard_map/ppermute | solution.py:154
  10.1 0.5 collective-permute-start.3
  10.6 0.0 collective-permute-start.7
  10.6 6.1 %collective-permute-done.refs_1_.refs_2_ = bf16[1088,256]{1,0:T(8,128)(2,1)S(1)} collective-permute-done((bf16[1088,256]{1,0:T(8,128)(2,1)}, bf16[1088,256]{1,0:T(8,128)(2,1)S(1)}, u32[]{:S(2)}, u32[]{:S(2)}) %collective-permute-start) | collective-permute-done | bytes 557088 | tf_op jit(solution)/shard_map/ppermute | solution.py:543
  16.7 3.1 %collective-permute-start.11 = (bf16[1088,256]{1,0:T(8,128)(2,1)}, bf16[1088,256]{1,0:T(8,128)(2,1)S(1)}, u32[]{:S(2)}, u32[]{:S(2)}) collective-permute-start(bf16[1088,256]{1,0:T(8,128)(2,1)} %q_ref.3), channel_id=1, source_target_pairs={{0,16},{2,18},{4,20},{6,22},{8,24},{10,26},{12,28},{14,30},{16,0},... | collective-permute-start | bytes 1671176 | tf_op jit(solution)/shard_map/ppermute | solution.py:546
  19.8 0.0 collective-permute-done.1.refs_3_.refs_1_
  19.8 7.5 %collective-permute-done.2.refs_4_.refs_2_ = bf16[768,256]{1,0:T(8,128)(2,1)S(1)} collective-permute-done((bf16[768,256]{1,0:T(8,128)(2,1)S(1)}, bf16[768,256]{1,0:T(8,128)(2,1)S(1)}, u32[]{:S(2)}, u32[]{:S(2)}) %collective-permute-start.2) | collective-permute-done | bytes 393248 | tf_op jit(solution)/shard_map/ppermute | solution.py:154
  27.3 0.0 collective-permute-done.3.refs_5_.refs_3_
  27.3 0.7 copy-done.6
  28.0 0.7 gather_blocks.5
  28.7 0.0 copy-start.7
  28.7 1.3 %collective-permute-start.4 = (bf16[448,256]{1,0:T(8,128)(2,1)S(1)}, bf16[448,256]{1,0:T(8,128)(2,1)S(1)}, u32[]{:S(2)}, u32[]{:S(2)}) collective-permute-start(bf16[448,256]{1,0:T(8,128)(2,1)S(1)} %get-tuple-element.33), channel_id=1, source_target_pairs={{0,2},{2,0},{4,6},{6,4},{8,10},{10,8},{12,14},{14,12},{16,18},{18,... | collective-permute-start | bytes 688136 | tf_op jit(solution)/shard_map/ppermute | solution.py:154
  30.0 0.8 collective-permute-start.5
  30.8 1.4 %collective-permute-start.6 = (bf16[448,256]{1,0:T(8,128)(2,1)S(1)}, bf16[448,256]{1,0:T(8,128)(2,1)S(1)}, u32[]{:S(2)}, u32[]{:S(2)}) collective-permute-start(bf16[448,256]{1,0:T(8,128)(2,1)S(1)} %get-tuple-element.35), channel_id=1, source_target_pairs={{0,6},{2,4},{4,2},{6,0},{8,14},{10,12},{12,10},{14,8},{16,22},{18,... | collective-permute-start | bytes 688136 | tf_op jit(solution)/shard_map/ppermute | solution.py:154
  32.2 6.8 %collective-permute-done.7.refs_1_.refs_3_ = bf16[1088,256]{1,0:T(8,128)(2,1)S(1)} collective-permute-done((bf16[1088,256]{1,0:T(8,128)(2,1)}, bf16[1088,256]{1,0:T(8,128)(2,1)S(1)}, u32[]{:S(2)}, u32[]{:S(2)}) %collective-permute-start.7) | collective-permute-done | bytes 557088 | tf_op jit(solution)/shard_map/ppermute | solution.py:544
  39.0 0.0 collective-permute-done.4.refs_3_.refs_5_.refs_1_
  39.0 1.2 %gather_blocks.6 = (bf16[448,256]{1,0:T(8,128)(2,1)S(1)}, bf16[448,256]{1,0:T(8,128)(2,1)S(1)}, bf16[448,256]{1,0:T(8,128)(2,1)S(1)}, bf16[448,256]{1,0:T(8,128)(2,1)S(1)}) custom-call(s32[8,128]{1,0:T(8,128)S(1)} %get-tuple-element.28.spot_ref, bf16[1088,256]{1,0:T(8,128)(2,1)} %v_ref.1, bf16[1088,256]{1,0:T(8,128)(2,1)S(1)} %collective-permute-done.7.refs_1_.refs_3_, ...), custom_call_target="tpu_custom_call" | custom-call | flops 1 | bytes 1 | tf_op jit(solution)/shard_map/gather_blocks/pallas_call | solution.py:137
  40.2 1.9 %collective-permute-start.8 = (bf16[448,256]{1,0:T(8,128)(2,1)S(1)}, bf16[448,256]{1,0:T(8,128)(2,1)S(1)}, u32[]{:S(2)}, u32[]{:S(2)}) collective-permute-start(bf16[448,256]{1,0:T(8,128)(2,1)S(1)} %get-tuple-element.37), channel_id=1, source_target_pairs={{0,2},{2,0},{4,6},{6,4},{8,10},{10,8},{12,14},{14,12},{16,18},{18,... | collective-permute-start | bytes 688136 | tf_op jit(solution)/shard_map/ppermute | solution.py:154
  42.0 1.5 %collective-permute-start.9 = (bf16[448,256]{1,0:T(8,128)(2,1)S(1)}, bf16[448,256]{1,0:T(8,128)(2,1)S(1)}, u32[]{:S(2)}, u32[]{:S(2)}) collective-permute-start(bf16[448,256]{1,0:T(8,128)(2,1)S(1)} %get-tuple-element.38), channel_id=1, source_target_pairs={{0,4},{2,6},{4,0},{6,2},{8,12},{10,14},{12,8},{14,10},{16,20},{18,... | collective-permute-start | bytes 688136 | tf_op jit(solution)/shard_map/ppermute | solution.py:154
  43.6 0.0 collective-permute-done.5.refs_6_.refs_2_
  43.6 0.2 collective-permute-start.10
  43.7 0.0 copy-done.1
  43.7 1.2 %gather_blocks.7 = (bf16[768,256]{1,0:T(8,128)(2,1)S(1)}, bf16[768,256]{1,0:T(8,128)(2,1)S(1)}, bf16[768,256]{1,0:T(8,128)(2,1)S(1)}, bf16[768,256]{1,0:T(8,128)(2,1)S(1)}) custom-call(s32[8,128]{1,0:T(8,128)S(1)} %get-tuple-element.28.spot_ref, bf16[1088,256]{1,0:T(8,128)(2,1)S(1)} %copy-done.1, bf16[1088,256]{1,0:T(8,128)(2,1)} %v_ref.1, ...), custom_call_target="tpu_custom_call" | custom-call | flops 1 | bytes 1 | tf_op jit(solution)/shard_map/gather_blocks/pallas_call | solution.py:137
  44.9 0.0 collective-permute-done.6.refs_7_.refs_3_
  44.9 1.9 %collective-permute-start.12 = (bf16[768,256]{1,0:T(8,128)(2,1)S(1)}, bf16[768,256]{1,0:T(8,128)(2,1)S(1)}, u32[]{:S(2)}, u32[]{:S(2)}) collective-permute-start(bf16[768,256]{1,0:T(8,128)(2,1)S(1)} %get-tuple-element.46), channel_id=1, source_target_pairs={{0,2},{2,0},{4,6},{6,4},{8,10},{10,8},{12,14},{14,12},{16,18},{18,... | collective-permute-start | bytes 1179656 | tf_op jit(solution)/shard_map/ppermute | solution.py:154
  46.8 2.0 %collective-permute-done.8.refs_9_.refs_5_ = bf16[448,256]{1,0:T(8,128)(2,1)S(1)} collective-permute-done((bf16[448,256]{1,0:T(8,128)(2,1)S(1)}, bf16[448,256]{1,0:T(8,128)(2,1)S(1)}, u32[]{:S(2)}, u32[]{:S(2)}) %collective-permute-start.8) | collective-permute-done | bytes 229408 | tf_op jit(solution)/shard_map/ppermute | solution.py:154
  48.8 1.8 %collective-permute-start.13 = (bf16[768,256]{1,0:T(8,128)(2,1)S(1)}, bf16[768,256]{1,0:T(8,128)(2,1)S(1)}, u32[]{:S(2)}, u32[]{:S(2)}) collective-permute-start(bf16[768,256]{1,0:T(8,128)(2,1)S(1)} %get-tuple-element.47), channel_id=1, source_target_pairs={{0,4},{2,6},{4,0},{6,2},{8,12},{10,14},{12,8},{14,10},{16,20},{18,... | collective-permute-start | bytes 1179656 | tf_op jit(solution)/shard_map/ppermute | solution.py:154
  50.6 3.3 %collective-permute-done.9.refs_10_.refs_6_ = bf16[448,256]{1,0:T(8,128)(2,1)S(1)} collective-permute-done((bf16[448,256]{1,0:T(8,128)(2,1)S(1)}, bf16[448,256]{1,0:T(8,128)(2,1)S(1)}, u32[]{:S(2)}, u32[]{:S(2)}) %collective-permute-start.9) | collective-permute-done | bytes 229408 | tf_op jit(solution)/shard_map/ppermute | solution.py:154
  53.9 0.8 collective-permute-start.14
  54.7 0.2 collective-permute-done.10.refs_11_.refs_7_
  55.0 0.0 collective-permute-done.11.q_ref
  55.0 0.0 copy-done.7
  55.0 3.2 %far_part.2.refs_12_ = bf16[608,256]{1,0:T(8,128)(2,1)S(1)} custom-call(s32[8,384]{1,0:T(8,128)S(1)} %get-tuple-element.40.arrive_ref, s32[2]{0:T(128)S(1)} %copy-done.7, bf16[1088,256]{1,0:T(8,128)(2,1)S(1)} %collective-permute-done.11.q_ref, bf16[768,256]{1,0:T(8,128)(2,1)S(1)} %get-tuple-element.42.refs_0_, ...), custom_call_target="tpu_custom_call" | custom-call | flops 4000000000 | bytes 1 | tf_op jit(solution)/shard_map/far_part/pallas_call | solution.py:335
  58.1 0.0 copy-start.3
  58.2 0.6 collective-permute-start.17
  58.8 2.9 %far_part.3.refs_8_ = bf16[544,256]{1,0:T(8,128)(2,1)S(1)} custom-call(s32[8,384]{1,0:T(8,128)S(1)} %get-tuple-element.40.arrive_ref, s32[2]{0:T(128)S(1)} %copy-done.7, bf16[1088,256]{1,0:T(8,128)(2,1)S(1)} %collective-permute-done.11.q_ref, bf16[768,256]{1,0:T(8,128)(2,1)S(1)} %get-tuple-element.42.refs_0_, ...), custom_call_target="tpu_custom_call" | custom-call | flops 4000000000 | bytes 1 | tf_op jit(solution)/shard_map/far_part/pallas_call | solution.py:335
  61.7 2.4 %collective-permute-start.15 = (bf16[544,256]{1,0:T(8,128)(2,1)S(1)}, bf16[544,256]{1,0:T(8,128)(2,1)S(1)}, u32[]{:S(2)}, u32[]{:S(2)}) collective-permute-start(bf16[544,256]{1,0:T(8,128)(2,1)S(1)} %far_part.3.refs_8_), channel_id=1, source_target_pairs={{0,16},{2,18},{4,20},{6,22},{8,24},{10,26},{12,28},{14,30},{16,0},... | collective-permute-start | bytes 835592 | tf_op jit(solution)/shard_map/ppermute | solution.py:569
  64.1 0.0 copy-done.3
  64.1 5.4 %near_part.1 = (f32[1088,256]{1,0:T(8,128)S(1)}, f32[24,256]{1,0:T(8,128)S(1)}) custom-call(s32[2]{0:T(128)S(1)} %copy-done.7, bf16[1088,256]{1,0:T(8,128)(2,1)S(1)} %copy-done.3, bf16[1088,256]{1,0:T(8,128)(2,1)S(1)} %copy-done.1, bf16[1088,256]{1,0:T(8,128)(2,1)} %v_ref.1, bf16[448,256]{1,0:T(8,128)(2,1)S(1)} %get-tuple-element.32.refs_4_.refs_0_, ...), custom_call_target="tpu_custom_call" | custom-call | flops 1 | bytes 1 | tf_op jit(solution)/shard_map/near_part/pallas_call | solution.py:402
  69.6 0.0 collective-permute-done.12.refs_5_
  69.6 0.4 collective-permute-done.13.refs_6_
  70.0 0.0 collective-permute-done.14.refs_7_
  70.0 3.4 %rand_part.1 = (f32[1088,256]{1,0:T(8,128)S(1)}, f32[24,256]{1,0:T(8,128)S(1)}) custom-call(s32[8,384]{1,0:T(8,128)S(1)} %get-tuple-element.40.arrive_ref, bf16[1088,256]{1,0:T(8,128)(2,1)S(1)} %copy-done.3, bf16[768,256]{1,0:T(8,128)(2,1)S(1)} %get-tuple-element.42.refs_0_, bf16[768,256]{1,0:T(8,128)(2,1)S(1)} %collective-permute-done.1.refs_3_.refs_1_, ...), custom_call_target="tpu_custom_call" | custom-call | flops 4000000000 | bytes 1 | tf_op jit(solution)/shard_map/rand_part/pallas_call | solution.py:437
  73.4 4.5 %collective-permute-done.17.far_ref = bf16[608,256]{1,0:T(8,128)(2,1)S(1)} collective-permute-done((bf16[608,256]{1,0:T(8,128)(2,1)S(1)}, bf16[608,256]{1,0:T(8,128)(2,1)S(1)}, u32[]{:S(2)}, u32[]{:S(2)}) %collective-permute-start.17) | collective-permute-done | bytes 311328 | tf_op jit(solution)/shard_map/ppermute | solution.py:569
  77.9 0.7 contexts.3.refs_0_
  78.6 0.0 copy-start.2
  78.6 0.1 collective-permute-start.18
  78.7 3.4 %collective-permute-done.15.far_ref = bf16[544,256]{1,0:T(8,128)(2,1)S(1)} collective-permute-done((bf16[544,256]{1,0:T(8,128)(2,1)S(1)}, bf16[544,256]{1,0:T(8,128)(2,1)S(1)}, u32[]{:S(2)}, u32[]{:S(2)}) %collective-permute-start.15) | collective-permute-done | bytes 278560 | tf_op jit(solution)/shard_map/ppermute | solution.py:569
  82.1 0.7 contexts.2.refs_0_
  82.7 0.1 collective-permute-start.16
  82.8 0.0 collective-permute-done.18.refs_1_
  82.8 0.0 copy-done.2
  82.8 2.3 %project.2.refs_3_ = bf16[1088,2048]{1,0:T(8,128)(2,1)} custom-call(bf16[576,256]{1,0:T(8,128)(2,1)S(1)} %contexts.3.refs_0_, bf16[576,256]{1,0:T(8,128)(2,1)S(1)} %collective-permute-done.18.refs_1_, bf16[512,2048]{1,0:T(8,128)(2,1)S(1)} %copy-done.2), custom_call_target="tpu_custom_call" | custom-call | flops 1 | bytes 1 | tf_op jit(solution)/shard_map/project/pallas_call | solution.py:517
  85.1 0.0 collective-permute-done.16.refs_1_
  85.2 2.2 %project.3 = bf16[1088,2048]{1,0:T(8,128)(2,1)} custom-call(bf16[512,256]{1,0:T(8,128)(2,1)S(1)} %contexts.2.refs_0_, bf16[512,256]{1,0:T(8,128)(2,1)S(1)} %collective-permute-done.16.refs_1_, bf16[512,2048]{1,0:T(8,128)(2,1)S(1)} %copy-done.2, bf16[1088,2048]{1,0:T(8,128)(2,1)} %project.2.refs_3_), custom_call_target="tpu_custom_call", output_to_operand_aliasing={{}: (3, {})} | custom-call | flops 1 | bytes 1 | tf_op jit(solution)/shard_map/project/pallas_call | solution.py:517
  (3 shorter events, 0.0 us)
Async XLA Ops:
  0.0 16.7 %collective-permute-start = (bf16[1088,256]{1,0:T(8,128)(2,1)}, bf16[1088,256]{1,0:T(8,128)(2,1)S(1)}, u32[]{:S(2)}, u32[]{:S(2)}) collective-permute-start(bf16[1088,256]{1,0:T(8,128)(2,1)} %k_ref.1), channel_id=1, source_target_pairs={{0,8},{2,10},{4,12},{6,14},{8,0},{10,2},{12,4},{14,6},{16,24},{18,... | collective-permute-start | bytes 1671176 | tf_op jit(solution)/shard_map/ppermute | solution.py:543
  3.0 0.7 copy-start.4
  3.7 0.7 copy-start.5
  4.8 1.1 %copy-start = (bf16[1088,256]{1,0:T(8,128)(2,1)S(1)}, bf16[1088,256]{1,0:T(8,128)(2,1)}, u32[]{:S(2)}) copy-start(bf16[1088,256]{1,0:T(8,128)(2,1)} %k_ref.1) | copy-start | bytes 1671172
  7.0 36.7 %copy-start.1 = (bf16[1088,256]{1,0:T(8,128)(2,1)S(1)}, bf16[1088,256]{1,0:T(8,128)(2,1)}, u32[]{:S(2)}) copy-start(bf16[1088,256]{1,0:T(8,128)(2,1)} %k_ref.1) | copy-start | bytes 1671172
  7.0 12.7 %collective-permute-start.1 = (bf16[768,256]{1,0:T(8,128)(2,1)S(1)}, bf16[768,256]{1,0:T(8,128)(2,1)S(1)}, u32[]{:S(2)}, u32[]{:S(2)}) collective-permute-start(bf16[768,256]{1,0:T(8,128)(2,1)S(1)} %get-tuple-element.29), channel_id=1, source_target_pairs={{0,2},{2,0},{4,6},{6,4},{8,10},{10,8},{12,14},{14,12},{16,18},{18,... | collective-permute-start | bytes 1179656 | tf_op jit(solution)/shard_map/ppermute | solution.py:154
  8.6 18.7 %collective-permute-start.2 = (bf16[768,256]{1,0:T(8,128)(2,1)S(1)}, bf16[768,256]{1,0:T(8,128)(2,1)S(1)}, u32[]{:S(2)}, u32[]{:S(2)}) collective-permute-start(bf16[768,256]{1,0:T(8,128)(2,1)S(1)} %get-tuple-element.30), channel_id=1, source_target_pairs={{0,4},{2,6},{4,0},{6,2},{8,12},{10,14},{12,8},{14,10},{16,20},{18,... | collective-permute-start | bytes 1179656 | tf_op jit(solution)/shard_map/ppermute | solution.py:154
  10.1 17.2 %collective-permute-start.3 = (bf16[768,256]{1,0:T(8,128)(2,1)S(1)}, bf16[768,256]{1,0:T(8,128)(2,1)S(1)}, u32[]{:S(2)}, u32[]{:S(2)}) collective-permute-start(bf16[768,256]{1,0:T(8,128)(2,1)S(1)} %get-tuple-element.31), channel_id=1, source_target_pairs={{0,6},{2,4},{4,2},{6,0},{8,14},{10,12},{12,10},{14,8},{16,22},{18,... | collective-permute-start | bytes 1179656 | tf_op jit(solution)/shard_map/ppermute | solution.py:154
  10.6 28.4 %collective-permute-start.7 = (bf16[1088,256]{1,0:T(8,128)(2,1)}, bf16[1088,256]{1,0:T(8,128)(2,1)S(1)}, u32[]{:S(2)}, u32[]{:S(2)}) collective-permute-start(bf16[1088,256]{1,0:T(8,128)(2,1)} %v_ref.1), channel_id=1, source_target_pairs={{0,8},{2,10},{4,12},{6,14},{8,0},{10,2},{12,4},{14,6},{16,24},{18,... | collective-permute-start | bytes 1671176 | tf_op jit(solution)/shard_map/ppermute | solution.py:544
  16.7 38.3 %collective-permute-start.11 = (bf16[1088,256]{1,0:T(8,128)(2,1)}, bf16[1088,256]{1,0:T(8,128)(2,1)S(1)}, u32[]{:S(2)}, u32[]{:S(2)}) collective-permute-start(bf16[1088,256]{1,0:T(8,128)(2,1)} %q_ref.3), channel_id=1, source_target_pairs={{0,16},{2,18},{4,20},{6,22},{8,24},{10,26},{12,28},{14,30},{16,0},... | collective-permute-start | bytes 1671176 | tf_op jit(solution)/shard_map/ppermute | solution.py:546
  27.3 0.7 copy-start.6
  28.7 26.3 %copy-start.7 = (s32[2]{0:T(128)S(1)}, s32[2]{0:T(128)}, u32[]{:S(2)}) copy-start(s32[2]{0:T(128)} %place_ref.5) | copy-start | bytes 28
  28.7 10.3 %collective-permute-start.4 = (bf16[448,256]{1,0:T(8,128)(2,1)S(1)}, bf16[448,256]{1,0:T(8,128)(2,1)S(1)}, u32[]{:S(2)}, u32[]{:S(2)}) collective-permute-start(bf16[448,256]{1,0:T(8,128)(2,1)S(1)} %get-tuple-element.33), channel_id=1, source_target_pairs={{0,2},{2,0},{4,6},{6,4},{8,10},{10,8},{12,14},{14,12},{16,18},{18,... | collective-permute-start | bytes 688136 | tf_op jit(solution)/shard_map/ppermute | solution.py:154
  30.0 13.6 %collective-permute-start.5 = (bf16[448,256]{1,0:T(8,128)(2,1)S(1)}, bf16[448,256]{1,0:T(8,128)(2,1)S(1)}, u32[]{:S(2)}, u32[]{:S(2)}) collective-permute-start(bf16[448,256]{1,0:T(8,128)(2,1)S(1)} %get-tuple-element.34), channel_id=1, source_target_pairs={{0,4},{2,6},{4,0},{6,2},{8,12},{10,14},{12,8},{14,10},{16,20},{18,... | collective-permute-start | bytes 688136 | tf_op jit(solution)/shard_map/ppermute | solution.py:154
  30.8 14.1 %collective-permute-start.6 = (bf16[448,256]{1,0:T(8,128)(2,1)S(1)}, bf16[448,256]{1,0:T(8,128)(2,1)S(1)}, u32[]{:S(2)}, u32[]{:S(2)}) collective-permute-start(bf16[448,256]{1,0:T(8,128)(2,1)S(1)} %get-tuple-element.35), channel_id=1, source_target_pairs={{0,6},{2,4},{4,2},{6,0},{8,14},{10,12},{12,10},{14,8},{16,22},{18,... | collective-permute-start | bytes 688136 | tf_op jit(solution)/shard_map/ppermute | solution.py:154
  40.2 8.6 %collective-permute-start.8 = (bf16[448,256]{1,0:T(8,128)(2,1)S(1)}, bf16[448,256]{1,0:T(8,128)(2,1)S(1)}, u32[]{:S(2)}, u32[]{:S(2)}) collective-permute-start(bf16[448,256]{1,0:T(8,128)(2,1)S(1)} %get-tuple-element.37), channel_id=1, source_target_pairs={{0,2},{2,0},{4,6},{6,4},{8,10},{10,8},{12,14},{14,12},{16,18},{18,... | collective-permute-start | bytes 688136 | tf_op jit(solution)/shard_map/ppermute | solution.py:154
  42.0 11.9 %collective-permute-start.9 = (bf16[448,256]{1,0:T(8,128)(2,1)S(1)}, bf16[448,256]{1,0:T(8,128)(2,1)S(1)}, u32[]{:S(2)}, u32[]{:S(2)}) collective-permute-start(bf16[448,256]{1,0:T(8,128)(2,1)S(1)} %get-tuple-element.38), channel_id=1, source_target_pairs={{0,4},{2,6},{4,0},{6,2},{8,12},{10,14},{12,8},{14,10},{16,20},{18,... | collective-permute-start | bytes 688136 | tf_op jit(solution)/shard_map/ppermute | solution.py:154
  43.6 11.4 %collective-permute-start.10 = (bf16[448,256]{1,0:T(8,128)(2,1)S(1)}, bf16[448,256]{1,0:T(8,128)(2,1)S(1)}, u32[]{:S(2)}, u32[]{:S(2)}) collective-permute-start(bf16[448,256]{1,0:T(8,128)(2,1)S(1)} %get-tuple-element.39), channel_id=1, source_target_pairs={{0,6},{2,4},{4,2},{6,0},{8,14},{10,12},{12,10},{14,8},{16,22},{18,... | collective-permute-start | bytes 688136 | tf_op jit(solution)/shard_map/ppermute | solution.py:154
  44.9 24.7 %collective-permute-start.12 = (bf16[768,256]{1,0:T(8,128)(2,1)S(1)}, bf16[768,256]{1,0:T(8,128)(2,1)S(1)}, u32[]{:S(2)}, u32[]{:S(2)}) collective-permute-start(bf16[768,256]{1,0:T(8,128)(2,1)S(1)} %get-tuple-element.46), channel_id=1, source_target_pairs={{0,2},{2,0},{4,6},{6,4},{8,10},{10,8},{12,14},{14,12},{16,18},{18,... | collective-permute-start | bytes 1179656 | tf_op jit(solution)/shard_map/ppermute | solution.py:154
  48.8 21.2 %collective-permute-start.13 = (bf16[768,256]{1,0:T(8,128)(2,1)S(1)}, bf16[768,256]{1,0:T(8,128)(2,1)S(1)}, u32[]{:S(2)}, u32[]{:S(2)}) collective-permute-start(bf16[768,256]{1,0:T(8,128)(2,1)S(1)} %get-tuple-element.47), channel_id=1, source_target_pairs={{0,4},{2,6},{4,0},{6,2},{8,12},{10,14},{12,8},{14,10},{16,20},{18,... | collective-permute-start | bytes 1179656 | tf_op jit(solution)/shard_map/ppermute | solution.py:154
  53.9 16.1 %collective-permute-start.14 = (bf16[768,256]{1,0:T(8,128)(2,1)S(1)}, bf16[768,256]{1,0:T(8,128)(2,1)S(1)}, u32[]{:S(2)}, u32[]{:S(2)}) collective-permute-start(bf16[768,256]{1,0:T(8,128)(2,1)S(1)} %get-tuple-element.48), channel_id=1, source_target_pairs={{0,6},{2,4},{4,2},{6,0},{8,14},{10,12},{12,10},{14,8},{16,22},{18,... | collective-permute-start | bytes 1179656 | tf_op jit(solution)/shard_map/ppermute | solution.py:154
  58.1 6.0 %copy-start.3 = (bf16[1088,256]{1,0:T(8,128)(2,1)S(1)}, bf16[1088,256]{1,0:T(8,128)(2,1)}, u32[]{:S(2)}) copy-start(bf16[1088,256]{1,0:T(8,128)(2,1)} %q_ref.3) | copy-start | bytes 1671172
  58.2 19.7 %collective-permute-start.17 = (bf16[608,256]{1,0:T(8,128)(2,1)S(1)}, bf16[608,256]{1,0:T(8,128)(2,1)S(1)}, u32[]{:S(2)}, u32[]{:S(2)}) collective-permute-start(bf16[608,256]{1,0:T(8,128)(2,1)S(1)} %far_part.2.refs_12_), channel_id=1, source_target_pairs={{0,16},{2,18},{4,20},{6,22},{8,24},{10,26},{12,28},{14,30},{16,0},... | collective-permute-start | bytes 933896 | tf_op jit(solution)/shard_map/ppermute | solution.py:569
  61.7 20.3 %collective-permute-start.15 = (bf16[544,256]{1,0:T(8,128)(2,1)S(1)}, bf16[544,256]{1,0:T(8,128)(2,1)S(1)}, u32[]{:S(2)}, u32[]{:S(2)}) collective-permute-start(bf16[544,256]{1,0:T(8,128)(2,1)S(1)} %far_part.3.refs_8_), channel_id=1, source_target_pairs={{0,16},{2,18},{4,20},{6,22},{8,24},{10,26},{12,28},{14,30},{16,0},... | collective-permute-start | bytes 835592 | tf_op jit(solution)/shard_map/ppermute | solution.py:569
  78.6 4.2 %copy-start.2 = (bf16[512,2048]{1,0:T(8,128)(2,1)S(1)}, bf16[512,2048]{1,0:T(8,128)(2,1)}, u32[]{:S(2)}) copy-start(bf16[512,2048]{1,0:T(8,128)(2,1)} %refs_2_.7) | copy-start | bytes 6291460
  78.6 4.2 %collective-permute-start.18 = (bf16[576,256]{1,0:T(8,128)(2,1)S(1)}, bf16[576,256]{1,0:T(8,128)(2,1)S(1)}, u32[]{:S(2)}, u32[]{:S(2)}) collective-permute-start(bf16[576,256]{1,0:T(8,128)(2,1)S(1)} %contexts.3.refs_0_), channel_id=1, source_target_pairs={{1,0},{0,1},{3,2},{2,3},{5,4},{4,5},{7,6},{6,7},{9,8},{8,9},{11,10... | collective-permute-start | bytes 884744 | tf_op jit(solution)/shard_map/ppermute | solution.py:577
  82.7 2.4 %collective-permute-start.16 = (bf16[512,256]{1,0:T(8,128)(2,1)S(1)}, bf16[512,256]{1,0:T(8,128)(2,1)S(1)}, u32[]{:S(2)}, u32[]{:S(2)}) collective-permute-start(bf16[512,256]{1,0:T(8,128)(2,1)S(1)} %contexts.2.refs_0_), channel_id=1, source_target_pairs={{1,0},{0,1},{3,2},{2,3},{5,4},{4,5},{7,6},{6,7},{9,8},{8,9},{11,10... | collective-permute-start | bytes 786440 | tf_op jit(solution)/shard_map/ppermute | solution.py:577
where the time goes:
time: 87.9 us; the launch traced here: 87.5 us
  waiting for transfers between devices  34.2 us (39%)
  Pallas kernels  25.3 us (29%)
  starting transfers between devices  24.5 us (28%)
  local copies, waits for them, and re-layouts  3.12 us (4%)
    ppermute x12, starting transfers between devices, exchange(): got.append(lax.ppermute(parts[k], 'seq', [(i, i ^ k) for i in range(n)]))  15.2 us
    ppermute x12, waiting for transfers between devices, exchange(): got.append(lax.ppermute(parts[k], 'seq', [(i, i ^ k) for i in range(n)]))  13.5 us
    ppermute x2, waiting for transfers between devices, on_device(): fars.append(lax.ppermute(earlier, 'seq', partners))  7.86 us
    ppermute x1, waiting for transfers between devices, on_device(): mate_v = lax.ppermute(values, 'seq', mates)  6.76 us
    ppermute x1, waiting for transfers between devices, on_device(): mate_k = lax.ppermute(keys, 'seq', mates)  6.1 us
    pallas_call x2, Pallas kernels, far_part(): pl.pallas_call(functools.partial(far_kernel, n, cap, per, heads, span), o...  6.09 us
    pallas_call x1, Pallas kernels, near_part(): pl.pallas_call(functools.partial(near_kernel, n, cap, per, heads), out_sh...  5.44 us
    pallas_call x2, Pallas kernels, project(): pl.pallas_call(functools.partial(project_kernel, span, len(parts), steps)...  4.48 us
  transfers between devices with their start and end apart: 19, of which 9 were waited for; matrix products, arithmetic and copies ran while one was open for 0% of the time, Pallas kernels for 26%

commit v1 on v0

--- a/solution.py
+++ b/solution.py
@@ -414,14 +414,16 @@
 
 def rand_kernel(n, cap, per, heads, arrive_ref, q_ref, *refs):
     plane = n // 4
-    early, late = refs[:plane], refs[plane : 2 * plane]
-    part_ref, stat_ref, held, keys, vals = refs[2 * plane :]
+    part_ref, stat_ref, held, keys, vals = refs[plane:]
     diagonal = eye()
     stat_ref[...] = jnp.zeros_like(stat_ref)
     me = lax.axis_index("seq")
     size = cap * BLOCK
-    sources = [((x, 2 * size), (y, 0)) for x, y in zip(early, late)]
-    sources += [((y, size), (y, 2 * size)) for y in late]
+    sources = [
+        ((ref, 2 * side * size), (ref, (2 * side + 1) * size))
+        for side in range(2)
+        for ref in refs[:plane]
+    ]
     biases = choose(n, cap, per, (0, per), arrive_ref, me, sources, held, keys, vals)
     for pairs in batches((0, per), heads, 4):
         sets = [
@@ -432,18 +434,18 @@
         store_part(heads, pairs, *parts, part_ref, stat_ref, diagonal)
 
 
-def rand_part(n, cap, per, arrive, q, early, late):
+def rand_part(n, cap, per, arrive, q, got):
     columns = q.shape[1]
     return pl.pallas_call(
         functools.partial(rand_kernel, n, cap, per, columns // DH),
         out_shape=part_shapes(per, columns),
-        in_specs=[spec(SMEM), spec()] + [spec()] * (len(early) + len(late)),
+        in_specs=[spec(SMEM), spec()] + [spec()] * len(got),
         out_specs=(spec(), spec()),
         scratch_shapes=scratches(n, cap, per, columns)[:3],
         compiler_params=params(16),
         cost_estimate=HEAVY,
         name="rand_part",
-    )(arrive, q, *early, *late)
+    )(arrive, q, *got)
 
 
 def context_kernel(
@@ -542,12 +544,12 @@
     partners = [(i, i ^ (n // 2)) for i in range(n)]
     mate_k = lax.ppermute(keys, "seq", mates)
     mate_v = lax.ppermute(values, "seq", mates)
-    later_q, _ = lax.optimization_barrier((queries, mate_k))
-    far_q = lax.ppermute(later_q, "seq", partners)
     spots, arrive = ranks(n, per, cap, rand_group.T, rand_offset.T)
     rows = {(0, 0): keys, (0, 1): values}
-    lists = ((0, True, (0, 1)), (0, False, (0,)))
+    lists = ((0, True, (0, 1)),)
     first = exchange(gather(n, per, cap, lists, spots, rows), n)
+    later_q = lax.optimization_barrier((queries, *first[1:4]))[0]
+    far_q = lax.ppermute(later_q, "seq", partners)
     rows = {(0, 0): keys, (1, 0): mate_k}
     lists = ((1, True, (0,)),)
     second_k = exchange(gather(n, per, cap, lists, spots, rows, [glob_blocks], first[1:4]), n)
@@ -556,7 +558,7 @@
     sent = gather(n, per, cap, lists, spots, rows, [glob_blocks], second_k[1:2])
     second = second_k + exchange(sent, n)
     rows = {(0, 0): keys, (0, 1): values, (1, 0): mate_k, (1, 1): mate_v}
-    lists = ((0, False, (1,)), (1, False, (0, 1)))
+    lists = ((0, False, (0, 1)), (1, False, (0, 1)))
     third = gather(n, per, cap, lists, spots, rows, (), sent[:1])
     middle = (per + 1) // 2
     spans = ((0, middle), (middle, per))
@@ -569,7 +571,7 @@
         fars.append(lax.ppermute(earlier, "seq", partners))
     third = exchange(third, n)
     near, near_stat = near_part(n, cap, per, glob_blocks, queries, keys, values, second, earlier)
-    rand, rand_stat = rand_part(n, cap, per, arrive, queries, first, third)
+    rand, rand_stat = rand_part(n, cap, per, arrive, queries, third)
     out = None
     for span, far in zip(spans, fars):
         context = contexts(span, near, near_stat, rand, rand_stat, far)

time: 87.9 us -> 85.6 us (0.974)
  waiting for transfers between devices: 34.2 us -> 31.8 us
    ppermute x1, waiting for transfers between devices: 6.1 us -> 0.01 us  [on_device(): mate_k = lax.ppermute(keys, 'seq', mates)]
    ppermute x1, waiting for transfers between devices: 0.01 us -> 5.58 us  [on_device(): far_q = lax.ppermute(later_q, 'seq', partners)]
    ppermute x12, waiting for transfers between devices: 13.5 us -> 17.7 us  [exchange(): got.append(lax.ppermute(parts[k], 'seq', [(i, i ^ k) for i in range(n)]))]
    ppermute x2, waiting for transfers between devices: 7.86 us -> 3.72 us  [on_device(): fars.append(lax.ppermute(earlier, 'seq', partners))]
    ppermute x1, waiting for transfers between devices: 6.76 us -> 4.76 us  [on_device(): mate_v = lax.ppermute(values, 'seq', mates)]
  transfers between devices with their start and end apart: 19 -> 19, of which waited for: 9 -> 7; matrix products, arithmetic and copies ran while one was open for 0% -> 0% of each run, Pallas kernels for 26% -> 27%
where the time goes in v1:
time: 85.6 us; the launch traced here: 85.2 us
  waiting for transfers between devices  31.8 us (37%)
  Pallas kernels  25.4 us (30%)
  starting transfers between devices  24.6 us (29%)
  local copies, waits for them, and re-layouts  3.12 us (4%)
    ppermute x12, waiting for transfers between devices, exchange(): got.append(lax.ppermute(parts[k], 'seq', [(i, i ^ k) for i in range(n)]))  17.7 us
    ppermute x12, starting transfers between devices, exchange(): got.append(lax.ppermute(parts[k], 'seq', [(i, i ^ k) for i in range(n)]))  15.8 us
    pallas_call x2, Pallas kernels, far_part(): pl.pallas_call(functools.partial(far_kernel, n, cap, per, heads, span), o...  6.08 us
    ppermute x1, waiting for transfers between devices, on_device(): far_q = lax.ppermute(later_q, 'seq', partners)  5.58 us
    pallas_call x1, Pallas kernels, near_part(): pl.pallas_call(functools.partial(near_kernel, n, cap, per, heads), out_sh...  5.44 us
    ppermute x1, waiting for transfers between devices, on_device(): mate_v = lax.ppermute(values, 'seq', mates)  4.76 us
    pallas_call x2, Pallas kernels, project(): pl.pallas_call(functools.partial(project_kernel, span, len(parts), steps)...  4.48 us
    pallas_call x4, Pallas kernels, gather(): pl.pallas_call(functools.partial(gather_kernel, n, per, cap, lists, bool(...  4.28 us
  transfers between devices with their start and end apart: 19, of which 7 were waited for; matrix products, arithmetic and copies ran while one was open for 0% of the time, Pallas kernels for 27%

profile of v1, /device:TPU:0, one launch (start us, length us, event | category | flops | bytes accessed | tf_op | source)
XLA Modules:
  0.0 85.2 jit_solution(9638309095792257623)
XLA Ops:
  0.0 3.0 %collective-permute-start = (bf16[1088,256]{1,0:T(8,128)(2,1)}, bf16[1088,256]{1,0:T(8,128)(2,1)S(1)}, u32[]{:S(2)}, u32[]{:S(2)}) collective-permute-start(bf16[1088,256]{1,0:T(8,128)(2,1)} %k_ref.1), channel_id=1, source_target_pairs={{0,8},{2,10},{4,12},{6,14},{8,0},{10,2},{12,4},{14,6},{16,24},{18,... | collective-permute-start | bytes 1671176 | tf_op jit(solution)/shard_map/ppermute | solution.py:545
  3.0 0.0 copy-start.4
  3.0 0.7 copy-done.4
  3.7 0.0 copy-start.5
  3.7 0.7 copy-done.5
  4.4 0.4 ranks.1
  4.8 1.1 %copy-done = bf16[1088,256]{1,0:T(8,128)(2,1)S(1)} copy-done((bf16[1088,256]{1,0:T(8,128)(2,1)S(1)}, bf16[1088,256]{1,0:T(8,128)(2,1)}, u32[]{:S(2)}) %copy-start) | copy-done | bytes 557080
  5.8 1.2 %gather_blocks.4 = (bf16[512,256]{1,0:T(8,128)(2,1)S(1)}, bf16[512,256]{1,0:T(8,128)(2,1)S(1)}, bf16[512,256]{1,0:T(8,128)(2,1)S(1)}, bf16[512,256]{1,0:T(8,128)(2,1)S(1)}) custom-call(s32[8,128]{1,0:T(8,128)S(1)} %get-tuple-element.28.spot_ref, bf16[1088,256]{1,0:T(8,128)(2,1)S(1)} %copy-done, bf16[1088,256]{1,0:T(8,128)(2,1)} %v_ref.1), custom_call_target="tpu_custom_call" | custom-call | flops 1 | bytes 1 | tf_op jit(solution)/shard_map/gather_blocks/pallas_call | solution.py:137
  7.0 1.6 %collective-permute-start.1 = (bf16[512,256]{1,0:T(8,128)(2,1)S(1)}, bf16[512,256]{1,0:T(8,128)(2,1)S(1)}, u32[]{:S(2)}, u32[]{:S(2)}) collective-permute-start(bf16[512,256]{1,0:T(8,128)(2,1)S(1)} %get-tuple-element.29), channel_id=1, source_target_pairs={{0,2},{2,0},{4,6},{6,4},{8,10},{10,8},{12,14},{14,12},{16,18},{18,... | collective-permute-start | bytes 786440 | tf_op jit(solution)/shard_map/ppermute | solution.py:154
  8.6 1.5 %collective-permute-start.2 = (bf16[512,256]{1,0:T(8,128)(2,1)S(1)}, bf16[512,256]{1,0:T(8,128)(2,1)S(1)}, u32[]{:S(2)}, u32[]{:S(2)}) collective-permute-start(bf16[512,256]{1,0:T(8,128)(2,1)S(1)} %get-tuple-element.30), channel_id=1, source_target_pairs={{0,4},{2,6},{4,0},{6,2},{8,12},{10,14},{12,8},{14,10},{16,20},{18,... | collective-permute-start | bytes 786440 | tf_op jit(solution)/shard_map/ppermute | solution.py:154
  10.1 0.5 collective-permute-start.3
  10.6 0.0 collective-permute-start.7
  10.6 5.7 %collective-permute-done.1.refs_3_.refs_1_ = bf16[512,256]{1,0:T(8,128)(2,1)S(1)} collective-permute-done((bf16[512,256]{1,0:T(8,128)(2,1)S(1)}, bf16[512,256]{1,0:T(8,128)(2,1)S(1)}, u32[]{:S(2)}, u32[]{:S(2)}) %collective-permute-start.1) | collective-permute-done | bytes 262176 | tf_op jit(solution)/shard_map/ppermute | solution.py:154
  16.3 5.4 %collective-permute-done.2.refs_4_.refs_2_ = bf16[512,256]{1,0:T(8,128)(2,1)S(1)} collective-permute-done((bf16[512,256]{1,0:T(8,128)(2,1)S(1)}, bf16[512,256]{1,0:T(8,128)(2,1)S(1)}, u32[]{:S(2)}, u32[]{:S(2)}) %collective-permute-start.2) | collective-permute-done | bytes 262176 | tf_op jit(solution)/shard_map/ppermute | solution.py:154
  21.7 0.0 collective-permute-done.3.refs_5_.refs_3_
  21.7 2.6 %collective-permute-start.11 = (bf16[1088,256]{1,0:T(8,128)(2,1)}, bf16[1088,256]{1,0:T(8,128)(2,1)S(1)}, u32[]{:S(2)}, u32[]{:S(2)}) collective-permute-start(bf16[1088,256]{1,0:T(8,128)(2,1)} %q_ref.3), channel_id=1, source_target_pairs={{0,16},{2,18},{4,20},{6,22},{8,24},{10,26},{12,28},{14,30},{16,0},... | collective-permute-start | bytes 1671176 | tf_op jit(solution)/shard_map/ppermute | solution.py:552
  24.3 0.0 collective-permute-done.refs_1_.refs_2_
  24.3 0.7 copy-done.6
  25.0 0.7 gather_blocks.5
  25.7 0.0 copy-start.7
  25.7 1.3 %collective-permute-start.4 = (bf16[448,256]{1,0:T(8,128)(2,1)S(1)}, bf16[448,256]{1,0:T(8,128)(2,1)S(1)}, u32[]{:S(2)}, u32[]{:S(2)}) collective-permute-start(bf16[448,256]{1,0:T(8,128)(2,1)S(1)} %get-tuple-element.33), channel_id=1, source_target_pairs={{0,2},{2,0},{4,6},{6,4},{8,10},{10,8},{12,14},{14,12},{16,18},{18,... | collective-permute-start | bytes 688136 | tf_op jit(solution)/shard_map/ppermute | solution.py:154
  27.0 0.8 collective-permute-start.5
  27.8 1.4 %collective-permute-start.6 = (bf16[448,256]{1,0:T(8,128)(2,1)S(1)}, bf16[448,256]{1,0:T(8,128)(2,1)S(1)}, u32[]{:S(2)}, u32[]{:S(2)}) collective-permute-start(bf16[448,256]{1,0:T(8,128)(2,1)S(1)} %get-tuple-element.35), channel_id=1, source_target_pairs={{0,6},{2,4},{4,2},{6,0},{8,14},{10,12},{12,10},{14,8},{16,22},{18,... | collective-permute-start | bytes 688136 | tf_op jit(solution)/shard_map/ppermute | solution.py:154
  29.2 4.8 %collective-permute-done.7.refs_1_.refs_3_ = bf16[1088,256]{1,0:T(8,128)(2,1)S(1)} collective-permute-done((bf16[1088,256]{1,0:T(8,128)(2,1)}, bf16[1088,256]{1,0:T(8,128)(2,1)S(1)}, u32[]{:S(2)}, u32[]{:S(2)}) %collective-permute-start.7) | collective-permute-done | bytes 557088 | tf_op jit(solution)/shard_map/ppermute | solution.py:546
  34.0 0.0 collective-permute-done.4.refs_3_.refs_5_.refs_1_
  34.0 1.2 %gather_blocks.6 = (bf16[448,256]{1,0:T(8,128)(2,1)S(1)}, bf16[448,256]{1,0:T(8,128)(2,1)S(1)}, bf16[448,256]{1,0:T(8,128)(2,1)S(1)}, bf16[448,256]{1,0:T(8,128)(2,1)S(1)}) custom-call(s32[8,128]{1,0:T(8,128)S(1)} %get-tuple-element.28.spot_ref, bf16[1088,256]{1,0:T(8,128)(2,1)} %v_ref.1, bf16[1088,256]{1,0:T(8,128)(2,1)S(1)} %collective-permute-done.7.refs_1_.refs_3_, ...), custom_call_target="tpu_custom_call" | custom-call | flops 1 | bytes 1 | tf_op jit(solution)/shard_map/gather_blocks/pallas_call | solution.py:137
  35.2 1.8 %collective-permute-start.8 = (bf16[448,256]{1,0:T(8,128)(2,1)S(1)}, bf16[448,256]{1,0:T(8,128)(2,1)S(1)}, u32[]{:S(2)}, u32[]{:S(2)}) collective-permute-start(bf16[448,256]{1,0:T(8,128)(2,1)S(1)} %get-tuple-element.37), channel_id=1, source_target_pairs={{0,2},{2,0},{4,6},{6,4},{8,10},{10,8},{12,14},{14,12},{16,18},{18,... | collective-permute-start | bytes 688136 | tf_op jit(solution)/shard_map/ppermute | solution.py:154
  36.9 2.5 %collective-permute-start.9 = (bf16[448,256]{1,0:T(8,128)(2,1)S(1)}, bf16[448,256]{1,0:T(8,128)(2,1)S(1)}, u32[]{:S(2)}, u32[]{:S(2)}) collective-permute-start(bf16[448,256]{1,0:T(8,128)(2,1)S(1)} %get-tuple-element.38), channel_id=1, source_target_pairs={{0,4},{2,6},{4,0},{6,2},{8,12},{10,14},{12,8},{14,10},{16,20},{18,... | collective-permute-start | bytes 688136 | tf_op jit(solution)/shard_map/ppermute | solution.py:154
  39.4 0.0 collective-permute-done.5.refs_6_.refs_2_
  39.4 0.0 collective-permute-start.10
  39.4 0.0 copy-done.1
  39.4 1.2 %gather_blocks.7 = (bf16[1024,256]{1,0:T(8,128)(2,1)S(1)}, bf16[1024,256]{1,0:T(8,128)(2,1)S(1)}, bf16[1024,256]{1,0:T(8,128)(2,1)S(1)}, bf16[1024,256]{1,0:T(8,128)(2,1)S(1)}) custom-call(s32[8,128]{1,0:T(8,128)S(1)} %get-tuple-element.28.spot_ref, bf16[1088,256]{1,0:T(8,128)(2,1)S(1)} %copy-done.1, bf16[1088,256]{1,0:T(8,128)(2,1)} %v_ref.1, ...), custom_call_target="tpu_custom_call" | custom-call | flops 1 | bytes 1 | tf_op jit(solution)/shard_map/gather_blocks/pallas_call | solution.py:137
  40.7 0.0 collective-permute-done.6.refs_7_.refs_3_
  40.7 1.5 %collective-permute-start.12 = (bf16[1024,256]{1,0:T(8,128)(2,1)S(1)}, bf16[1024,256]{1,0:T(8,128)(2,1)S(1)}, u32[]{:S(2)}, u32[]{:S(2)}) collective-permute-start(bf16[1024,256]{1,0:T(8,128)(2,1)S(1)} %get-tuple-element.46), channel_id=1, source_target_pairs={{0,2},{2,0},{4,6},{6,4},{8,10},{10,8},{12,14},{14,12},{16,18},{18,... | collective-permute-start | bytes 1572872 | tf_op jit(solution)/shard_map/ppermute | solution.py:154
  42.2 5.6 %collective-permute-done.11.q_ref = bf16[1088,256]{1,0:T(8,128)(2,1)S(1)} collective-permute-done((bf16[1088,256]{1,0:T(8,128)(2,1)}, bf16[1088,256]{1,0:T(8,128)(2,1)S(1)}, u32[]{:S(2)}, u32[]{:S(2)}) %collective-permute-start.11) | collective-permute-done | bytes 557088 | tf_op jit(solution)/shard_map/ppermute | solution.py:552
  47.8 0.5 collective-permute-start.13
  48.3 0.0 collective-permute-done.8.refs_9_.refs_5_
  48.3 2.4 %collective-permute-start.14 = (bf16[1024,256]{1,0:T(8,128)(2,1)S(1)}, bf16[1024,256]{1,0:T(8,128)(2,1)S(1)}, u32[]{:S(2)}, u32[]{:S(2)}) collective-permute-start(bf16[1024,256]{1,0:T(8,128)(2,1)S(1)} %get-tuple-element.48), channel_id=1, source_target_pairs={{0,6},{2,4},{4,2},{6,0},{8,14},{10,12},{12,10},{14,8},{16,22},{18,... | collective-permute-start | bytes 1572872 | tf_op jit(solution)/shard_map/ppermute | solution.py:154
  50.7 0.0 collective-permute-done.9.refs_10_.refs_6_
  50.7 0.1 collective-permute-done.10.refs_11_.refs_7_
  50.8 0.0 copy-done.7
  50.8 3.2 %far_part.2.refs_12_ = bf16[608,256]{1,0:T(8,128)(2,1)S(1)} custom-call(s32[8,384]{1,0:T(8,128)S(1)} %get-tuple-element.40.arrive_ref, s32[2]{0:T(128)S(1)} %copy-done.7, bf16[1088,256]{1,0:T(8,128)(2,1)S(1)} %collective-permute-done.11.q_ref, bf16[512,256]{1,0:T(8,128)(2,1)S(1)} %get-tuple-element.42.refs_0_, ...), custom_call_target="tpu_custom_call" | custom-call | flops 4000000000 | bytes 1 | tf_op jit(solution)/shard_map/far_part/pallas_call | solution.py:335
  54.0 0.0 copy-start.3
  54.0 0.7 collective-permute-start.17
  54.7 2.9 %far_part.3.refs_8_ = bf16[544,256]{1,0:T(8,128)(2,1)S(1)} custom-call(s32[8,384]{1,0:T(8,128)S(1)} %get-tuple-element.40.arrive_ref, s32[2]{0:T(128)S(1)} %copy-done.7, bf16[1088,256]{1,0:T(8,128)(2,1)S(1)} %collective-permute-done.11.q_ref, bf16[512,256]{1,0:T(8,128)(2,1)S(1)} %get-tuple-element.42.refs_0_, ...), custom_call_target="tpu_custom_call" | custom-call | flops 4000000000 | bytes 1 | tf_op jit(solution)/shard_map/far_part/pallas_call | solution.py:335
  57.7 2.3 %collective-permute-start.15 = (bf16[544,256]{1,0:T(8,128)(2,1)S(1)}, bf16[544,256]{1,0:T(8,128)(2,1)S(1)}, u32[]{:S(2)}, u32[]{:S(2)}) collective-permute-start(bf16[544,256]{1,0:T(8,128)(2,1)S(1)} %far_part.3.refs_8_), channel_id=1, source_target_pairs={{0,16},{2,18},{4,20},{6,22},{8,24},{10,26},{12,28},{14,30},{16,0},... | collective-permute-start | bytes 835592 | tf_op jit(solution)/shard_map/ppermute | solution.py:571
  60.0 0.0 copy-done.3
  60.0 5.4 %near_part.1 = (f32[1088,256]{1,0:T(8,128)S(1)}, f32[24,256]{1,0:T(8,128)S(1)}) custom-call(s32[2]{0:T(128)S(1)} %copy-done.7, bf16[1088,256]{1,0:T(8,128)(2,1)S(1)} %copy-done.3, bf16[1088,256]{1,0:T(8,128)(2,1)S(1)} %copy-done.1, bf16[1088,256]{1,0:T(8,128)(2,1)} %v_ref.1, bf16[448,256]{1,0:T(8,128)(2,1)S(1)} %get-tuple-element.32.refs_4_.refs_0_, ...), custom_call_target="tpu_custom_call" | custom-call | flops 1 | bytes 1 | tf_op jit(solution)/shard_map/near_part/pallas_call | solution.py:402
  65.4 0.0 collective-permute-done.12.refs_1_
  65.4 6.4 %collective-permute-done.13.refs_2_ = bf16[1024,256]{1,0:T(8,128)(2,1)S(1)} collective-permute-done((bf16[1024,256]{1,0:T(8,128)(2,1)S(1)}, bf16[1024,256]{1,0:T(8,128)(2,1)S(1)}, u32[]{:S(2)}, u32[]{:S(2)}) %collective-permute-start.13) | collective-permute-done | bytes 524320 | tf_op jit(solution)/shard_map/ppermute | solution.py:154
  71.8 0.0 collective-permute-done.14.refs_3_
  71.8 3.4 %rand_part.1 = (f32[1088,256]{1,0:T(8,128)S(1)}, f32[24,256]{1,0:T(8,128)S(1)}) custom-call(s32[8,384]{1,0:T(8,128)S(1)} %get-tuple-element.40.arrive_ref, bf16[1088,256]{1,0:T(8,128)(2,1)S(1)} %copy-done.3, bf16[1024,256]{1,0:T(8,128)(2,1)S(1)} %get-tuple-element.43.refs_12_.refs_0_, bf16[1024,256]{1,0:T(8,128)(2,1)S(1)} %collective-permute-done.12.refs_1_, ...), custom_call_target="tpu_custom_call" | custom-call | flops 4000000000 | bytes 1 | tf_op jit(solution)/shard_map/rand_part/pallas_call | solution.py:439
  75.2 0.0 collective-permute-done.17.far_ref
  75.2 0.7 contexts.3.refs_0_
  76.0 0.0 copy-start.2
  76.0 0.1 collective-permute-start.18
  76.0 3.7 %collective-permute-done.15.far_ref = bf16[544,256]{1,0:T(8,128)(2,1)S(1)} collective-permute-done((bf16[544,256]{1,0:T(8,128)(2,1)S(1)}, bf16[544,256]{1,0:T(8,128)(2,1)S(1)}, u32[]{:S(2)}, u32[]{:S(2)}) %collective-permute-start.15) | collective-permute-done | bytes 278560 | tf_op jit(solution)/shard_map/ppermute | solution.py:571
  79.8 0.7 contexts.2.refs_0_
  80.4 0.1 collective-permute-start.16
  80.5 0.0 collective-permute-done.18.refs_1_
  80.5 0.0 copy-done.2
  80.5 2.3 %project.2.refs_3_ = bf16[1088,2048]{1,0:T(8,128)(2,1)} custom-call(bf16[576,256]{1,0:T(8,128)(2,1)S(1)} %contexts.3.refs_0_, bf16[576,256]{1,0:T(8,128)(2,1)S(1)} %collective-permute-done.18.refs_1_, bf16[512,2048]{1,0:T(8,128)(2,1)S(1)} %copy-done.2), custom_call_target="tpu_custom_call" | custom-call | flops 1 | bytes 1 | tf_op jit(solution)/shard_map/project/pallas_call | solution.py:519
  82.8 0.0 collective-permute-done.16.refs_1_
  82.9 2.2 %project.3 = bf16[1088,2048]{1,0:T(8,128)(2,1)} custom-call(bf16[512,256]{1,0:T(8,128)(2,1)S(1)} %contexts.2.refs_0_, bf16[512,256]{1,0:T(8,128)(2,1)S(1)} %collective-permute-done.16.refs_1_, bf16[512,2048]{1,0:T(8,128)(2,1)S(1)} %copy-done.2, bf16[1088,2048]{1,0:T(8,128)(2,1)} %project.2.refs_3_), custom_call_target="tpu_custom_call", output_to_operand_aliasing={{}: (3, {})} | custom-call | flops 1 | bytes 1 | tf_op jit(solution)/shard_map/project/pallas_call | solution.py:519
  (3 shorter events, 0.0 us)
Async XLA Ops:
  0.0 24.3 %collective-permute-start = (bf16[1088,256]{1,0:T(8,128)(2,1)}, bf16[1088,256]{1,0:T(8,128)(2,1)S(1)}, u32[]{:S(2)}, u32[]{:S(2)}) collective-permute-start(bf16[1088,256]{1,0:T(8,128)(2,1)} %k_ref.1), channel_id=1, source_target_pairs={{0,8},{2,10},{4,12},{6,14},{8,0},{10,2},{12,4},{14,6},{16,24},{18,... | collective-permute-start | bytes 1671176 | tf_op jit(solution)/shard_map/ppermute | solution.py:545
  3.0 0.7 copy-start.4
  3.7 0.7 copy-start.5
  4.8 1.1 %copy-start = (bf16[1088,256]{1,0:T(8,128)(2,1)S(1)}, bf16[1088,256]{1,0:T(8,128)(2,1)}, u32[]{:S(2)}) copy-start(bf16[1088,256]{1,0:T(8,128)(2,1)} %k_ref.1) | copy-start | bytes 1671172
  5.8 33.6 %copy-start.1 = (bf16[1088,256]{1,0:T(8,128)(2,1)S(1)}, bf16[1088,256]{1,0:T(8,128)(2,1)}, u32[]{:S(2)}) copy-start(bf16[1088,256]{1,0:T(8,128)(2,1)} %k_ref.1) | copy-start | bytes 1671172
  7.0 9.3 %collective-permute-start.1 = (bf16[512,256]{1,0:T(8,128)(2,1)S(1)}, bf16[512,256]{1,0:T(8,128)(2,1)S(1)}, u32[]{:S(2)}, u32[]{:S(2)}) collective-permute-start(bf16[512,256]{1,0:T(8,128)(2,1)S(1)} %get-tuple-element.29), channel_id=1, source_target_pairs={{0,2},{2,0},{4,6},{6,4},{8,10},{10,8},{12,14},{14,12},{16,18},{18,... | collective-permute-start | bytes 786440 | tf_op jit(solution)/shard_map/ppermute | solution.py:154
  8.6 13.1 %collective-permute-start.2 = (bf16[512,256]{1,0:T(8,128)(2,1)S(1)}, bf16[512,256]{1,0:T(8,128)(2,1)S(1)}, u32[]{:S(2)}, u32[]{:S(2)}) collective-permute-start(bf16[512,256]{1,0:T(8,128)(2,1)S(1)} %get-tuple-element.30), channel_id=1, source_target_pairs={{0,4},{2,6},{4,0},{6,2},{8,12},{10,14},{12,8},{14,10},{16,20},{18,... | collective-permute-start | bytes 786440 | tf_op jit(solution)/shard_map/ppermute | solution.py:154
  10.1 11.6 %collective-permute-start.3 = (bf16[512,256]{1,0:T(8,128)(2,1)S(1)}, bf16[512,256]{1,0:T(8,128)(2,1)S(1)}, u32[]{:S(2)}, u32[]{:S(2)}) collective-permute-start(bf16[512,256]{1,0:T(8,128)(2,1)S(1)} %get-tuple-element.31), channel_id=1, source_target_pairs={{0,6},{2,4},{4,2},{6,0},{8,14},{10,12},{12,10},{14,8},{16,22},{18,... | collective-permute-start | bytes 786440 | tf_op jit(solution)/shard_map/ppermute | solution.py:154
  10.6 23.4 %collective-permute-start.7 = (bf16[1088,256]{1,0:T(8,128)(2,1)}, bf16[1088,256]{1,0:T(8,128)(2,1)S(1)}, u32[]{:S(2)}, u32[]{:S(2)}) collective-permute-start(bf16[1088,256]{1,0:T(8,128)(2,1)} %v_ref.1), channel_id=1, source_target_pairs={{0,8},{2,10},{4,12},{6,14},{8,0},{10,2},{12,4},{14,6},{16,24},{18,... | collective-permute-start | bytes 1671176 | tf_op jit(solution)/shard_map/ppermute | solution.py:546
  21.7 26.1 %collective-permute-start.11 = (bf16[1088,256]{1,0:T(8,128)(2,1)}, bf16[1088,256]{1,0:T(8,128)(2,1)S(1)}, u32[]{:S(2)}, u32[]{:S(2)}) collective-permute-start(bf16[1088,256]{1,0:T(8,128)(2,1)} %q_ref.3), channel_id=1, source_target_pairs={{0,16},{2,18},{4,20},{6,22},{8,24},{10,26},{12,28},{14,30},{16,0},... | collective-permute-start | bytes 1671176 | tf_op jit(solution)/shard_map/ppermute | solution.py:552
  24.3 0.7 copy-start.6
  25.7 25.2 %copy-start.7 = (s32[2]{0:T(128)S(1)}, s32[2]{0:T(128)}, u32[]{:S(2)}) copy-start(s32[2]{0:T(128)} %place_ref.5) | copy-start | bytes 28
  25.7 8.3 %collective-permute-start.4 = (bf16[448,256]{1,0:T(8,128)(2,1)S(1)}, bf16[448,256]{1,0:T(8,128)(2,1)S(1)}, u32[]{:S(2)}, u32[]{:S(2)}) collective-permute-start(bf16[448,256]{1,0:T(8,128)(2,1)S(1)} %get-tuple-element.33), channel_id=1, source_target_pairs={{0,2},{2,0},{4,6},{6,4},{8,10},{10,8},{12,14},{14,12},{16,18},{18,... | collective-permute-start | bytes 688136 | tf_op jit(solution)/shard_map/ppermute | solution.py:154
  27.0 12.5 %collective-permute-start.5 = (bf16[448,256]{1,0:T(8,128)(2,1)S(1)}, bf16[448,256]{1,0:T(8,128)(2,1)S(1)}, u32[]{:S(2)}, u32[]{:S(2)}) collective-permute-start(bf16[448,256]{1,0:T(8,128)(2,1)S(1)} %get-tuple-element.34), channel_id=1, source_target_pairs={{0,4},{2,6},{4,0},{6,2},{8,12},{10,14},{12,8},{14,10},{16,20},{18,... | collective-permute-start | bytes 688136 | tf_op jit(solution)/shard_map/ppermute | solution.py:154
  27.8 12.9 %collective-permute-start.6 = (bf16[448,256]{1,0:T(8,128)(2,1)S(1)}, bf16[448,256]{1,0:T(8,128)(2,1)S(1)}, u32[]{:S(2)}, u32[]{:S(2)}) collective-permute-start(bf16[448,256]{1,0:T(8,128)(2,1)S(1)} %get-tuple-element.35), channel_id=1, source_target_pairs={{0,6},{2,4},{4,2},{6,0},{8,14},{10,12},{12,10},{14,8},{16,22},{18,... | collective-permute-start | bytes 688136 | tf_op jit(solution)/shard_map/ppermute | solution.py:154
  35.2 13.1 %collective-permute-start.8 = (bf16[448,256]{1,0:T(8,128)(2,1)S(1)}, bf16[448,256]{1,0:T(8,128)(2,1)S(1)}, u32[]{:S(2)}, u32[]{:S(2)}) collective-permute-start(bf16[448,256]{1,0:T(8,128)(2,1)S(1)} %get-tuple-element.37), channel_id=1, source_target_pairs={{0,2},{2,0},{4,6},{6,4},{8,10},{10,8},{12,14},{14,12},{16,18},{18,... | collective-permute-start | bytes 688136 | tf_op jit(solution)/shard_map/ppermute | solution.py:154
  36.9 13.7 %collective-permute-start.9 = (bf16[448,256]{1,0:T(8,128)(2,1)S(1)}, bf16[448,256]{1,0:T(8,128)(2,1)S(1)}, u32[]{:S(2)}, u32[]{:S(2)}) collective-permute-start(bf16[448,256]{1,0:T(8,128)(2,1)S(1)} %get-tuple-element.38), channel_id=1, source_target_pairs={{0,4},{2,6},{4,0},{6,2},{8,12},{10,14},{12,8},{14,10},{16,20},{18,... | collective-permute-start | bytes 688136 | tf_op jit(solution)/shard_map/ppermute | solution.py:154
  39.4 11.4 %collective-permute-start.10 = (bf16[448,256]{1,0:T(8,128)(2,1)S(1)}, bf16[448,256]{1,0:T(8,128)(2,1)S(1)}, u32[]{:S(2)}, u32[]{:S(2)}) collective-permute-start(bf16[448,256]{1,0:T(8,128)(2,1)S(1)} %get-tuple-element.39), channel_id=1, source_target_pairs={{0,6},{2,4},{4,2},{6,0},{8,14},{10,12},{12,10},{14,8},{16,22},{18,... | collective-permute-start | bytes 688136 | tf_op jit(solution)/shard_map/ppermute | solution.py:154
  40.7 24.8 %collective-permute-start.12 = (bf16[1024,256]{1,0:T(8,128)(2,1)S(1)}, bf16[1024,256]{1,0:T(8,128)(2,1)S(1)}, u32[]{:S(2)}, u32[]{:S(2)}) collective-permute-start(bf16[1024,256]{1,0:T(8,128)(2,1)S(1)} %get-tuple-element.46), channel_id=1, source_target_pairs={{0,2},{2,0},{4,6},{6,4},{8,10},{10,8},{12,14},{14,12},{16,18},{18,... | collective-permute-start | bytes 1572872 | tf_op jit(solution)/shard_map/ppermute | solution.py:154
  47.8 24.1 %collective-permute-start.13 = (bf16[1024,256]{1,0:T(8,128)(2,1)S(1)}, bf16[1024,256]{1,0:T(8,128)(2,1)S(1)}, u32[]{:S(2)}, u32[]{:S(2)}) collective-permute-start(bf16[1024,256]{1,0:T(8,128)(2,1)S(1)} %get-tuple-element.47), channel_id=1, source_target_pairs={{0,4},{2,6},{4,0},{6,2},{8,12},{10,14},{12,8},{14,10},{16,20},{18,... | collective-permute-start | bytes 1572872 | tf_op jit(solution)/shard_map/ppermute | solution.py:154
  48.3 23.6 %collective-permute-start.14 = (bf16[1024,256]{1,0:T(8,128)(2,1)S(1)}, bf16[1024,256]{1,0:T(8,128)(2,1)S(1)}, u32[]{:S(2)}, u32[]{:S(2)}) collective-permute-start(bf16[1024,256]{1,0:T(8,128)(2,1)S(1)} %get-tuple-element.48), channel_id=1, source_target_pairs={{0,6},{2,4},{4,2},{6,0},{8,14},{10,12},{12,10},{14,8},{16,22},{18,... | collective-permute-start | bytes 1572872 | tf_op jit(solution)/shard_map/ppermute | solution.py:154
  54.0 6.0 %copy-start.3 = (bf16[1088,256]{1,0:T(8,128)(2,1)S(1)}, bf16[1088,256]{1,0:T(8,128)(2,1)}, u32[]{:S(2)}) copy-start(bf16[1088,256]{1,0:T(8,128)(2,1)} %q_ref.3) | copy-start | bytes 1671172
  54.0 21.2 %collective-permute-start.17 = (bf16[608,256]{1,0:T(8,128)(2,1)S(1)}, bf16[608,256]{1,0:T(8,128)(2,1)S(1)}, u32[]{:S(2)}, u32[]{:S(2)}) collective-permute-start(bf16[608,256]{1,0:T(8,128)(2,1)S(1)} %far_part.2.refs_12_), channel_id=1, source_target_pairs={{0,16},{2,18},{4,20},{6,22},{8,24},{10,26},{12,28},{14,30},{16,0},... | collective-permute-start | bytes 933896 | tf_op jit(solution)/shard_map/ppermute | solution.py:571
  57.7 22.1 %collective-permute-start.15 = (bf16[544,256]{1,0:T(8,128)(2,1)S(1)}, bf16[544,256]{1,0:T(8,128)(2,1)S(1)}, u32[]{:S(2)}, u32[]{:S(2)}) collective-permute-start(bf16[544,256]{1,0:T(8,128)(2,1)S(1)} %far_part.3.refs_8_), channel_id=1, source_target_pairs={{0,16},{2,18},{4,20},{6,22},{8,24},{10,26},{12,28},{14,30},{16,0},... | collective-permute-start | bytes 835592 | tf_op jit(solution)/shard_map/ppermute | solution.py:571
  76.0 4.6 %copy-start.2 = (bf16[512,2048]{1,0:T(8,128)(2,1)S(1)}, bf16[512,2048]{1,0:T(8,128)(2,1)}, u32[]{:S(2)}) copy-start(bf16[512,2048]{1,0:T(8,128)(2,1)} %refs_2_.7) | copy-start | bytes 6291460
  76.0 4.5 %collective-permute-start.18 = (bf16[576,256]{1,0:T(8,128)(2,1)S(1)}, bf16[576,256]{1,0:T(8,128)(2,1)S(1)}, u32[]{:S(2)}, u32[]{:S(2)}) collective-permute-start(bf16[576,256]{1,0:T(8,128)(2,1)S(1)} %contexts.3.refs_0_), channel_id=1, source_target_pairs={{1,0},{0,1},{3,2},{2,3},{5,4},{4,5},{7,6},{6,7},{9,8},{8,9},{11,10... | collective-permute-start | bytes 884744 | tf_op jit(solution)/shard_map/ppermute | solution.py:579
  80.4 2.4 %collective-permute-start.16 = (bf16[512,256]{1,0:T(8,128)(2,1)S(1)}, bf16[512,256]{1,0:T(8,128)(2,1)S(1)}, u32[]{:S(2)}, u32[]{:S(2)}) collective-permute-start(bf16[512,256]{1,0:T(8,128)(2,1)S(1)} %contexts.2.refs_0_), channel_id=1, source_target_pairs={{1,0},{0,1},{3,2},{2,3},{5,4},{4,5},{7,6},{6,7},{9,8},{8,9},{11,10... | collective-permute-start | bytes 786440 | tf_op jit(solution)/shard_map/ppermute | solution.py:579

commit v2 on v1

--- a/solution.py
+++ b/solution.py
@@ -568,8 +568,10 @@
         earlier = far_part(
             n, cap, per, span, arrive, glob_blocks, far_q, first + second, earlier
         )
-        fars.append(lax.ppermute(earlier, "seq", partners))
-    third = exchange(third, n)
+        fars.append(earlier)
+    last, _ = lax.optimization_barrier((third[-1], fars[1]))
+    third = exchange([*third[:-1], last], n)
+    fars = [lax.ppermute(far, "seq", partners) for far in fars]
     near, near_stat = near_part(n, cap, per, glob_blocks, queries, keys, values, second, earlier)
     rand, rand_stat = rand_part(n, cap, per, arrive, queries, third)
     out = None

time: 85.6 us -> 90.1 us (1.053)
  waiting for transfers between devices: 31.8 us -> 37.8 us
  starting transfers between devices: 24.6 us -> 23.1 us
    ppermute x2, waiting for transfers between devices: 3.72 us -> 7.47 us  [on_device(): fars = [lax.ppermute(far, 'seq', partners) for far in fars]]
    ppermute x12, waiting for transfers between devices: 17.7 us -> 19.7 us  [exchange(): got.append(lax.ppermute(parts[k], 'seq', [(i, i ^ k) for i in range(n)]))]
    ppermute x12, starting transfers between devices: 15.8 us -> 13.9 us  [exchange(): got.append(lax.ppermute(parts[k], 'seq', [(i, i ^ k) for i in range(n)]))]
  transfers between devices with their start and end apart: 19 -> 19, of which waited for: 7 -> 9; matrix products, arithmetic and copies ran while one was open for 0% -> 0% of each run, Pallas kernels for 27% -> 26%
where the time goes in v2:
time: 90.1 us; the launch traced here: 89.7 us
  waiting for transfers between devices  37.8 us (42%)
  Pallas kernels  25.4 us (28%)
  starting transfers between devices  23.1 us (26%)
  local copies, waits for them, and re-layouts  3.12 us (3%)
    ppermute x12, waiting for transfers between devices, exchange(): got.append(lax.ppermute(parts[k], 'seq', [(i, i ^ k) for i in range(n)]))  19.7 us
    ppermute x12, starting transfers between devices, exchange(): got.append(lax.ppermute(parts[k], 'seq', [(i, i ^ k) for i in range(n)]))  13.9 us
    ppermute x2, waiting for transfers between devices, on_device(): fars = [lax.ppermute(far, 'seq', partners) for far in fars]  7.47 us
    pallas_call x2, Pallas kernels, far_part(): pl.pallas_call(functools.partial(far_kernel, n, cap, per, heads, span), o...  6.1 us
    ppermute x1, waiting for transfers between devices, on_device(): far_q = lax.ppermute(later_q, 'seq', partners)  5.58 us
    pallas_call x1, Pallas kernels, near_part(): pl.pallas_call(functools.partial(near_kernel, n, cap, per, heads), out_sh...  5.44 us
    ppermute x1, waiting for transfers between devices, on_device(): mate_v = lax.ppermute(values, 'seq', mates)  4.76 us
    pallas_call x2, Pallas kernels, project(): pl.pallas_call(functools.partial(project_kernel, span, len(parts), steps)...  4.46 us
  transfers between devices with their start and end apart: 19, of which 9 were waited for; matrix products, arithmetic and copies ran while one was open for 0% of the time, Pallas kernels for 26%

profile of v2, /device:TPU:0, one launch (start us, length us, event | category | flops | bytes accessed | tf_op | source)
XLA Modules:
  0.0 89.7 jit_solution(9364650152392634839)
XLA Ops:
  0.0 3.0 %collective-permute-start = (bf16[1088,256]{1,0:T(8,128)(2,1)}, bf16[1088,256]{1,0:T(8,128)(2,1)S(1)}, u32[]{:S(2)}, u32[]{:S(2)}) collective-permute-start(bf16[1088,256]{1,0:T(8,128)(2,1)} %k_ref.1), channel_id=1, source_target_pairs={{0,8},{2,10},{4,12},{6,14},{8,0},{10,2},{12,4},{14,6},{16,24},{18,... | collective-permute-start | bytes 1671176 | tf_op jit(solution)/shard_map/ppermute | solution.py:545
  3.0 0.0 copy-start.4
  3.0 0.7 copy-done.4
  3.7 0.0 copy-start.5
  3.7 0.7 copy-done.5
  4.4 0.4 ranks.1
  4.8 1.1 %copy-done = bf16[1088,256]{1,0:T(8,128)(2,1)S(1)} copy-done((bf16[1088,256]{1,0:T(8,128)(2,1)S(1)}, bf16[1088,256]{1,0:T(8,128)(2,1)}, u32[]{:S(2)}) %copy-start) | copy-done | bytes 557080
  5.8 1.2 %gather_blocks.4 = (bf16[512,256]{1,0:T(8,128)(2,1)S(1)}, bf16[512,256]{1,0:T(8,128)(2,1)S(1)}, bf16[512,256]{1,0:T(8,128)(2,1)S(1)}, bf16[512,256]{1,0:T(8,128)(2,1)S(1)}) custom-call(s32[8,128]{1,0:T(8,128)S(1)} %get-tuple-element.29.spot_ref, bf16[1088,256]{1,0:T(8,128)(2,1)S(1)} %copy-done, bf16[1088,256]{1,0:T(8,128)(2,1)} %v_ref.1), custom_call_target="tpu_custom_call" | custom-call | flops 1 | bytes 1 | tf_op jit(solution)/shard_map/gather_blocks/pallas_call | solution.py:137
  7.0 1.6 %collective-permute-start.1 = (bf16[512,256]{1,0:T(8,128)(2,1)S(1)}, bf16[512,256]{1,0:T(8,128)(2,1)S(1)}, u32[]{:S(2)}, u32[]{:S(2)}) collective-permute-start(bf16[512,256]{1,0:T(8,128)(2,1)S(1)} %get-tuple-element.30), channel_id=1, source_target_pairs={{0,2},{2,0},{4,6},{6,4},{8,10},{10,8},{12,14},{14,12},{16,18},{18,... | collective-permute-start | bytes 786440 | tf_op jit(solution)/shard_map/ppermute | solution.py:154
  8.6 1.5 %collective-permute-start.2 = (bf16[512,256]{1,0:T(8,128)(2,1)S(1)}, bf16[512,256]{1,0:T(8,128)(2,1)S(1)}, u32[]{:S(2)}, u32[]{:S(2)}) collective-permute-start(bf16[512,256]{1,0:T(8,128)(2,1)S(1)} %get-tuple-element.31), channel_id=1, source_target_pairs={{0,4},{2,6},{4,0},{6,2},{8,12},{10,14},{12,8},{14,10},{16,20},{18,... | collective-permute-start | bytes 786440 | tf_op jit(solution)/shard_map/ppermute | solution.py:154
  10.1 0.5 collective-permute-start.3
  10.6 0.0 collective-permute-start.7
  10.6 5.7 %collective-permute-done.1.refs_3_.refs_1_ = bf16[512,256]{1,0:T(8,128)(2,1)S(1)} collective-permute-done((bf16[512,256]{1,0:T(8,128)(2,1)S(1)}, bf16[512,256]{1,0:T(8,128)(2,1)S(1)}, u32[]{:S(2)}, u32[]{:S(2)}) %collective-permute-start.1) | collective-permute-done | bytes 262176 | tf_op jit(solution)/shard_map/ppermute | solution.py:154
  16.3 5.4 %collective-permute-done.2.refs_4_.refs_2_ = bf16[512,256]{1,0:T(8,128)(2,1)S(1)} collective-permute-done((bf16[512,256]{1,0:T(8,128)(2,1)S(1)}, bf16[512,256]{1,0:T(8,128)(2,1)S(1)}, u32[]{:S(2)}, u32[]{:S(2)}) %collective-permute-start.2) | collective-permute-done | bytes 262176 | tf_op jit(solution)/shard_map/ppermute | solution.py:154
  21.7 0.0 collective-permute-done.3.refs_5_.refs_3_
  21.7 2.6 %collective-permute-start.11 = (bf16[1088,256]{1,0:T(8,128)(2,1)}, bf16[1088,256]{1,0:T(8,128)(2,1)S(1)}, u32[]{:S(2)}, u32[]{:S(2)}) collective-permute-start(bf16[1088,256]{1,0:T(8,128)(2,1)} %q_ref.3), channel_id=1, source_target_pairs={{0,16},{2,18},{4,20},{6,22},{8,24},{10,26},{12,28},{14,30},{16,0},... | collective-permute-start | bytes 1671176 | tf_op jit(solution)/shard_map/ppermute | solution.py:552
  24.3 0.0 collective-permute-done.refs_1_.refs_2_
  24.3 0.7 copy-done.6
  25.0 0.7 gather_blocks.5
  25.7 0.0 copy-start.7
  25.7 1.3 %collective-permute-start.4 = (bf16[448,256]{1,0:T(8,128)(2,1)S(1)}, bf16[448,256]{1,0:T(8,128)(2,1)S(1)}, u32[]{:S(2)}, u32[]{:S(2)}) collective-permute-start(bf16[448,256]{1,0:T(8,128)(2,1)S(1)} %get-tuple-element.34), channel_id=1, source_target_pairs={{0,2},{2,0},{4,6},{6,4},{8,10},{10,8},{12,14},{14,12},{16,18},{18,... | collective-permute-start | bytes 688136 | tf_op jit(solution)/shard_map/ppermute | solution.py:154
  27.0 0.8 collective-permute-start.5
  27.8 1.4 %collective-permute-start.6 = (bf16[448,256]{1,0:T(8,128)(2,1)S(1)}, bf16[448,256]{1,0:T(8,128)(2,1)S(1)}, u32[]{:S(2)}, u32[]{:S(2)}) collective-permute-start(bf16[448,256]{1,0:T(8,128)(2,1)S(1)} %get-tuple-element.36), channel_id=1, source_target_pairs={{0,6},{2,4},{4,2},{6,0},{8,14},{10,12},{12,10},{14,8},{16,22},{18,... | collective-permute-start | bytes 688136 | tf_op jit(solution)/shard_map/ppermute | solution.py:154
  29.2 4.8 %collective-permute-done.7.refs_1_.refs_3_ = bf16[1088,256]{1,0:T(8,128)(2,1)S(1)} collective-permute-done((bf16[1088,256]{1,0:T(8,128)(2,1)}, bf16[1088,256]{1,0:T(8,128)(2,1)S(1)}, u32[]{:S(2)}, u32[]{:S(2)}) %collective-permute-start.7) | collective-permute-done | bytes 557088 | tf_op jit(solution)/shard_map/ppermute | solution.py:546
  34.0 0.0 collective-permute-done.4.refs_3_.refs_5_.refs_1_
  34.0 1.2 %gather_blocks.6 = (bf16[448,256]{1,0:T(8,128)(2,1)S(1)}, bf16[448,256]{1,0:T(8,128)(2,1)S(1)}, bf16[448,256]{1,0:T(8,128)(2,1)S(1)}, bf16[448,256]{1,0:T(8,128)(2,1)S(1)}) custom-call(s32[8,128]{1,0:T(8,128)S(1)} %get-tuple-element.29.spot_ref, bf16[1088,256]{1,0:T(8,128)(2,1)} %v_ref.1, bf16[1088,256]{1,0:T(8,128)(2,1)S(1)} %collective-permute-done.7.refs_1_.refs_3_, ...), custom_call_target="tpu_custom_call" | custom-call | flops 1 | bytes 1 | tf_op jit(solution)/shard_map/gather_blocks/pallas_call | solution.py:137
  35.2 1.8 %collective-permute-start.8 = (bf16[448,256]{1,0:T(8,128)(2,1)S(1)}, bf16[448,256]{1,0:T(8,128)(2,1)S(1)}, u32[]{:S(2)}, u32[]{:S(2)}) collective-permute-start(bf16[448,256]{1,0:T(8,128)(2,1)S(1)} %get-tuple-element.38), channel_id=1, source_target_pairs={{0,2},{2,0},{4,6},{6,4},{8,10},{10,8},{12,14},{14,12},{16,18},{18,... | collective-permute-start | bytes 688136 | tf_op jit(solution)/shard_map/ppermute | solution.py:154
  36.9 2.5 %collective-permute-start.9 = (bf16[448,256]{1,0:T(8,128)(2,1)S(1)}, bf16[448,256]{1,0:T(8,128)(2,1)S(1)}, u32[]{:S(2)}, u32[]{:S(2)}) collective-permute-start(bf16[448,256]{1,0:T(8,128)(2,1)S(1)} %get-tuple-element.39), channel_id=1, source_target_pairs={{0,4},{2,6},{4,0},{6,2},{8,12},{10,14},{12,8},{14,10},{16,20},{18,... | collective-permute-start | bytes 688136 | tf_op jit(solution)/shard_map/ppermute | solution.py:154
  39.4 0.0 collective-permute-done.5.refs_6_.refs_2_
  39.4 0.0 collective-permute-start.10
  39.4 0.0 copy-done.1
  39.4 1.2 %gather_blocks.7 = (bf16[1024,256]{1,0:T(8,128)(2,1)S(1)}, bf16[1024,256]{1,0:T(8,128)(2,1)S(1)}, bf16[1024,256]{1,0:T(8,128)(2,1)S(1)}, bf16[1024,256]{1,0:T(8,128)(2,1)S(1)}) custom-call(s32[8,128]{1,0:T(8,128)S(1)} %get-tuple-element.29.spot_ref, bf16[1088,256]{1,0:T(8,128)(2,1)S(1)} %copy-done.1, bf16[1088,256]{1,0:T(8,128)(2,1)} %v_ref.1, ...), custom_call_target="tpu_custom_call" | custom-call | flops 1 | bytes 1 | tf_op jit(solution)/shard_map/gather_blocks/pallas_call | solution.py:137
  40.7 0.0 collective-permute-done.6.refs_7_.refs_3_
  40.7 1.5 %collective-permute-start.12 = (bf16[1024,256]{1,0:T(8,128)(2,1)S(1)}, bf16[1024,256]{1,0:T(8,128)(2,1)S(1)}, u32[]{:S(2)}, u32[]{:S(2)}) collective-permute-start(bf16[1024,256]{1,0:T(8,128)(2,1)S(1)} %get-tuple-element.47), channel_id=1, source_target_pairs={{0,2},{2,0},{4,6},{6,4},{8,10},{10,8},{12,14},{14,12},{16,18},{18,... | collective-permute-start | bytes 1572872 | tf_op jit(solution)/shard_map/ppermute | solution.py:154
  42.2 5.6 %collective-permute-done.11.q_ref = bf16[1088,256]{1,0:T(8,128)(2,1)S(1)} collective-permute-done((bf16[1088,256]{1,0:T(8,128)(2,1)}, bf16[1088,256]{1,0:T(8,128)(2,1)S(1)}, u32[]{:S(2)}, u32[]{:S(2)}) %collective-permute-start.11) | collective-permute-done | bytes 557088 | tf_op jit(solution)/shard_map/ppermute | solution.py:552
  47.8 0.5 collective-permute-start.13
  48.3 0.0 collective-permute-done.8.refs_9_.refs_5_
  48.3 1.0 %collective-permute-done.9.refs_10_.refs_6_ = bf16[448,256]{1,0:T(8,128)(2,1)S(1)} collective-permute-done((bf16[448,256]{1,0:T(8,128)(2,1)S(1)}, bf16[448,256]{1,0:T(8,128)(2,1)S(1)}, u32[]{:S(2)}, u32[]{:S(2)}) %collective-permute-start.9) | collective-permute-done | bytes 229408 | tf_op jit(solution)/shard_map/ppermute | solution.py:154
  49.3 1.5 %collective-permute-done.10.refs_11_.refs_7_ = bf16[448,256]{1,0:T(8,128)(2,1)S(1)} collective-permute-done((bf16[448,256]{1,0:T(8,128)(2,1)S(1)}, bf16[448,256]{1,0:T(8,128)(2,1)S(1)}, u32[]{:S(2)}, u32[]{:S(2)}) %collective-permute-start.10) | collective-permute-done | bytes 229408 | tf_op jit(solution)/shard_map/ppermute | solution.py:154
  50.8 0.0 copy-done.7
  50.8 3.2 %far_part.2.refs_12_ = bf16[608,256]{1,0:T(8,128)(2,1)S(1)} custom-call(s32[8,384]{1,0:T(8,128)S(1)} %get-tuple-element.41.arrive_ref, s32[2]{0:T(128)S(1)} %copy-done.7, bf16[1088,256]{1,0:T(8,128)(2,1)S(1)} %collective-permute-done.11.q_ref, bf16[512,256]{1,0:T(8,128)(2,1)S(1)} %get-tuple-element.43.refs_0_, ...), custom_call_target="tpu_custom_call" | custom-call | flops 4000000000 | bytes 1 | tf_op jit(solution)/shard_map/far_part/pallas_call | solution.py:335
  54.0 0.0 copy-start.3
  54.0 2.9 %far_part.3.refs_8_ = bf16[544,256]{1,0:T(8,128)(2,1)S(1)} custom-call(s32[8,384]{1,0:T(8,128)S(1)} %get-tuple-element.41.arrive_ref, s32[2]{0:T(128)S(1)} %copy-done.7, bf16[1088,256]{1,0:T(8,128)(2,1)S(1)} %collective-permute-done.11.q_ref, bf16[512,256]{1,0:T(8,128)(2,1)S(1)} %get-tuple-element.43.refs_0_, ...), custom_call_target="tpu_custom_call" | custom-call | flops 4000000000 | bytes 1 | tf_op jit(solution)/shard_map/far_part/pallas_call | solution.py:335
  56.9 0.5 collective-permute-start.14
  57.5 0.7 collective-permute-start.15
  58.1 2.3 %collective-permute-start.17 = (bf16[608,256]{1,0:T(8,128)(2,1)S(1)}, bf16[608,256]{1,0:T(8,128)(2,1)S(1)}, u32[]{:S(2)}, u32[]{:S(2)}) collective-permute-start(bf16[608,256]{1,0:T(8,128)(2,1)S(1)} %far_part.2.refs_12_), channel_id=1, source_target_pairs={{0,16},{2,18},{4,20},{6,22},{8,24},{10,26},{12,28},{14,30},{16,0},... | collective-permute-start | bytes 933896 | tf_op jit(solution)/shard_map/ppermute | solution.py:574
  60.4 0.0 copy-done.3
  60.4 5.4 %near_part.1 = (f32[1088,256]{1,0:T(8,128)S(1)}, f32[24,256]{1,0:T(8,128)S(1)}) custom-call(s32[2]{0:T(128)S(1)} %copy-done.7, bf16[1088,256]{1,0:T(8,128)(2,1)S(1)} %copy-done.3, bf16[1088,256]{1,0:T(8,128)(2,1)S(1)} %copy-done.1, bf16[1088,256]{1,0:T(8,128)(2,1)} %v_ref.1, bf16[448,256]{1,0:T(8,128)(2,1)S(1)} %get-tuple-element.33.refs_4_.refs_0_, ...), custom_call_target="tpu_custom_call" | custom-call | flops 1 | bytes 1 | tf_op jit(solution)/shard_map/near_part/pallas_call | solution.py:402
  65.8 0.0 collective-permute-done.12.refs_1_
  65.9 6.0 %collective-permute-done.13.refs_2_ = bf16[1024,256]{1,0:T(8,128)(2,1)S(1)} collective-permute-done((bf16[1024,256]{1,0:T(8,128)(2,1)S(1)}, bf16[1024,256]{1,0:T(8,128)(2,1)S(1)}, u32[]{:S(2)}, u32[]{:S(2)}) %collective-permute-start.13) | collective-permute-done | bytes 524320 | tf_op jit(solution)/shard_map/ppermute | solution.py:154
  71.8 0.0 collective-permute-done.14.refs_3_
  71.8 3.4 %rand_part.1 = (f32[1088,256]{1,0:T(8,128)S(1)}, f32[24,256]{1,0:T(8,128)S(1)}) custom-call(s32[8,384]{1,0:T(8,128)S(1)} %get-tuple-element.41.arrive_ref, bf16[1088,256]{1,0:T(8,128)(2,1)S(1)} %copy-done.3, bf16[1024,256]{1,0:T(8,128)(2,1)S(1)} %get-tuple-element.44.refs_12_.refs_0_, bf16[1024,256]{1,0:T(8,128)(2,1)S(1)} %collective-permute-done.12.refs_1_, ...), custom_call_target="tpu_custom_call" | custom-call | flops 4000000000 | bytes 1 | tf_op jit(solution)/shard_map/rand_part/pallas_call | solution.py:439
  75.2 7.5 %collective-permute-done.17.far_ref = bf16[608,256]{1,0:T(8,128)(2,1)S(1)} collective-permute-done((bf16[608,256]{1,0:T(8,128)(2,1)S(1)}, bf16[608,256]{1,0:T(8,128)(2,1)S(1)}, u32[]{:S(2)}, u32[]{:S(2)}) %collective-permute-start.17) | collective-permute-done | bytes 311328 | tf_op jit(solution)/shard_map/ppermute | solution.py:574
  82.7 0.7 contexts.3.refs_0_
  83.4 0.0 copy-start.2
  83.4 0.1 collective-permute-start.18
  83.5 0.0 collective-permute-done.15.far_ref
  83.5 0.7 contexts.2.refs_0_
  84.2 0.6 collective-permute-start.16
  84.7 0.3 collective-permute-done.18.refs_1_
  85.1 0.0 copy-done.2
  85.1 2.3 %project.2.refs_3_ = bf16[1088,2048]{1,0:T(8,128)(2,1)} custom-call(bf16[576,256]{1,0:T(8,128)(2,1)S(1)} %contexts.3.refs_0_, bf16[576,256]{1,0:T(8,128)(2,1)S(1)} %collective-permute-done.18.refs_1_, bf16[512,2048]{1,0:T(8,128)(2,1)S(1)} %copy-done.2), custom_call_target="tpu_custom_call" | custom-call | flops 1 | bytes 1 | tf_op jit(solution)/shard_map/project/pallas_call | solution.py:519
  87.4 0.0 collective-permute-done.16.refs_1_
  87.4 2.2 %project.3 = bf16[1088,2048]{1,0:T(8,128)(2,1)} custom-call(bf16[512,256]{1,0:T(8,128)(2,1)S(1)} %contexts.2.refs_0_, bf16[512,256]{1,0:T(8,128)(2,1)S(1)} %collective-permute-done.16.refs_1_, bf16[512,2048]{1,0:T(8,128)(2,1)S(1)} %copy-done.2, bf16[1088,2048]{1,0:T(8,128)(2,1)} %project.2.refs_3_), custom_call_target="tpu_custom_call", output_to_operand_aliasing={{}: (3, {})} | custom-call | flops 1 | bytes 1 | tf_op jit(solution)/shard_map/project/pallas_call | solution.py:519
  (3 shorter events, 0.0 us)
Async XLA Ops:
  0.0 24.3 %collective-permute-start = (bf16[1088,256]{1,0:T(8,128)(2,1)}, bf16[1088,256]{1,0:T(8,128)(2,1)S(1)}, u32[]{:S(2)}, u32[]{:S(2)}) collective-permute-start(bf16[1088,256]{1,0:T(8,128)(2,1)} %k_ref.1), channel_id=1, source_target_pairs={{0,8},{2,10},{4,12},{6,14},{8,0},{10,2},{12,4},{14,6},{16,24},{18,... | collective-permute-start | bytes 1671176 | tf_op jit(solution)/shard_map/ppermute | solution.py:545
  3.0 0.7 copy-start.4
  3.7 0.7 copy-start.5
  4.8 1.1 %copy-start = (bf16[1088,256]{1,0:T(8,128)(2,1)S(1)}, bf16[1088,256]{1,0:T(8,128)(2,1)}, u32[]{:S(2)}) copy-start(bf16[1088,256]{1,0:T(8,128)(2,1)} %k_ref.1) | copy-start | bytes 1671172
  5.8 33.6 %copy-start.1 = (bf16[1088,256]{1,0:T(8,128)(2,1)S(1)}, bf16[1088,256]{1,0:T(8,128)(2,1)}, u32[]{:S(2)}) copy-start(bf16[1088,256]{1,0:T(8,128)(2,1)} %k_ref.1) | copy-start | bytes 1671172
  7.0 9.3 %collective-permute-start.1 = (bf16[512,256]{1,0:T(8,128)(2,1)S(1)}, bf16[512,256]{1,0:T(8,128)(2,1)S(1)}, u32[]{:S(2)}, u32[]{:S(2)}) collective-permute-start(bf16[512,256]{1,0:T(8,128)(2,1)S(1)} %get-tuple-element.30), channel_id=1, source_target_pairs={{0,2},{2,0},{4,6},{6,4},{8,10},{10,8},{12,14},{14,12},{16,18},{18,... | collective-permute-start | bytes 786440 | tf_op jit(solution)/shard_map/ppermute | solution.py:154
  8.6 13.1 %collective-permute-start.2 = (bf16[512,256]{1,0:T(8,128)(2,1)S(1)}, bf16[512,256]{1,0:T(8,128)(2,1)S(1)}, u32[]{:S(2)}, u32[]{:S(2)}) collective-permute-start(bf16[512,256]{1,0:T(8,128)(2,1)S(1)} %get-tuple-element.31), channel_id=1, source_target_pairs={{0,4},{2,6},{4,0},{6,2},{8,12},{10,14},{12,8},{14,10},{16,20},{18,... | collective-permute-start | bytes 786440 | tf_op jit(solution)/shard_map/ppermute | solution.py:154
  10.1 11.6 %collective-permute-start.3 = (bf16[512,256]{1,0:T(8,128)(2,1)S(1)}, bf16[512,256]{1,0:T(8,128)(2,1)S(1)}, u32[]{:S(2)}, u32[]{:S(2)}) collective-permute-start(bf16[512,256]{1,0:T(8,128)(2,1)S(1)} %get-tuple-element.32), channel_id=1, source_target_pairs={{0,6},{2,4},{4,2},{6,0},{8,14},{10,12},{12,10},{14,8},{16,22},{18,... | collective-permute-start | bytes 786440 | tf_op jit(solution)/shard_map/ppermute | solution.py:154
  10.6 23.4 %collective-permute-start.7 = (bf16[1088,256]{1,0:T(8,128)(2,1)}, bf16[1088,256]{1,0:T(8,128)(2,1)S(1)}, u32[]{:S(2)}, u32[]{:S(2)}) collective-permute-start(bf16[1088,256]{1,0:T(8,128)(2,1)} %v_ref.1), channel_id=1, source_target_pairs={{0,8},{2,10},{4,12},{6,14},{8,0},{10,2},{12,4},{14,6},{16,24},{18,... | collective-permute-start | bytes 1671176 | tf_op jit(solution)/shard_map/ppermute | solution.py:546
  21.7 26.1 %collective-permute-start.11 = (bf16[1088,256]{1,0:T(8,128)(2,1)}, bf16[1088,256]{1,0:T(8,128)(2,1)S(1)}, u32[]{:S(2)}, u32[]{:S(2)}) collective-permute-start(bf16[1088,256]{1,0:T(8,128)(2,1)} %q_ref.3), channel_id=1, source_target_pairs={{0,16},{2,18},{4,20},{6,22},{8,24},{10,26},{12,28},{14,30},{16,0},... | collective-permute-start | bytes 1671176 | tf_op jit(solution)/shard_map/ppermute | solution.py:552
  24.3 0.7 copy-start.6
  25.7 25.2 %copy-start.7 = (s32[2]{0:T(128)S(1)}, s32[2]{0:T(128)}, u32[]{:S(2)}) copy-start(s32[2]{0:T(128)} %place_ref.5) | copy-start | bytes 28
  25.7 8.3 %collective-permute-start.4 = (bf16[448,256]{1,0:T(8,128)(2,1)S(1)}, bf16[448,256]{1,0:T(8,128)(2,1)S(1)}, u32[]{:S(2)}, u32[]{:S(2)}) collective-permute-start(bf16[448,256]{1,0:T(8,128)(2,1)S(1)} %get-tuple-element.34), channel_id=1, source_target_pairs={{0,2},{2,0},{4,6},{6,4},{8,10},{10,8},{12,14},{14,12},{16,18},{18,... | collective-permute-start | bytes 688136 | tf_op jit(solution)/shard_map/ppermute | solution.py:154
  27.0 12.5 %collective-permute-start.5 = (bf16[448,256]{1,0:T(8,128)(2,1)S(1)}, bf16[448,256]{1,0:T(8,128)(2,1)S(1)}, u32[]{:S(2)}, u32[]{:S(2)}) collective-permute-start(bf16[448,256]{1,0:T(8,128)(2,1)S(1)} %get-tuple-element.35), channel_id=1, source_target_pairs={{0,4},{2,6},{4,0},{6,2},{8,12},{10,14},{12,8},{14,10},{16,20},{18,... | collective-permute-start | bytes 688136 | tf_op jit(solution)/shard_map/ppermute | solution.py:154
  27.8 12.9 %collective-permute-start.6 = (bf16[448,256]{1,0:T(8,128)(2,1)S(1)}, bf16[448,256]{1,0:T(8,128)(2,1)S(1)}, u32[]{:S(2)}, u32[]{:S(2)}) collective-permute-start(bf16[448,256]{1,0:T(8,128)(2,1)S(1)} %get-tuple-element.36), channel_id=1, source_target_pairs={{0,6},{2,4},{4,2},{6,0},{8,14},{10,12},{12,10},{14,8},{16,22},{18,... | collective-permute-start | bytes 688136 | tf_op jit(solution)/shard_map/ppermute | solution.py:154
  35.2 13.1 %collective-permute-start.8 = (bf16[448,256]{1,0:T(8,128)(2,1)S(1)}, bf16[448,256]{1,0:T(8,128)(2,1)S(1)}, u32[]{:S(2)}, u32[]{:S(2)}) collective-permute-start(bf16[448,256]{1,0:T(8,128)(2,1)S(1)} %get-tuple-element.38), channel_id=1, source_target_pairs={{0,2},{2,0},{4,6},{6,4},{8,10},{10,8},{12,14},{14,12},{16,18},{18,... | collective-permute-start | bytes 688136 | tf_op jit(solution)/shard_map/ppermute | solution.py:154
  36.9 12.4 %collective-permute-start.9 = (bf16[448,256]{1,0:T(8,128)(2,1)S(1)}, bf16[448,256]{1,0:T(8,128)(2,1)S(1)}, u32[]{:S(2)}, u32[]{:S(2)}) collective-permute-start(bf16[448,256]{1,0:T(8,128)(2,1)S(1)} %get-tuple-element.39), channel_id=1, source_target_pairs={{0,4},{2,6},{4,0},{6,2},{8,12},{10,14},{12,8},{14,10},{16,20},{18,... | collective-permute-start | bytes 688136 | tf_op jit(solution)/shard_map/ppermute | solution.py:154
  39.4 11.4 %collective-permute-start.10 = (bf16[448,256]{1,0:T(8,128)(2,1)S(1)}, bf16[448,256]{1,0:T(8,128)(2,1)S(1)}, u32[]{:S(2)}, u32[]{:S(2)}) collective-permute-start(bf16[448,256]{1,0:T(8,128)(2,1)S(1)} %get-tuple-element.40), channel_id=1, source_target_pairs={{0,6},{2,4},{4,2},{6,0},{8,14},{10,12},{12,10},{14,8},{16,22},{18,... | collective-permute-start | bytes 688136 | tf_op jit(solution)/shard_map/ppermute | solution.py:154
  40.7 25.2 %collective-permute-start.12 = (bf16[1024,256]{1,0:T(8,128)(2,1)S(1)}, bf16[1024,256]{1,0:T(8,128)(2,1)S(1)}, u32[]{:S(2)}, u32[]{:S(2)}) collective-permute-start(bf16[1024,256]{1,0:T(8,128)(2,1)S(1)} %get-tuple-element.47), channel_id=1, source_target_pairs={{0,2},{2,0},{4,6},{6,4},{8,10},{10,8},{12,14},{14,12},{16,18},{18,... | collective-permute-start | bytes 1572872 | tf_op jit(solution)/shard_map/ppermute | solution.py:154
  47.8 24.1 %collective-permute-start.13 = (bf16[1024,256]{1,0:T(8,128)(2,1)S(1)}, bf16[1024,256]{1,0:T(8,128)(2,1)S(1)}, u32[]{:S(2)}, u32[]{:S(2)}) collective-permute-start(bf16[1024,256]{1,0:T(8,128)(2,1)S(1)} %get-tuple-element.48), channel_id=1, source_target_pairs={{0,4},{2,6},{4,0},{6,2},{8,12},{10,14},{12,8},{14,10},{16,20},{18,... | collective-permute-start | bytes 1572872 | tf_op jit(solution)/shard_map/ppermute | solution.py:154
  54.0 6.4 %copy-start.3 = (bf16[1088,256]{1,0:T(8,128)(2,1)S(1)}, bf16[1088,256]{1,0:T(8,128)(2,1)}, u32[]{:S(2)}) copy-start(bf16[1088,256]{1,0:T(8,128)(2,1)} %q_ref.3) | copy-start | bytes 1671172
  56.9 14.9 %collective-permute-start.14 = (bf16[1024,256]{1,0:T(8,128)(2,1)S(1)}, bf16[1024,256]{1,0:T(8,128)(2,1)S(1)}, u32[]{:S(2)}, u32[]{:S(2)}) collective-permute-start(bf16[1024,256]{1,0:T(8,128)(2,1)S(1)} %get-tuple-element.50), channel_id=1, source_target_pairs={{0,6},{2,4},{4,2},{6,0},{8,14},{10,12},{12,10},{14,8},{16,22},{18,... | collective-permute-start | bytes 1572872 | tf_op jit(solution)/shard_map/ppermute | solution.py:154
  57.5 26.0 %collective-permute-start.15 = (bf16[544,256]{1,0:T(8,128)(2,1)S(1)}, bf16[544,256]{1,0:T(8,128)(2,1)S(1)}, u32[]{:S(2)}, u32[]{:S(2)}) collective-permute-start(bf16[544,256]{1,0:T(8,128)(2,1)S(1)} %far_part.3.refs_8_), channel_id=1, source_target_pairs={{0,16},{2,18},{4,20},{6,22},{8,24},{10,26},{12,28},{14,30},{16,0},... | collective-permute-start | bytes 835592 | tf_op jit(solution)/shard_map/ppermute | solution.py:574
  58.1 24.6 %collective-permute-start.17 = (bf16[608,256]{1,0:T(8,128)(2,1)S(1)}, bf16[608,256]{1,0:T(8,128)(2,1)S(1)}, u32[]{:S(2)}, u32[]{:S(2)}) collective-permute-start(bf16[608,256]{1,0:T(8,128)(2,1)S(1)} %far_part.2.refs_12_), channel_id=1, source_target_pairs={{0,16},{2,18},{4,20},{6,22},{8,24},{10,26},{12,28},{14,30},{16,0},... | collective-permute-start | bytes 933896 | tf_op jit(solution)/shard_map/ppermute | solution.py:574
  83.4 1.7 %copy-start.2 = (bf16[512,2048]{1,0:T(8,128)(2,1)S(1)}, bf16[512,2048]{1,0:T(8,128)(2,1)}, u32[]{:S(2)}) copy-start(bf16[512,2048]{1,0:T(8,128)(2,1)} %refs_2_.7) | copy-start | bytes 6291460
  83.4 1.6 %collective-permute-start.18 = (bf16[576,256]{1,0:T(8,128)(2,1)S(1)}, bf16[576,256]{1,0:T(8,128)(2,1)S(1)}, u32[]{:S(2)}, u32[]{:S(2)}) collective-permute-start(bf16[576,256]{1,0:T(8,128)(2,1)S(1)} %contexts.3.refs_0_), channel_id=1, source_target_pairs={{1,0},{0,1},{3,2},{2,3},{5,4},{4,5},{7,6},{6,7},{9,8},{8,9},{11,10... | collective-permute-start | bytes 884744 | tf_op jit(solution)/shard_map/ppermute | solution.py:581
  84.2 3.2 %collective-permute-start.16 = (bf16[512,256]{1,0:T(8,128)(2,1)S(1)}, bf16[512,256]{1,0:T(8,128)(2,1)S(1)}, u32[]{:S(2)}, u32[]{:S(2)}) collective-permute-start(bf16[512,256]{1,0:T(8,128)(2,1)S(1)} %contexts.2.refs_0_), channel_id=1, source_target_pairs={{1,0},{0,1},{3,2},{2,3},{5,4},{4,5},{7,6},{6,7},{9,8},{8,9},{11,10... | collective-permute-start | bytes 786440 | tf_op jit(solution)/shard_map/ppermute | solution.py:581

commit v3 on v1

--- a/solution.py
+++ b/solution.py
@@ -560,7 +560,7 @@
     rows = {(0, 0): keys, (0, 1): values, (1, 0): mate_k, (1, 1): mate_v}
     lists = ((0, False, (0, 1)), (1, False, (0, 1)))
     third = gather(n, per, cap, lists, spots, rows, (), sent[:1])
-    middle = (per + 1) // 2
+    middle = per * 7 // 17
     spans = ((0, middle), (middle, per))
     fars = []
     earlier = third[0]

time: 85.6 us -> 87.7 us (1.025)
  waiting for transfers between devices: 31.8 us -> 33.3 us
    ppermute x2, waiting for transfers between devices: 0.01 us -> 1.12 us  [on_device(): lax.ppermute(context, 'head', [((i + s) % heads, i) for i in range(heads)])]
  transfers between devices with their start and end apart: 19 -> 19, of which waited for: 7 -> 8; matrix products, arithmetic and copies ran while one was open for 0% -> 0% of each run, Pallas kernels for 27% -> 26%
where the time goes in v3:
time: 87.7 us; the launch traced here: 87.3 us
  waiting for transfers between devices  33.3 us (38%)
  Pallas kernels  25.5 us (29%)
  starting transfers between devices  25.1 us (29%)
  local copies, waits for them, and re-layouts  3.12 us (4%)
    ppermute x12, waiting for transfers between devices, exchange(): got.append(lax.ppermute(parts[k], 'seq', [(i, i ^ k) for i in range(n)]))  17.8 us
    ppermute x12, starting transfers between devices, exchange(): got.append(lax.ppermute(parts[k], 'seq', [(i, i ^ k) for i in range(n)]))  15.8 us
    pallas_call x2, Pallas kernels, far_part(): pl.pallas_call(functools.partial(far_kernel, n, cap, per, heads, span), o...  5.93 us
    ppermute x1, waiting for transfers between devices, on_device(): far_q = lax.ppermute(later_q, 'seq', partners)  5.58 us
    pallas_call x1, Pallas kernels, near_part(): pl.pallas_call(functools.partial(near_kernel, n, cap, per, heads), out_sh...  5.44 us
    ppermute x1, waiting for transfers between devices, on_device(): mate_v = lax.ppermute(values, 'seq', mates)  4.76 us
    pallas_call x2, Pallas kernels, project(): pl.pallas_call(functools.partial(project_kernel, span, len(parts), steps)...  4.7 us
    pallas_call x4, Pallas kernels, gather(): pl.pallas_call(functools.partial(gather_kernel, n, per, cap, lists, bool(...  4.28 us
  transfers between devices with their start and end apart: 19, of which 8 were waited for; matrix products, arithmetic and copies ran while one was open for 0% of the time, Pallas kernels for 26%

profile of v3, /device:TPU:0, one launch (start us, length us, event | category | flops | bytes accessed | tf_op | source)
XLA Modules:
  0.0 87.3 jit_solution(16000844394065793701)
XLA Ops:
  0.0 3.0 %collective-permute-start = (bf16[1088,256]{1,0:T(8,128)(2,1)}, bf16[1088,256]{1,0:T(8,128)(2,1)S(1)}, u32[]{:S(2)}, u32[]{:S(2)}) collective-permute-start(bf16[1088,256]{1,0:T(8,128)(2,1)} %k_ref.1), channel_id=1, source_target_pairs={{0,8},{2,10},{4,12},{6,14},{8,0},{10,2},{12,4},{14,6},{16,24},{18,... | collective-permute-start | bytes 1671176 | tf_op jit(solution)/shard_map/ppermute | solution.py:545
  3.0 0.0 copy-start.4
  3.0 0.7 copy-done.4
  3.7 0.7 copy-done.5
  4.4 0.4 ranks.1
  4.8 0.0 copy-start
  4.8 1.1 %copy-done = bf16[1088,256]{1,0:T(8,128)(2,1)S(1)} copy-done((bf16[1088,256]{1,0:T(8,128)(2,1)S(1)}, bf16[1088,256]{1,0:T(8,128)(2,1)}, u32[]{:S(2)}) %copy-start) | copy-done | bytes 557080
  5.8 1.2 %gather_blocks.4 = (bf16[512,256]{1,0:T(8,128)(2,1)S(1)}, bf16[512,256]{1,0:T(8,128)(2,1)S(1)}, bf16[512,256]{1,0:T(8,128)(2,1)S(1)}, bf16[512,256]{1,0:T(8,128)(2,1)S(1)}) custom-call(s32[8,128]{1,0:T(8,128)S(1)} %get-tuple-element.28.spot_ref, bf16[1088,256]{1,0:T(8,128)(2,1)S(1)} %copy-done, bf16[1088,256]{1,0:T(8,128)(2,1)} %v_ref.1), custom_call_target="tpu_custom_call" | custom-call | flops 1 | bytes 1 | tf_op jit(solution)/shard_map/gather_blocks/pallas_call | solution.py:137
  7.0 1.6 %collective-permute-start.1 = (bf16[512,256]{1,0:T(8,128)(2,1)S(1)}, bf16[512,256]{1,0:T(8,128)(2,1)S(1)}, u32[]{:S(2)}, u32[]{:S(2)}) collective-permute-start(bf16[512,256]{1,0:T(8,128)(2,1)S(1)} %get-tuple-element.29), channel_id=1, source_target_pairs={{0,2},{2,0},{4,6},{6,4},{8,10},{10,8},{12,14},{14,12},{16,18},{18,... | collective-permute-start | bytes 786440 | tf_op jit(solution)/shard_map/ppermute | solution.py:154
  8.6 1.5 %collective-permute-start.2 = (bf16[512,256]{1,0:T(8,128)(2,1)S(1)}, bf16[512,256]{1,0:T(8,128)(2,1)S(1)}, u32[]{:S(2)}, u32[]{:S(2)}) collective-permute-start(bf16[512,256]{1,0:T(8,128)(2,1)S(1)} %get-tuple-element.30), channel_id=1, source_target_pairs={{0,4},{2,6},{4,0},{6,2},{8,12},{10,14},{12,8},{14,10},{16,20},{18,... | collective-permute-start | bytes 786440 | tf_op jit(solution)/shard_map/ppermute | solution.py:154
  10.1 0.5 collective-permute-start.3
  10.6 0.0 collective-permute-start.7
  10.6 5.7 %collective-permute-done.1.refs_3_.refs_1_ = bf16[512,256]{1,0:T(8,128)(2,1)S(1)} collective-permute-done((bf16[512,256]{1,0:T(8,128)(2,1)S(1)}, bf16[512,256]{1,0:T(8,128)(2,1)S(1)}, u32[]{:S(2)}, u32[]{:S(2)}) %collective-permute-start.1) | collective-permute-done | bytes 262176 | tf_op jit(solution)/shard_map/ppermute | solution.py:154
  16.3 5.4 %collective-permute-done.2.refs_4_.refs_2_ = bf16[512,256]{1,0:T(8,128)(2,1)S(1)} collective-permute-done((bf16[512,256]{1,0:T(8,128)(2,1)S(1)}, bf16[512,256]{1,0:T(8,128)(2,1)S(1)}, u32[]{:S(2)}, u32[]{:S(2)}) %collective-permute-start.2) | collective-permute-done | bytes 262176 | tf_op jit(solution)/shard_map/ppermute | solution.py:154
  21.7 0.0 collective-permute-done.3.refs_5_.refs_3_
  21.7 2.6 %collective-permute-start.11 = (bf16[1088,256]{1,0:T(8,128)(2,1)}, bf16[1088,256]{1,0:T(8,128)(2,1)S(1)}, u32[]{:S(2)}, u32[]{:S(2)}) collective-permute-start(bf16[1088,256]{1,0:T(8,128)(2,1)} %q_ref.3), channel_id=1, source_target_pairs={{0,16},{2,18},{4,20},{6,22},{8,24},{10,26},{12,28},{14,30},{16,0},... | collective-permute-start | bytes 1671176 | tf_op jit(solution)/shard_map/ppermute | solution.py:552
  24.3 0.0 collective-permute-done.refs_1_.refs_2_
  24.3 0.7 copy-done.6
  25.0 0.7 gather_blocks.5
  25.7 0.0 copy-start.7
  25.7 1.3 %collective-permute-start.4 = (bf16[448,256]{1,0:T(8,128)(2,1)S(1)}, bf16[448,256]{1,0:T(8,128)(2,1)S(1)}, u32[]{:S(2)}, u32[]{:S(2)}) collective-permute-start(bf16[448,256]{1,0:T(8,128)(2,1)S(1)} %get-tuple-element.33), channel_id=1, source_target_pairs={{0,2},{2,0},{4,6},{6,4},{8,10},{10,8},{12,14},{14,12},{16,18},{18,... | collective-permute-start | bytes 688136 | tf_op jit(solution)/shard_map/ppermute | solution.py:154
  27.0 0.8 collective-permute-start.5
  27.8 1.4 %collective-permute-start.6 = (bf16[448,256]{1,0:T(8,128)(2,1)S(1)}, bf16[448,256]{1,0:T(8,128)(2,1)S(1)}, u32[]{:S(2)}, u32[]{:S(2)}) collective-permute-start(bf16[448,256]{1,0:T(8,128)(2,1)S(1)} %get-tuple-element.35), channel_id=1, source_target_pairs={{0,6},{2,4},{4,2},{6,0},{8,14},{10,12},{12,10},{14,8},{16,22},{18,... | collective-permute-start | bytes 688136 | tf_op jit(solution)/shard_map/ppermute | solution.py:154
  29.2 4.8 %collective-permute-done.7.refs_1_.refs_3_ = bf16[1088,256]{1,0:T(8,128)(2,1)S(1)} collective-permute-done((bf16[1088,256]{1,0:T(8,128)(2,1)}, bf16[1088,256]{1,0:T(8,128)(2,1)S(1)}, u32[]{:S(2)}, u32[]{:S(2)}) %collective-permute-start.7) | collective-permute-done | bytes 557088 | tf_op jit(solution)/shard_map/ppermute | solution.py:546
  34.0 0.0 collective-permute-done.4.refs_3_.refs_5_.refs_1_
  34.0 1.2 %gather_blocks.6 = (bf16[448,256]{1,0:T(8,128)(2,1)S(1)}, bf16[448,256]{1,0:T(8,128)(2,1)S(1)}, bf16[448,256]{1,0:T(8,128)(2,1)S(1)}, bf16[448,256]{1,0:T(8,128)(2,1)S(1)}) custom-call(s32[8,128]{1,0:T(8,128)S(1)} %get-tuple-element.28.spot_ref, bf16[1088,256]{1,0:T(8,128)(2,1)} %v_ref.1, bf16[1088,256]{1,0:T(8,128)(2,1)S(1)} %collective-permute-done.7.refs_1_.refs_3_, ...), custom_call_target="tpu_custom_call" | custom-call | flops 1 | bytes 1 | tf_op jit(solution)/shard_map/gather_blocks/pallas_call | solution.py:137
  35.2 1.8 %collective-permute-start.8 = (bf16[448,256]{1,0:T(8,128)(2,1)S(1)}, bf16[448,256]{1,0:T(8,128)(2,1)S(1)}, u32[]{:S(2)}, u32[]{:S(2)}) collective-permute-start(bf16[448,256]{1,0:T(8,128)(2,1)S(1)} %get-tuple-element.37), channel_id=1, source_target_pairs={{0,2},{2,0},{4,6},{6,4},{8,10},{10,8},{12,14},{14,12},{16,18},{18,... | collective-permute-start | bytes 688136 | tf_op jit(solution)/shard_map/ppermute | solution.py:154
  36.9 2.5 %collective-permute-start.9 = (bf16[448,256]{1,0:T(8,128)(2,1)S(1)}, bf16[448,256]{1,0:T(8,128)(2,1)S(1)}, u32[]{:S(2)}, u32[]{:S(2)}) collective-permute-start(bf16[448,256]{1,0:T(8,128)(2,1)S(1)} %get-tuple-element.38), channel_id=1, source_target_pairs={{0,4},{2,6},{4,0},{6,2},{8,12},{10,14},{12,8},{14,10},{16,20},{18,... | collective-permute-start | bytes 688136 | tf_op jit(solution)/shard_map/ppermute | solution.py:154
  39.4 0.0 collective-permute-done.5.refs_6_.refs_2_
  39.4 0.0 collective-permute-start.10
  39.4 0.0 copy-done.1
  39.4 1.2 %gather_blocks.7 = (bf16[1024,256]{1,0:T(8,128)(2,1)S(1)}, bf16[1024,256]{1,0:T(8,128)(2,1)S(1)}, bf16[1024,256]{1,0:T(8,128)(2,1)S(1)}, bf16[1024,256]{1,0:T(8,128)(2,1)S(1)}) custom-call(s32[8,128]{1,0:T(8,128)S(1)} %get-tuple-element.28.spot_ref, bf16[1088,256]{1,0:T(8,128)(2,1)S(1)} %copy-done.1, bf16[1088,256]{1,0:T(8,128)(2,1)} %v_ref.1, ...), custom_call_target="tpu_custom_call" | custom-call | flops 1 | bytes 1 | tf_op jit(solution)/shard_map/gather_blocks/pallas_call | solution.py:137
  40.7 0.0 collective-permute-done.6.refs_7_.refs_3_
  40.7 1.5 %collective-permute-start.12 = (bf16[1024,256]{1,0:T(8,128)(2,1)S(1)}, bf16[1024,256]{1,0:T(8,128)(2,1)S(1)}, u32[]{:S(2)}, u32[]{:S(2)}) collective-permute-start(bf16[1024,256]{1,0:T(8,128)(2,1)S(1)} %get-tuple-element.46), channel_id=1, source_target_pairs={{0,2},{2,0},{4,6},{6,4},{8,10},{10,8},{12,14},{14,12},{16,18},{18,... | collective-permute-start | bytes 1572872 | tf_op jit(solution)/shard_map/ppermute | solution.py:154
  42.2 5.6 %collective-permute-done.11.q_ref = bf16[1088,256]{1,0:T(8,128)(2,1)S(1)} collective-permute-done((bf16[1088,256]{1,0:T(8,128)(2,1)}, bf16[1088,256]{1,0:T(8,128)(2,1)S(1)}, u32[]{:S(2)}, u32[]{:S(2)}) %collective-permute-start.11) | collective-permute-done | bytes 557088 | tf_op jit(solution)/shard_map/ppermute | solution.py:552
  47.8 0.5 collective-permute-start.13
  48.3 0.0 collective-permute-done.8.refs_9_.refs_5_
  48.3 2.4 %collective-permute-start.14 = (bf16[1024,256]{1,0:T(8,128)(2,1)S(1)}, bf16[1024,256]{1,0:T(8,128)(2,1)S(1)}, u32[]{:S(2)}, u32[]{:S(2)}) collective-permute-start(bf16[1024,256]{1,0:T(8,128)(2,1)S(1)} %get-tuple-element.48), channel_id=1, source_target_pairs={{0,6},{2,4},{4,2},{6,0},{8,14},{10,12},{12,10},{14,8},{16,22},{18,... | collective-permute-start | bytes 1572872 | tf_op jit(solution)/shard_map/ppermute | solution.py:154
  50.7 0.0 collective-permute-done.9.refs_10_.refs_6_
  50.7 0.1 collective-permute-done.10.refs_11_.refs_7_
  50.8 0.0 copy-done.7
  50.8 2.6 %far_part.2.refs_12_ = bf16[480,256]{1,0:T(8,128)(2,1)S(1)} custom-call(s32[8,384]{1,0:T(8,128)S(1)} %get-tuple-element.40.arrive_ref, s32[2]{0:T(128)S(1)} %copy-done.7, bf16[1088,256]{1,0:T(8,128)(2,1)S(1)} %collective-permute-done.11.q_ref, bf16[512,256]{1,0:T(8,128)(2,1)S(1)} %get-tuple-element.42.refs_0_, ...), custom_call_target="tpu_custom_call" | custom-call | flops 4000000000 | bytes 1 | tf_op jit(solution)/shard_map/far_part/pallas_call | solution.py:335
  53.5 0.0 copy-start.3
  53.5 0.7 collective-permute-start.17
  54.2 3.3 %far_part.3.refs_8_ = bf16[672,256]{1,0:T(8,128)(2,1)S(1)} custom-call(s32[8,384]{1,0:T(8,128)S(1)} %get-tuple-element.40.arrive_ref, s32[2]{0:T(128)S(1)} %copy-done.7, bf16[1088,256]{1,0:T(8,128)(2,1)S(1)} %collective-permute-done.11.q_ref, bf16[512,256]{1,0:T(8,128)(2,1)S(1)} %get-tuple-element.42.refs_0_, ...), custom_call_target="tpu_custom_call" | custom-call | flops 4000000000 | bytes 1 | tf_op jit(solution)/shard_map/far_part/pallas_call | solution.py:335
  57.5 2.3 %collective-permute-start.15 = (bf16[672,256]{1,0:T(8,128)(2,1)S(1)}, bf16[672,256]{1,0:T(8,128)(2,1)S(1)}, u32[]{:S(2)}, u32[]{:S(2)}) collective-permute-start(bf16[672,256]{1,0:T(8,128)(2,1)S(1)} %far_part.3.refs_8_), channel_id=1, source_target_pairs={{0,16},{2,18},{4,20},{6,22},{8,24},{10,26},{12,28},{14,30},{16,0},... | collective-permute-start | bytes 1032200 | tf_op jit(solution)/shard_map/ppermute | solution.py:571
  59.8 0.0 copy-done.3
  59.8 5.4 %near_part.1 = (f32[1088,256]{1,0:T(8,128)S(1)}, f32[24,256]{1,0:T(8,128)S(1)}) custom-call(s32[2]{0:T(128)S(1)} %copy-done.7, bf16[1088,256]{1,0:T(8,128)(2,1)S(1)} %copy-done.3, bf16[1088,256]{1,0:T(8,128)(2,1)S(1)} %copy-done.1, bf16[1088,256]{1,0:T(8,128)(2,1)} %v_ref.1, bf16[448,256]{1,0:T(8,128)(2,1)S(1)} %get-tuple-element.32.refs_4_.refs_0_, ...), custom_call_target="tpu_custom_call" | custom-call | flops 1 | bytes 1 | tf_op jit(solution)/shard_map/near_part/pallas_call | solution.py:402
  65.3 0.0 collective-permute-done.12.refs_1_
  65.3 6.6 %collective-permute-done.13.refs_2_ = bf16[1024,256]{1,0:T(8,128)(2,1)S(1)} collective-permute-done((bf16[1024,256]{1,0:T(8,128)(2,1)S(1)}, bf16[1024,256]{1,0:T(8,128)(2,1)S(1)}, u32[]{:S(2)}, u32[]{:S(2)}) %collective-permute-start.13) | collective-permute-done | bytes 524320 | tf_op jit(solution)/shard_map/ppermute | solution.py:154
  71.8 0.0 collective-permute-done.14.refs_3_
  71.8 3.4 %rand_part.1 = (f32[1088,256]{1,0:T(8,128)S(1)}, f32[24,256]{1,0:T(8,128)S(1)}) custom-call(s32[8,384]{1,0:T(8,128)S(1)} %get-tuple-element.40.arrive_ref, bf16[1088,256]{1,0:T(8,128)(2,1)S(1)} %copy-done.3, bf16[1024,256]{1,0:T(8,128)(2,1)S(1)} %get-tuple-element.43.refs_12_.refs_0_, bf16[1024,256]{1,0:T(8,128)(2,1)S(1)} %collective-permute-done.12.refs_1_, ...), custom_call_target="tpu_custom_call" | custom-call | flops 4000000000 | bytes 1 | tf_op jit(solution)/shard_map/rand_part/pallas_call | solution.py:439
  75.2 4.0 %collective-permute-done.15.far_ref = bf16[672,256]{1,0:T(8,128)(2,1)S(1)} collective-permute-done((bf16[672,256]{1,0:T(8,128)(2,1)S(1)}, bf16[672,256]{1,0:T(8,128)(2,1)S(1)}, u32[]{:S(2)}, u32[]{:S(2)}) %collective-permute-start.15) | collective-permute-done | bytes 344096 | tf_op jit(solution)/shard_map/ppermute | solution.py:571
  79.2 0.8 contexts.2.refs_0_
  80.0 0.0 copy-start.2
  80.0 0.1 collective-permute-start.16
  80.1 0.0 collective-permute-done.17.far_ref
  80.1 0.6 contexts.3.refs_0_
  80.7 0.6 collective-permute-start.18
  81.3 1.1 %collective-permute-done.18.refs_1_ = bf16[448,256]{1,0:T(8,128)(2,1)S(1)} collective-permute-done((bf16[448,256]{1,0:T(8,128)(2,1)S(1)}, bf16[448,256]{1,0:T(8,128)(2,1)S(1)}, u32[]{:S(2)}, u32[]{:S(2)}) %collective-permute-start.18) | collective-permute-done | bytes 229408 | tf_op jit(solution)/shard_map/ppermute | solution.py:579
  82.4 0.0 copy-done.2
  82.4 2.2 %project.2.refs_3_ = bf16[1088,2048]{1,0:T(8,128)(2,1)} custom-call(bf16[448,256]{1,0:T(8,128)(2,1)S(1)} %contexts.3.refs_0_, bf16[448,256]{1,0:T(8,128)(2,1)S(1)} %collective-permute-done.18.refs_1_, bf16[512,2048]{1,0:T(8,128)(2,1)S(1)} %copy-done.2), custom_call_target="tpu_custom_call" | custom-call | flops 1 | bytes 1 | tf_op jit(solution)/shard_map/project/pallas_call | solution.py:519
  84.6 0.0 collective-permute-done.16.refs_1_
  84.7 2.5 %project.3 = bf16[1088,2048]{1,0:T(8,128)(2,1)} custom-call(bf16[640,256]{1,0:T(8,128)(2,1)S(1)} %contexts.2.refs_0_, bf16[640,256]{1,0:T(8,128)(2,1)S(1)} %collective-permute-done.16.refs_1_, bf16[512,2048]{1,0:T(8,128)(2,1)S(1)} %copy-done.2, bf16[1088,2048]{1,0:T(8,128)(2,1)} %project.2.refs_3_), custom_call_target="tpu_custom_call", output_to_operand_aliasing={{}: (3, {})} | custom-call | flops 1 | bytes 1 | tf_op jit(solution)/shard_map/project/pallas_call | solution.py:519
  (3 shorter events, 0.0 us)
Async XLA Ops:
  0.0 24.3 %collective-permute-start = (bf16[1088,256]{1,0:T(8,128)(2,1)}, bf16[1088,256]{1,0:T(8,128)(2,1)S(1)}, u32[]{:S(2)}, u32[]{:S(2)}) collective-permute-start(bf16[1088,256]{1,0:T(8,128)(2,1)} %k_ref.1), channel_id=1, source_target_pairs={{0,8},{2,10},{4,12},{6,14},{8,0},{10,2},{12,4},{14,6},{16,24},{18,... | collective-permute-start | bytes 1671176 | tf_op jit(solution)/shard_map/ppermute | solution.py:545
  3.0 0.7 copy-start.4
  3.7 0.7 copy-start.5
  4.8 1.1 %copy-start = (bf16[1088,256]{1,0:T(8,128)(2,1)S(1)}, bf16[1088,256]{1,0:T(8,128)(2,1)}, u32[]{:S(2)}) copy-start(bf16[1088,256]{1,0:T(8,128)(2,1)} %k_ref.1) | copy-start | bytes 1671172
  5.8 33.6 %copy-start.1 = (bf16[1088,256]{1,0:T(8,128)(2,1)S(1)}, bf16[1088,256]{1,0:T(8,128)(2,1)}, u32[]{:S(2)}) copy-start(bf16[1088,256]{1,0:T(8,128)(2,1)} %k_ref.1) | copy-start | bytes 1671172
  7.0 9.3 %collective-permute-start.1 = (bf16[512,256]{1,0:T(8,128)(2,1)S(1)}, bf16[512,256]{1,0:T(8,128)(2,1)S(1)}, u32[]{:S(2)}, u32[]{:S(2)}) collective-permute-start(bf16[512,256]{1,0:T(8,128)(2,1)S(1)} %get-tuple-element.29), channel_id=1, source_target_pairs={{0,2},{2,0},{4,6},{6,4},{8,10},{10,8},{12,14},{14,12},{16,18},{18,... | collective-permute-start | bytes 786440 | tf_op jit(solution)/shard_map/ppermute | solution.py:154
  8.6 13.1 %collective-permute-start.2 = (bf16[512,256]{1,0:T(8,128)(2,1)S(1)}, bf16[512,256]{1,0:T(8,128)(2,1)S(1)}, u32[]{:S(2)}, u32[]{:S(2)}) collective-permute-start(bf16[512,256]{1,0:T(8,128)(2,1)S(1)} %get-tuple-element.30), channel_id=1, source_target_pairs={{0,4},{2,6},{4,0},{6,2},{8,12},{10,14},{12,8},{14,10},{16,20},{18,... | collective-permute-start | bytes 786440 | tf_op jit(solution)/shard_map/ppermute | solution.py:154
  10.1 11.6 %collective-permute-start.3 = (bf16[512,256]{1,0:T(8,128)(2,1)S(1)}, bf16[512,256]{1,0:T(8,128)(2,1)S(1)}, u32[]{:S(2)}, u32[]{:S(2)}) collective-permute-start(bf16[512,256]{1,0:T(8,128)(2,1)S(1)} %get-tuple-element.31), channel_id=1, source_target_pairs={{0,6},{2,4},{4,2},{6,0},{8,14},{10,12},{12,10},{14,8},{16,22},{18,... | collective-permute-start | bytes 786440 | tf_op jit(solution)/shard_map/ppermute | solution.py:154
  10.6 23.4 %collective-permute-start.7 = (bf16[1088,256]{1,0:T(8,128)(2,1)}, bf16[1088,256]{1,0:T(8,128)(2,1)S(1)}, u32[]{:S(2)}, u32[]{:S(2)}) collective-permute-start(bf16[1088,256]{1,0:T(8,128)(2,1)} %v_ref.1), channel_id=1, source_target_pairs={{0,8},{2,10},{4,12},{6,14},{8,0},{10,2},{12,4},{14,6},{16,24},{18,... | collective-permute-start | bytes 1671176 | tf_op jit(solution)/shard_map/ppermute | solution.py:546
  21.7 26.1 %collective-permute-start.11 = (bf16[1088,256]{1,0:T(8,128)(2,1)}, bf16[1088,256]{1,0:T(8,128)(2,1)S(1)}, u32[]{:S(2)}, u32[]{:S(2)}) collective-permute-start(bf16[1088,256]{1,0:T(8,128)(2,1)} %q_ref.3), channel_id=1, source_target_pairs={{0,16},{2,18},{4,20},{6,22},{8,24},{10,26},{12,28},{14,30},{16,0},... | collective-permute-start | bytes 1671176 | tf_op jit(solution)/shard_map/ppermute | solution.py:552
  24.3 0.7 copy-start.6
  25.7 25.2 %copy-start.7 = (s32[2]{0:T(128)S(1)}, s32[2]{0:T(128)}, u32[]{:S(2)}) copy-start(s32[2]{0:T(128)} %place_ref.5) | copy-start | bytes 28
  25.7 8.3 %collective-permute-start.4 = (bf16[448,256]{1,0:T(8,128)(2,1)S(1)}, bf16[448,256]{1,0:T(8,128)(2,1)S(1)}, u32[]{:S(2)}, u32[]{:S(2)}) collective-permute-start(bf16[448,256]{1,0:T(8,128)(2,1)S(1)} %get-tuple-element.33), channel_id=1, source_target_pairs={{0,2},{2,0},{4,6},{6,4},{8,10},{10,8},{12,14},{14,12},{16,18},{18,... | collective-permute-start | bytes 688136 | tf_op jit(solution)/shard_map/ppermute | solution.py:154
  27.0 12.5 %collective-permute-start.5 = (bf16[448,256]{1,0:T(8,128)(2,1)S(1)}, bf16[448,256]{1,0:T(8,128)(2,1)S(1)}, u32[]{:S(2)}, u32[]{:S(2)}) collective-permute-start(bf16[448,256]{1,0:T(8,128)(2,1)S(1)} %get-tuple-element.34), channel_id=1, source_target_pairs={{0,4},{2,6},{4,0},{6,2},{8,12},{10,14},{12,8},{14,10},{16,20},{18,... | collective-permute-start | bytes 688136 | tf_op jit(solution)/shard_map/ppermute | solution.py:154
  27.8 12.9 %collective-permute-start.6 = (bf16[448,256]{1,0:T(8,128)(2,1)S(1)}, bf16[448,256]{1,0:T(8,128)(2,1)S(1)}, u32[]{:S(2)}, u32[]{:S(2)}) collective-permute-start(bf16[448,256]{1,0:T(8,128)(2,1)S(1)} %get-tuple-element.35), channel_id=1, source_target_pairs={{0,6},{2,4},{4,2},{6,0},{8,14},{10,12},{12,10},{14,8},{16,22},{18,... | collective-permute-start | bytes 688136 | tf_op jit(solution)/shard_map/ppermute | solution.py:154
  35.2 13.1 %collective-permute-start.8 = (bf16[448,256]{1,0:T(8,128)(2,1)S(1)}, bf16[448,256]{1,0:T(8,128)(2,1)S(1)}, u32[]{:S(2)}, u32[]{:S(2)}) collective-permute-start(bf16[448,256]{1,0:T(8,128)(2,1)S(1)} %get-tuple-element.37), channel_id=1, source_target_pairs={{0,2},{2,0},{4,6},{6,4},{8,10},{10,8},{12,14},{14,12},{16,18},{18,... | collective-permute-start | bytes 688136 | tf_op jit(solution)/shard_map/ppermute | solution.py:154
  36.9 13.7 %collective-permute-start.9 = (bf16[448,256]{1,0:T(8,128)(2,1)S(1)}, bf16[448,256]{1,0:T(8,128)(2,1)S(1)}, u32[]{:S(2)}, u32[]{:S(2)}) collective-permute-start(bf16[448,256]{1,0:T(8,128)(2,1)S(1)} %get-tuple-element.38), channel_id=1, source_target_pairs={{0,4},{2,6},{4,0},{6,2},{8,12},{10,14},{12,8},{14,10},{16,20},{18,... | collective-permute-start | bytes 688136 | tf_op jit(solution)/shard_map/ppermute | solution.py:154
  39.4 11.4 %collective-permute-start.10 = (bf16[448,256]{1,0:T(8,128)(2,1)S(1)}, bf16[448,256]{1,0:T(8,128)(2,1)S(1)}, u32[]{:S(2)}, u32[]{:S(2)}) collective-permute-start(bf16[448,256]{1,0:T(8,128)(2,1)S(1)} %get-tuple-element.39), channel_id=1, source_target_pairs={{0,6},{2,4},{4,2},{6,0},{8,14},{10,12},{12,10},{14,8},{16,22},{18,... | collective-permute-start | bytes 688136 | tf_op jit(solution)/shard_map/ppermute | solution.py:154
  40.7 24.6 %collective-permute-start.12 = (bf16[1024,256]{1,0:T(8,128)(2,1)S(1)}, bf16[1024,256]{1,0:T(8,128)(2,1)S(1)}, u32[]{:S(2)}, u32[]{:S(2)}) collective-permute-start(bf16[1024,256]{1,0:T(8,128)(2,1)S(1)} %get-tuple-element.46), channel_id=1, source_target_pairs={{0,2},{2,0},{4,6},{6,4},{8,10},{10,8},{12,14},{14,12},{16,18},{18,... | collective-permute-start | bytes 1572872 | tf_op jit(solution)/shard_map/ppermute | solution.py:154
  47.8 24.1 %collective-permute-start.13 = (bf16[1024,256]{1,0:T(8,128)(2,1)S(1)}, bf16[1024,256]{1,0:T(8,128)(2,1)S(1)}, u32[]{:S(2)}, u32[]{:S(2)}) collective-permute-start(bf16[1024,256]{1,0:T(8,128)(2,1)S(1)} %get-tuple-element.47), channel_id=1, source_target_pairs={{0,4},{2,6},{4,0},{6,2},{8,12},{10,14},{12,8},{14,10},{16,20},{18,... | collective-permute-start | bytes 1572872 | tf_op jit(solution)/shard_map/ppermute | solution.py:154
  48.3 23.6 %collective-permute-start.14 = (bf16[1024,256]{1,0:T(8,128)(2,1)S(1)}, bf16[1024,256]{1,0:T(8,128)(2,1)S(1)}, u32[]{:S(2)}, u32[]{:S(2)}) collective-permute-start(bf16[1024,256]{1,0:T(8,128)(2,1)S(1)} %get-tuple-element.48), channel_id=1, source_target_pairs={{0,6},{2,4},{4,2},{6,0},{8,14},{10,12},{12,10},{14,8},{16,22},{18,... | collective-permute-start | bytes 1572872 | tf_op jit(solution)/shard_map/ppermute | solution.py:154
  53.5 6.4 %copy-start.3 = (bf16[1088,256]{1,0:T(8,128)(2,1)S(1)}, bf16[1088,256]{1,0:T(8,128)(2,1)}, u32[]{:S(2)}) copy-start(bf16[1088,256]{1,0:T(8,128)(2,1)} %q_ref.3) | copy-start | bytes 1671172
  53.5 26.6 %collective-permute-start.17 = (bf16[480,256]{1,0:T(8,128)(2,1)S(1)}, bf16[480,256]{1,0:T(8,128)(2,1)S(1)}, u32[]{:S(2)}, u32[]{:S(2)}) collective-permute-start(bf16[480,256]{1,0:T(8,128)(2,1)S(1)} %far_part.2.refs_12_), channel_id=1, source_target_pairs={{0,16},{2,18},{4,20},{6,22},{8,24},{10,26},{12,28},{14,30},{16,0},... | collective-permute-start | bytes 737288 | tf_op jit(solution)/shard_map/ppermute | solution.py:571
  57.5 21.7 %collective-permute-start.15 = (bf16[672,256]{1,0:T(8,128)(2,1)S(1)}, bf16[672,256]{1,0:T(8,128)(2,1)S(1)}, u32[]{:S(2)}, u32[]{:S(2)}) collective-permute-start(bf16[672,256]{1,0:T(8,128)(2,1)S(1)} %far_part.3.refs_8_), channel_id=1, source_target_pairs={{0,16},{2,18},{4,20},{6,22},{8,24},{10,26},{12,28},{14,30},{16,0},... | collective-permute-start | bytes 1032200 | tf_op jit(solution)/shard_map/ppermute | solution.py:571
  80.0 2.4 %copy-start.2 = (bf16[512,2048]{1,0:T(8,128)(2,1)S(1)}, bf16[512,2048]{1,0:T(8,128)(2,1)}, u32[]{:S(2)}) copy-start(bf16[512,2048]{1,0:T(8,128)(2,1)} %refs_2_.7) | copy-start | bytes 6291460
  80.0 4.6 %collective-permute-start.16 = (bf16[640,256]{1,0:T(8,128)(2,1)S(1)}, bf16[640,256]{1,0:T(8,128)(2,1)S(1)}, u32[]{:S(2)}, u32[]{:S(2)}) collective-permute-start(bf16[640,256]{1,0:T(8,128)(2,1)S(1)} %contexts.2.refs_0_), channel_id=1, source_target_pairs={{1,0},{0,1},{3,2},{2,3},{5,4},{4,5},{7,6},{6,7},{9,8},{8,9},{11,10... | collective-permute-start | bytes 983048 | tf_op jit(solution)/shard_map/ppermute | solution.py:579
  80.7 1.7 %collective-permute-start.18 = (bf16[448,256]{1,0:T(8,128)(2,1)S(1)}, bf16[448,256]{1,0:T(8,128)(2,1)S(1)}, u32[]{:S(2)}, u32[]{:S(2)}) collective-permute-start(bf16[448,256]{1,0:T(8,128)(2,1)S(1)} %contexts.3.refs_0_), channel_id=1, source_target_pairs={{1,0},{0,1},{3,2},{2,3},{5,4},{4,5},{7,6},{6,7},{9,8},{8,9},{11,10... | collective-permute-start | bytes 688136 | tf_op jit(solution)/shard_map/ppermute | solution.py:579

commit v4 on v1

--- a/solution.py
+++ b/solution.py
@@ -514,7 +514,7 @@
 def project(span, tokens, parts, w_out, done=None):
     rows = parts[0].shape[0]
     wide = w_out.shape[1]
-    steps = 4
+    steps = 2
     before = [] if done is None else [done]
     return pl.pallas_call(
         functools.partial(project_kernel, span, len(parts), steps),

time: 85.6 us -> 85.9 us (level)
  no operation moved by 1% of the time
where the time goes in v4:
time: 85.9 us; the launch traced here: 85.5 us
  waiting for transfers between devices  31.8 us (37%)
  Pallas kernels  25.7 us (30%)
  starting transfers between devices  24.6 us (29%)
  local copies, waits for them, and re-layouts  3.12 us (4%)
    ppermute x12, waiting for transfers between devices, exchange(): got.append(lax.ppermute(parts[k], 'seq', [(i, i ^ k) for i in range(n)]))  17.7 us
    ppermute x12, starting transfers between devices, exchange(): got.append(lax.ppermute(parts[k], 'seq', [(i, i ^ k) for i in range(n)]))  15.8 us
    pallas_call x2, Pallas kernels, far_part(): pl.pallas_call(functools.partial(far_kernel, n, cap, per, heads, span), o...  6.08 us
    ppermute x1, waiting for transfers between devices, on_device(): far_q = lax.ppermute(later_q, 'seq', partners)  5.58 us
    pallas_call x1, Pallas kernels, near_part(): pl.pallas_call(functools.partial(near_kernel, n, cap, per, heads), out_sh...  5.44 us
    pallas_call x2, Pallas kernels, project(): pl.pallas_call(functools.partial(project_kernel, span, len(parts), steps)...  4.8 us
    ppermute x1, waiting for transfers between devices, on_device(): mate_v = lax.ppermute(values, 'seq', mates)  4.76 us
    pallas_call x4, Pallas kernels, gather(): pl.pallas_call(functools.partial(gather_kernel, n, per, cap, lists, bool(...  4.28 us
  transfers between devices with their start and end apart: 19, of which 7 were waited for; matrix products, arithmetic and copies ran while one was open for 0% of the time, Pallas kernels for 27%

profile of v4, /device:TPU:0, one launch (start us, length us, event | category | flops | bytes accessed | tf_op | source)
XLA Modules:
  0.0 85.5 jit_solution(1479616534228923908)
XLA Ops:
  0.0 3.0 %collective-permute-start = (bf16[1088,256]{1,0:T(8,128)(2,1)}, bf16[1088,256]{1,0:T(8,128)(2,1)S(1)}, u32[]{:S(2)}, u32[]{:S(2)}) collective-permute-start(bf16[1088,256]{1,0:T(8,128)(2,1)} %k_ref.1), channel_id=1, source_target_pairs={{0,8},{2,10},{4,12},{6,14},{8,0},{10,2},{12,4},{14,6},{16,24},{18,... | collective-permute-start | bytes 1671176 | tf_op jit(solution)/shard_map/ppermute | solution.py:545
  3.0 0.0 copy-start.4
  3.0 0.7 copy-done.4
  3.7 0.0 copy-start.5
  3.7 0.7 copy-done.5
  4.4 0.4 ranks.1
  4.8 1.1 %copy-done = bf16[1088,256]{1,0:T(8,128)(2,1)S(1)} copy-done((bf16[1088,256]{1,0:T(8,128)(2,1)S(1)}, bf16[1088,256]{1,0:T(8,128)(2,1)}, u32[]{:S(2)}) %copy-start) | copy-done | bytes 557080
  5.8 1.2 %gather_blocks.4 = (bf16[512,256]{1,0:T(8,128)(2,1)S(1)}, bf16[512,256]{1,0:T(8,128)(2,1)S(1)}, bf16[512,256]{1,0:T(8,128)(2,1)S(1)}, bf16[512,256]{1,0:T(8,128)(2,1)S(1)}) custom-call(s32[8,128]{1,0:T(8,128)S(1)} %get-tuple-element.28.spot_ref, bf16[1088,256]{1,0:T(8,128)(2,1)S(1)} %copy-done, bf16[1088,256]{1,0:T(8,128)(2,1)} %v_ref.1), custom_call_target="tpu_custom_call" | custom-call | flops 1 | bytes 1 | tf_op jit(solution)/shard_map/gather_blocks/pallas_call | solution.py:137
  7.0 1.6 %collective-permute-start.1 = (bf16[512,256]{1,0:T(8,128)(2,1)S(1)}, bf16[512,256]{1,0:T(8,128)(2,1)S(1)}, u32[]{:S(2)}, u32[]{:S(2)}) collective-permute-start(bf16[512,256]{1,0:T(8,128)(2,1)S(1)} %get-tuple-element.29), channel_id=1, source_target_pairs={{0,2},{2,0},{4,6},{6,4},{8,10},{10,8},{12,14},{14,12},{16,18},{18,... | collective-permute-start | bytes 786440 | tf_op jit(solution)/shard_map/ppermute | solution.py:154
  8.6 1.5 %collective-permute-start.2 = (bf16[512,256]{1,0:T(8,128)(2,1)S(1)}, bf16[512,256]{1,0:T(8,128)(2,1)S(1)}, u32[]{:S(2)}, u32[]{:S(2)}) collective-permute-start(bf16[512,256]{1,0:T(8,128)(2,1)S(1)} %get-tuple-element.30), channel_id=1, source_target_pairs={{0,4},{2,6},{4,0},{6,2},{8,12},{10,14},{12,8},{14,10},{16,20},{18,... | collective-permute-start | bytes 786440 | tf_op jit(solution)/shard_map/ppermute | solution.py:154
  10.1 0.5 collective-permute-start.3
  10.6 0.0 collective-permute-start.7
  10.6 5.7 %collective-permute-done.1.refs_3_.refs_1_ = bf16[512,256]{1,0:T(8,128)(2,1)S(1)} collective-permute-done((bf16[512,256]{1,0:T(8,128)(2,1)S(1)}, bf16[512,256]{1,0:T(8,128)(2,1)S(1)}, u32[]{:S(2)}, u32[]{:S(2)}) %collective-permute-start.1) | collective-permute-done | bytes 262176 | tf_op jit(solution)/shard_map/ppermute | solution.py:154
  16.3 5.4 %collective-permute-done.2.refs_4_.refs_2_ = bf16[512,256]{1,0:T(8,128)(2,1)S(1)} collective-permute-done((bf16[512,256]{1,0:T(8,128)(2,1)S(1)}, bf16[512,256]{1,0:T(8,128)(2,1)S(1)}, u32[]{:S(2)}, u32[]{:S(2)}) %collective-permute-start.2) | collective-permute-done | bytes 262176 | tf_op jit(solution)/shard_map/ppermute | solution.py:154
  21.7 0.0 collective-permute-done.3.refs_5_.refs_3_
  21.7 2.6 %collective-permute-start.11 = (bf16[1088,256]{1,0:T(8,128)(2,1)}, bf16[1088,256]{1,0:T(8,128)(2,1)S(1)}, u32[]{:S(2)}, u32[]{:S(2)}) collective-permute-start(bf16[1088,256]{1,0:T(8,128)(2,1)} %q_ref.3), channel_id=1, source_target_pairs={{0,16},{2,18},{4,20},{6,22},{8,24},{10,26},{12,28},{14,30},{16,0},... | collective-permute-start | bytes 1671176 | tf_op jit(solution)/shard_map/ppermute | solution.py:552
  24.3 0.0 collective-permute-done.refs_1_.refs_2_
  24.3 0.7 copy-done.6
  25.0 0.7 gather_blocks.5
  25.7 0.0 copy-start.7
  25.7 1.3 %collective-permute-start.4 = (bf16[448,256]{1,0:T(8,128)(2,1)S(1)}, bf16[448,256]{1,0:T(8,128)(2,1)S(1)}, u32[]{:S(2)}, u32[]{:S(2)}) collective-permute-start(bf16[448,256]{1,0:T(8,128)(2,1)S(1)} %get-tuple-element.33), channel_id=1, source_target_pairs={{0,2},{2,0},{4,6},{6,4},{8,10},{10,8},{12,14},{14,12},{16,18},{18,... | collective-permute-start | bytes 688136 | tf_op jit(solution)/shard_map/ppermute | solution.py:154
  27.0 0.8 collective-permute-start.5
  27.8 1.4 %collective-permute-start.6 = (bf16[448,256]{1,0:T(8,128)(2,1)S(1)}, bf16[448,256]{1,0:T(8,128)(2,1)S(1)}, u32[]{:S(2)}, u32[]{:S(2)}) collective-permute-start(bf16[448,256]{1,0:T(8,128)(2,1)S(1)} %get-tuple-element.35), channel_id=1, source_target_pairs={{0,6},{2,4},{4,2},{6,0},{8,14},{10,12},{12,10},{14,8},{16,22},{18,... | collective-permute-start | bytes 688136 | tf_op jit(solution)/shard_map/ppermute | solution.py:154
  29.2 4.8 %collective-permute-done.7.refs_1_.refs_3_ = bf16[1088,256]{1,0:T(8,128)(2,1)S(1)} collective-permute-done((bf16[1088,256]{1,0:T(8,128)(2,1)}, bf16[1088,256]{1,0:T(8,128)(2,1)S(1)}, u32[]{:S(2)}, u32[]{:S(2)}) %collective-permute-start.7) | collective-permute-done | bytes 557088 | tf_op jit(solution)/shard_map/ppermute | solution.py:546
  34.0 0.0 collective-permute-done.4.refs_3_.refs_5_.refs_1_
  34.0 1.2 %gather_blocks.6 = (bf16[448,256]{1,0:T(8,128)(2,1)S(1)}, bf16[448,256]{1,0:T(8,128)(2,1)S(1)}, bf16[448,256]{1,0:T(8,128)(2,1)S(1)}, bf16[448,256]{1,0:T(8,128)(2,1)S(1)}) custom-call(s32[8,128]{1,0:T(8,128)S(1)} %get-tuple-element.28.spot_ref, bf16[1088,256]{1,0:T(8,128)(2,1)} %v_ref.1, bf16[1088,256]{1,0:T(8,128)(2,1)S(1)} %collective-permute-done.7.refs_1_.refs_3_, ...), custom_call_target="tpu_custom_call" | custom-call | flops 1 | bytes 1 | tf_op jit(solution)/shard_map/gather_blocks/pallas_call | solution.py:137
  35.2 1.8 %collective-permute-start.8 = (bf16[448,256]{1,0:T(8,128)(2,1)S(1)}, bf16[448,256]{1,0:T(8,128)(2,1)S(1)}, u32[]{:S(2)}, u32[]{:S(2)}) collective-permute-start(bf16[448,256]{1,0:T(8,128)(2,1)S(1)} %get-tuple-element.37), channel_id=1, source_target_pairs={{0,2},{2,0},{4,6},{6,4},{8,10},{10,8},{12,14},{14,12},{16,18},{18,... | collective-permute-start | bytes 688136 | tf_op jit(solution)/shard_map/ppermute | solution.py:154
  36.9 2.5 %collective-permute-start.9 = (bf16[448,256]{1,0:T(8,128)(2,1)S(1)}, bf16[448,256]{1,0:T(8,128)(2,1)S(1)}, u32[]{:S(2)}, u32[]{:S(2)}) collective-permute-start(bf16[448,256]{1,0:T(8,128)(2,1)S(1)} %get-tuple-element.38), channel_id=1, source_target_pairs={{0,4},{2,6},{4,0},{6,2},{8,12},{10,14},{12,8},{14,10},{16,20},{18,... | collective-permute-start | bytes 688136 | tf_op jit(solution)/shard_map/ppermute | solution.py:154
  39.4 0.0 collective-permute-done.5.refs_6_.refs_2_
  39.4 0.0 collective-permute-start.10
  39.4 0.0 copy-done.1
  39.4 1.2 %gather_blocks.7 = (bf16[1024,256]{1,0:T(8,128)(2,1)S(1)}, bf16[1024,256]{1,0:T(8,128)(2,1)S(1)}, bf16[1024,256]{1,0:T(8,128)(2,1)S(1)}, bf16[1024,256]{1,0:T(8,128)(2,1)S(1)}) custom-call(s32[8,128]{1,0:T(8,128)S(1)} %get-tuple-element.28.spot_ref, bf16[1088,256]{1,0:T(8,128)(2,1)S(1)} %copy-done.1, bf16[1088,256]{1,0:T(8,128)(2,1)} %v_ref.1, ...), custom_call_target="tpu_custom_call" | custom-call | flops 1 | bytes 1 | tf_op jit(solution)/shard_map/gather_blocks/pallas_call | solution.py:137
  40.7 0.0 collective-permute-done.6.refs_7_.refs_3_
  40.7 1.5 %collective-permute-start.12 = (bf16[1024,256]{1,0:T(8,128)(2,1)S(1)}, bf16[1024,256]{1,0:T(8,128)(2,1)S(1)}, u32[]{:S(2)}, u32[]{:S(2)}) collective-permute-start(bf16[1024,256]{1,0:T(8,128)(2,1)S(1)} %get-tuple-element.46), channel_id=1, source_target_pairs={{0,2},{2,0},{4,6},{6,4},{8,10},{10,8},{12,14},{14,12},{16,18},{18,... | collective-permute-start | bytes 1572872 | tf_op jit(solution)/shard_map/ppermute | solution.py:154
  42.2 5.6 %collective-permute-done.11.q_ref = bf16[1088,256]{1,0:T(8,128)(2,1)S(1)} collective-permute-done((bf16[1088,256]{1,0:T(8,128)(2,1)}, bf16[1088,256]{1,0:T(8,128)(2,1)S(1)}, u32[]{:S(2)}, u32[]{:S(2)}) %collective-permute-start.11) | collective-permute-done | bytes 557088 | tf_op jit(solution)/shard_map/ppermute | solution.py:552
  47.8 0.5 collective-permute-start.13
  48.3 0.0 collective-permute-done.8.refs_9_.refs_5_
  48.3 2.4 %collective-permute-start.14 = (bf16[1024,256]{1,0:T(8,128)(2,1)S(1)}, bf16[1024,256]{1,0:T(8,128)(2,1)S(1)}, u32[]{:S(2)}, u32[]{:S(2)}) collective-permute-start(bf16[1024,256]{1,0:T(8,128)(2,1)S(1)} %get-tuple-element.48), channel_id=1, source_target_pairs={{0,6},{2,4},{4,2},{6,0},{8,14},{10,12},{12,10},{14,8},{16,22},{18,... | collective-permute-start | bytes 1572872 | tf_op jit(solution)/shard_map/ppermute | solution.py:154
  50.7 0.0 collective-permute-done.9.refs_10_.refs_6_
  50.7 0.1 collective-permute-done.10.refs_11_.refs_7_
  50.8 0.0 copy-done.7
  50.8 3.2 %far_part.2.refs_12_ = bf16[608,256]{1,0:T(8,128)(2,1)S(1)} custom-call(s32[8,384]{1,0:T(8,128)S(1)} %get-tuple-element.40.arrive_ref, s32[2]{0:T(128)S(1)} %copy-done.7, bf16[1088,256]{1,0:T(8,128)(2,1)S(1)} %collective-permute-done.11.q_ref, bf16[512,256]{1,0:T(8,128)(2,1)S(1)} %get-tuple-element.42.refs_0_, ...), custom_call_target="tpu_custom_call" | custom-call | flops 4000000000 | bytes 1 | tf_op jit(solution)/shard_map/far_part/pallas_call | solution.py:335
  54.0 0.0 copy-start.3
  54.0 0.7 collective-permute-start.17
  54.7 2.9 %far_part.3.refs_8_ = bf16[544,256]{1,0:T(8,128)(2,1)S(1)} custom-call(s32[8,384]{1,0:T(8,128)S(1)} %get-tuple-element.40.arrive_ref, s32[2]{0:T(128)S(1)} %copy-done.7, bf16[1088,256]{1,0:T(8,128)(2,1)S(1)} %collective-permute-done.11.q_ref, bf16[512,256]{1,0:T(8,128)(2,1)S(1)} %get-tuple-element.42.refs_0_, ...), custom_call_target="tpu_custom_call" | custom-call | flops 4000000000 | bytes 1 | tf_op jit(solution)/shard_map/far_part/pallas_call | solution.py:335
  57.7 2.3 %collective-permute-start.15 = (bf16[544,256]{1,0:T(8,128)(2,1)S(1)}, bf16[544,256]{1,0:T(8,128)(2,1)S(1)}, u32[]{:S(2)}, u32[]{:S(2)}) collective-permute-start(bf16[544,256]{1,0:T(8,128)(2,1)S(1)} %far_part.3.refs_8_), channel_id=1, source_target_pairs={{0,16},{2,18},{4,20},{6,22},{8,24},{10,26},{12,28},{14,30},{16,0},... | collective-permute-start | bytes 835592 | tf_op jit(solution)/shard_map/ppermute | solution.py:571
  60.0 0.0 copy-done.3
  60.0 5.4 %near_part.1 = (f32[1088,256]{1,0:T(8,128)S(1)}, f32[24,256]{1,0:T(8,128)S(1)}) custom-call(s32[2]{0:T(128)S(1)} %copy-done.7, bf16[1088,256]{1,0:T(8,128)(2,1)S(1)} %copy-done.3, bf16[1088,256]{1,0:T(8,128)(2,1)S(1)} %copy-done.1, bf16[1088,256]{1,0:T(8,128)(2,1)} %v_ref.1, bf16[448,256]{1,0:T(8,128)(2,1)S(1)} %get-tuple-element.32.refs_4_.refs_0_, ...), custom_call_target="tpu_custom_call" | custom-call | flops 1 | bytes 1 | tf_op jit(solution)/shard_map/near_part/pallas_call | solution.py:402
  65.4 0.0 collective-permute-done.12.refs_1_
  65.4 6.4 %collective-permute-done.13.refs_2_ = bf16[1024,256]{1,0:T(8,128)(2,1)S(1)} collective-permute-done((bf16[1024,256]{1,0:T(8,128)(2,1)S(1)}, bf16[1024,256]{1,0:T(8,128)(2,1)S(1)}, u32[]{:S(2)}, u32[]{:S(2)}) %collective-permute-start.13) | collective-permute-done | bytes 524320 | tf_op jit(solution)/shard_map/ppermute | solution.py:154
  71.8 0.0 collective-permute-done.14.refs_3_
  71.8 3.4 %rand_part.1 = (f32[1088,256]{1,0:T(8,128)S(1)}, f32[24,256]{1,0:T(8,128)S(1)}) custom-call(s32[8,384]{1,0:T(8,128)S(1)} %get-tuple-element.40.arrive_ref, bf16[1088,256]{1,0:T(8,128)(2,1)S(1)} %copy-done.3, bf16[1024,256]{1,0:T(8,128)(2,1)S(1)} %get-tuple-element.43.refs_12_.refs_0_, bf16[1024,256]{1,0:T(8,128)(2,1)S(1)} %collective-permute-done.12.refs_1_, ...), custom_call_target="tpu_custom_call" | custom-call | flops 4000000000 | bytes 1 | tf_op jit(solution)/shard_map/rand_part/pallas_call | solution.py:439
  75.2 0.0 collective-permute-done.17.far_ref
  75.2 0.7 contexts.3.refs_0_
  76.0 0.0 copy-start.2
  76.0 0.1 collective-permute-start.18
  76.0 3.7 %collective-permute-done.15.far_ref = bf16[544,256]{1,0:T(8,128)(2,1)S(1)} collective-permute-done((bf16[544,256]{1,0:T(8,128)(2,1)S(1)}, bf16[544,256]{1,0:T(8,128)(2,1)S(1)}, u32[]{:S(2)}, u32[]{:S(2)}) %collective-permute-start.15) | collective-permute-done | bytes 278560 | tf_op jit(solution)/shard_map/ppermute | solution.py:571
  79.8 0.7 contexts.2.refs_0_
  80.4 0.1 collective-permute-start.16
  80.5 0.0 collective-permute-done.18.refs_1_
  80.5 0.0 copy-done.2
  80.5 2.5 %project.2.refs_3_ = bf16[1088,2048]{1,0:T(8,128)(2,1)} custom-call(bf16[576,256]{1,0:T(8,128)(2,1)S(1)} %contexts.3.refs_0_, bf16[576,256]{1,0:T(8,128)(2,1)S(1)} %collective-permute-done.18.refs_1_, bf16[512,2048]{1,0:T(8,128)(2,1)S(1)} %copy-done.2), custom_call_target="tpu_custom_call" | custom-call | flops 1 | bytes 1 | tf_op jit(solution)/shard_map/project/pallas_call | solution.py:519
  83.0 0.0 collective-permute-done.16.refs_1_
  83.0 2.3 %project.3 = bf16[1088,2048]{1,0:T(8,128)(2,1)} custom-call(bf16[512,256]{1,0:T(8,128)(2,1)S(1)} %contexts.2.refs_0_, bf16[512,256]{1,0:T(8,128)(2,1)S(1)} %collective-permute-done.16.refs_1_, bf16[512,2048]{1,0:T(8,128)(2,1)S(1)} %copy-done.2, bf16[1088,2048]{1,0:T(8,128)(2,1)} %project.2.refs_3_), custom_call_target="tpu_custom_call", output_to_operand_aliasing={{}: (3, {})} | custom-call | flops 1 | bytes 1 | tf_op jit(solution)/shard_map/project/pallas_call | solution.py:519
  (3 shorter events, 0.0 us)
Async XLA Ops:
  0.0 24.3 %collective-permute-start = (bf16[1088,256]{1,0:T(8,128)(2,1)}, bf16[1088,256]{1,0:T(8,128)(2,1)S(1)}, u32[]{:S(2)}, u32[]{:S(2)}) collective-permute-start(bf16[1088,256]{1,0:T(8,128)(2,1)} %k_ref.1), channel_id=1, source_target_pairs={{0,8},{2,10},{4,12},{6,14},{8,0},{10,2},{12,4},{14,6},{16,24},{18,... | collective-permute-start | bytes 1671176 | tf_op jit(solution)/shard_map/ppermute | solution.py:545
  3.0 0.7 copy-start.4
  3.7 0.7 copy-start.5
  4.8 1.1 %copy-start = (bf16[1088,256]{1,0:T(8,128)(2,1)S(1)}, bf16[1088,256]{1,0:T(8,128)(2,1)}, u32[]{:S(2)}) copy-start(bf16[1088,256]{1,0:T(8,128)(2,1)} %k_ref.1) | copy-start | bytes 1671172
  5.8 33.6 %copy-start.1 = (bf16[1088,256]{1,0:T(8,128)(2,1)S(1)}, bf16[1088,256]{1,0:T(8,128)(2,1)}, u32[]{:S(2)}) copy-start(bf16[1088,256]{1,0:T(8,128)(2,1)} %k_ref.1) | copy-start | bytes 1671172
  7.0 9.3 %collective-permute-start.1 = (bf16[512,256]{1,0:T(8,128)(2,1)S(1)}, bf16[512,256]{1,0:T(8,128)(2,1)S(1)}, u32[]{:S(2)}, u32[]{:S(2)}) collective-permute-start(bf16[512,256]{1,0:T(8,128)(2,1)S(1)} %get-tuple-element.29), channel_id=1, source_target_pairs={{0,2},{2,0},{4,6},{6,4},{8,10},{10,8},{12,14},{14,12},{16,18},{18,... | collective-permute-start | bytes 786440 | tf_op jit(solution)/shard_map/ppermute | solution.py:154
  8.6 13.1 %collective-permute-start.2 = (bf16[512,256]{1,0:T(8,128)(2,1)S(1)}, bf16[512,256]{1,0:T(8,128)(2,1)S(1)}, u32[]{:S(2)}, u32[]{:S(2)}) collective-permute-start(bf16[512,256]{1,0:T(8,128)(2,1)S(1)} %get-tuple-element.30), channel_id=1, source_target_pairs={{0,4},{2,6},{4,0},{6,2},{8,12},{10,14},{12,8},{14,10},{16,20},{18,... | collective-permute-start | bytes 786440 | tf_op jit(solution)/shard_map/ppermute | solution.py:154
  10.1 11.6 %collective-permute-start.3 = (bf16[512,256]{1,0:T(8,128)(2,1)S(1)}, bf16[512,256]{1,0:T(8,128)(2,1)S(1)}, u32[]{:S(2)}, u32[]{:S(2)}) collective-permute-start(bf16[512,256]{1,0:T(8,128)(2,1)S(1)} %get-tuple-element.31), channel_id=1, source_target_pairs={{0,6},{2,4},{4,2},{6,0},{8,14},{10,12},{12,10},{14,8},{16,22},{18,... | collective-permute-start | bytes 786440 | tf_op jit(solution)/shard_map/ppermute | solution.py:154
  10.6 23.4 %collective-permute-start.7 = (bf16[1088,256]{1,0:T(8,128)(2,1)}, bf16[1088,256]{1,0:T(8,128)(2,1)S(1)}, u32[]{:S(2)}, u32[]{:S(2)}) collective-permute-start(bf16[1088,256]{1,0:T(8,128)(2,1)} %v_ref.1), channel_id=1, source_target_pairs={{0,8},{2,10},{4,12},{6,14},{8,0},{10,2},{12,4},{14,6},{16,24},{18,... | collective-permute-start | bytes 1671176 | tf_op jit(solution)/shard_map/ppermute | solution.py:546
  21.7 26.1 %collective-permute-start.11 = (bf16[1088,256]{1,0:T(8,128)(2,1)}, bf16[1088,256]{1,0:T(8,128)(2,1)S(1)}, u32[]{:S(2)}, u32[]{:S(2)}) collective-permute-start(bf16[1088,256]{1,0:T(8,128)(2,1)} %q_ref.3), channel_id=1, source_target_pairs={{0,16},{2,18},{4,20},{6,22},{8,24},{10,26},{12,28},{14,30},{16,0},... | collective-permute-start | bytes 1671176 | tf_op jit(solution)/shard_map/ppermute | solution.py:552
  24.3 0.7 copy-start.6
  25.7 25.2 %copy-start.7 = (s32[2]{0:T(128)S(1)}, s32[2]{0:T(128)}, u32[]{:S(2)}) copy-start(s32[2]{0:T(128)} %place_ref.5) | copy-start | bytes 28
  25.7 8.3 %collective-permute-start.4 = (bf16[448,256]{1,0:T(8,128)(2,1)S(1)}, bf16[448,256]{1,0:T(8,128)(2,1)S(1)}, u32[]{:S(2)}, u32[]{:S(2)}) collective-permute-start(bf16[448,256]{1,0:T(8,128)(2,1)S(1)} %get-tuple-element.33), channel_id=1, source_target_pairs={{0,2},{2,0},{4,6},{6,4},{8,10},{10,8},{12,14},{14,12},{16,18},{18,... | collective-permute-start | bytes 688136 | tf_op jit(solution)/shard_map/ppermute | solution.py:154
  27.0 12.5 %collective-permute-start.5 = (bf16[448,256]{1,0:T(8,128)(2,1)S(1)}, bf16[448,256]{1,0:T(8,128)(2,1)S(1)}, u32[]{:S(2)}, u32[]{:S(2)}) collective-permute-start(bf16[448,256]{1,0:T(8,128)(2,1)S(1)} %get-tuple-element.34), channel_id=1, source_target_pairs={{0,4},{2,6},{4,0},{6,2},{8,12},{10,14},{12,8},{14,10},{16,20},{18,... | collective-permute-start | bytes 688136 | tf_op jit(solution)/shard_map/ppermute | solution.py:154
  27.8 12.9 %collective-permute-start.6 = (bf16[448,256]{1,0:T(8,128)(2,1)S(1)}, bf16[448,256]{1,0:T(8,128)(2,1)S(1)}, u32[]{:S(2)}, u32[]{:S(2)}) collective-permute-start(bf16[448,256]{1,0:T(8,128)(2,1)S(1)} %get-tuple-element.35), channel_id=1, source_target_pairs={{0,6},{2,4},{4,2},{6,0},{8,14},{10,12},{12,10},{14,8},{16,22},{18,... | collective-permute-start | bytes 688136 | tf_op jit(solution)/shard_map/ppermute | solution.py:154
  35.2 13.1 %collective-permute-start.8 = (bf16[448,256]{1,0:T(8,128)(2,1)S(1)}, bf16[448,256]{1,0:T(8,128)(2,1)S(1)}, u32[]{:S(2)}, u32[]{:S(2)}) collective-permute-start(bf16[448,256]{1,0:T(8,128)(2,1)S(1)} %get-tuple-element.37), channel_id=1, source_target_pairs={{0,2},{2,0},{4,6},{6,4},{8,10},{10,8},{12,14},{14,12},{16,18},{18,... | collective-permute-start | bytes 688136 | tf_op jit(solution)/shard_map/ppermute | solution.py:154
  36.9 13.7 %collective-permute-start.9 = (bf16[448,256]{1,0:T(8,128)(2,1)S(1)}, bf16[448,256]{1,0:T(8,128)(2,1)S(1)}, u32[]{:S(2)}, u32[]{:S(2)}) collective-permute-start(bf16[448,256]{1,0:T(8,128)(2,1)S(1)} %get-tuple-element.38), channel_id=1, source_target_pairs={{0,4},{2,6},{4,0},{6,2},{8,12},{10,14},{12,8},{14,10},{16,20},{18,... | collective-permute-start | bytes 688136 | tf_op jit(solution)/shard_map/ppermute | solution.py:154
  39.4 11.4 %collective-permute-start.10 = (bf16[448,256]{1,0:T(8,128)(2,1)S(1)}, bf16[448,256]{1,0:T(8,128)(2,1)S(1)}, u32[]{:S(2)}, u32[]{:S(2)}) collective-permute-start(bf16[448,256]{1,0:T(8,128)(2,1)S(1)} %get-tuple-element.39), channel_id=1, source_target_pairs={{0,6},{2,4},{4,2},{6,0},{8,14},{10,12},{12,10},{14,8},{16,22},{18,... | collective-permute-start | bytes 688136 | tf_op jit(solution)/shard_map/ppermute | solution.py:154
  40.7 24.8 %collective-permute-start.12 = (bf16[1024,256]{1,0:T(8,128)(2,1)S(1)}, bf16[1024,256]{1,0:T(8,128)(2,1)S(1)}, u32[]{:S(2)}, u32[]{:S(2)}) collective-permute-start(bf16[1024,256]{1,0:T(8,128)(2,1)S(1)} %get-tuple-element.46), channel_id=1, source_target_pairs={{0,2},{2,0},{4,6},{6,4},{8,10},{10,8},{12,14},{14,12},{16,18},{18,... | collective-permute-start | bytes 1572872 | tf_op jit(solution)/shard_map/ppermute | solution.py:154
  47.8 24.1 %collective-permute-start.13 = (bf16[1024,256]{1,0:T(8,128)(2,1)S(1)}, bf16[1024,256]{1,0:T(8,128)(2,1)S(1)}, u32[]{:S(2)}, u32[]{:S(2)}) collective-permute-start(bf16[1024,256]{1,0:T(8,128)(2,1)S(1)} %get-tuple-element.47), channel_id=1, source_target_pairs={{0,4},{2,6},{4,0},{6,2},{8,12},{10,14},{12,8},{14,10},{16,20},{18,... | collective-permute-start | bytes 1572872 | tf_op jit(solution)/shard_map/ppermute | solution.py:154
  48.3 23.6 %collective-permute-start.14 = (bf16[1024,256]{1,0:T(8,128)(2,1)S(1)}, bf16[1024,256]{1,0:T(8,128)(2,1)S(1)}, u32[]{:S(2)}, u32[]{:S(2)}) collective-permute-start(bf16[1024,256]{1,0:T(8,128)(2,1)S(1)} %get-tuple-element.48), channel_id=1, source_target_pairs={{0,6},{2,4},{4,2},{6,0},{8,14},{10,12},{12,10},{14,8},{16,22},{18,... | collective-permute-start | bytes 1572872 | tf_op jit(solution)/shard_map/ppermute | solution.py:154
  54.0 6.0 %copy-start.3 = (bf16[1088,256]{1,0:T(8,128)(2,1)S(1)}, bf16[1088,256]{1,0:T(8,128)(2,1)}, u32[]{:S(2)}) copy-start(bf16[1088,256]{1,0:T(8,128)(2,1)} %q_ref.3) | copy-start | bytes 1671172
  54.0 21.2 %collective-permute-start.17 = (bf16[608,256]{1,0:T(8,128)(2,1)S(1)}, bf16[608,256]{1,0:T(8,128)(2,1)S(1)}, u32[]{:S(2)}, u32[]{:S(2)}) collective-permute-start(bf16[608,256]{1,0:T(8,128)(2,1)S(1)} %far_part.2.refs_12_), channel_id=1, source_target_pairs={{0,16},{2,18},{4,20},{6,22},{8,24},{10,26},{12,28},{14,30},{16,0},... | collective-permute-start | bytes 933896 | tf_op jit(solution)/shard_map/ppermute | solution.py:571
  57.7 22.1 %collective-permute-start.15 = (bf16[544,256]{1,0:T(8,128)(2,1)S(1)}, bf16[544,256]{1,0:T(8,128)(2,1)S(1)}, u32[]{:S(2)}, u32[]{:S(2)}) collective-permute-start(bf16[544,256]{1,0:T(8,128)(2,1)S(1)} %far_part.3.refs_8_), channel_id=1, source_target_pairs={{0,16},{2,18},{4,20},{6,22},{8,24},{10,26},{12,28},{14,30},{16,0},... | collective-permute-start | bytes 835592 | tf_op jit(solution)/shard_map/ppermute | solution.py:571
  76.0 4.6 %copy-start.2 = (bf16[512,2048]{1,0:T(8,128)(2,1)S(1)}, bf16[512,2048]{1,0:T(8,128)(2,1)}, u32[]{:S(2)}) copy-start(bf16[512,2048]{1,0:T(8,128)(2,1)} %refs_2_.7) | copy-start | bytes 6291460
  76.0 4.5 %collective-permute-start.18 = (bf16[576,256]{1,0:T(8,128)(2,1)S(1)}, bf16[576,256]{1,0:T(8,128)(2,1)S(1)}, u32[]{:S(2)}, u32[]{:S(2)}) collective-permute-start(bf16[576,256]{1,0:T(8,128)(2,1)S(1)} %contexts.3.refs_0_), channel_id=1, source_target_pairs={{1,0},{0,1},{3,2},{2,3},{5,4},{4,5},{7,6},{6,7},{9,8},{8,9},{11,10... | collective-permute-start | bytes 884744 | tf_op jit(solution)/shard_map/ppermute | solution.py:579
  80.4 2.6 %collective-permute-start.16 = (bf16[512,256]{1,0:T(8,128)(2,1)S(1)}, bf16[512,256]{1,0:T(8,128)(2,1)S(1)}, u32[]{:S(2)}, u32[]{:S(2)}) collective-permute-start(bf16[512,256]{1,0:T(8,128)(2,1)S(1)} %contexts.2.refs_0_), channel_id=1, source_target_pairs={{1,0},{0,1},{3,2},{2,3},{5,4},{4,5},{7,6},{6,7},{9,8},{8,9},{11,10... | collective-permute-start | bytes 786440 | tf_op jit(solution)/shard_map/ppermute | solution.py:579
